TPU v7x, 256 devices: a whole 4x4x8 slice. The times are simulated.
256 devices in a mesh: virt: 64 (over x, z, core), pair: 4 (over y).
Axes of the slice: x: 4, y: 4, z: 8, core: 2. Of those that a mesh axis runs over, the one named last changes fastest.
Arguments:
- amplitudes: bfloat16 [8, 1024, 2, 1024], P('pair'), may hold values from -6 to 6
- integrals: bfloat16 [2, 512, 8, 65536], P(None, None, None, ('virt', 'pair')), may hold values from -0.125 to 0.125
- virt_counts: int32 [8], replicated, may hold values from 32 to 64, as said below
- pair_counts: int32 [8], replicated, may hold values from 512 to 1024, as said below
- pair_list: int32 [8, 1024, 2], P('pair'), may hold values from 0 to 99
- eps_occ: float32 [100], replicated, may hold values from -2 to -0.3
- eps_virt: float32 [512], replicated, may hold values from 0.3 to 4
Outputs:
- update: bfloat16 [8, 1024, 32768], P('pair', None, 'virt')
- pair_energy: float32 [8, 1024], P('pair', 'virt')
Inputs may be any that keep to these rules, and one draw needn't show every extreme that they name: virt_counts[0] = 64; every count is at least 32. `pair_counts`: some pair symmetry has exactly 1024 pairs; every count is at least 512.
All inputs are finite; a program needn't handle non-finite values.
Results may differ from a plain program's by a relative error of at most 0.001.
Values may be sent and summed in bfloat16 or wider, within the bound.
No kernel may reach another device: no remote copies, remote signals or barrier semaphores. Data moves between devices by JAX's collectives and lax.ppermute only.
A program may use at most 128 MiB of HBM per device.

v0:
```python
import jax
import jax.numpy as jnp
from jax import lax
from jax.sharding import PartitionSpec as P

IRREPS = 8
NV = 512
BLK = 64
CS = 16
SLABS = 2


def pick_counts(irrep_ids, table):
    onehot = irrep_ids[..., None] == jnp.arange(table.shape[0], dtype=jnp.int32)
    return jnp.sum(jnp.where(onehot, table, 0), axis=-1)


def shards(amplitudes, integrals, virt_counts, pair_counts, pair_list, eps_occ, eps_virt):
    local_irreps = amplitudes.shape[0]
    rows = amplitudes.shape[1]
    width = amplitudes.shape[3]
    n_virt = lax.axis_size("virt")
    n_pair = lax.axis_size("pair")
    a_local = NV // n_virt
    irrep_ids = lax.axis_index("pair") * local_irreps + jnp.arange(local_irreps, dtype=jnp.int32)
    slots = jnp.arange(BLK, dtype=jnp.int32)
    live_d = slots[None, :] < pick_counts(irrep_ids, virt_counts)[:, None]
    dmask = jnp.tile(live_d, (1, CS)).astype(jnp.bfloat16)
    masked = amplitudes * dmask[:, None, None, :]
    ladder = jnp.zeros((local_irreps, rows, a_local, BLK), jnp.float32)
    for s in range(SLABS):
        piece = integrals[s]
        moved = lax.all_to_all(
            lax.all_to_all(piece, "virt", split_axis=0, concat_axis=2, tiled=True),
            "pair",
            split_axis=1,
            concat_axis=2,
            tiled=True,
        )
        moved = moved.reshape(a_local, local_irreps, n_pair, n_virt, -1)
        moved = jnp.transpose(moved, (0, 1, 3, 2, 4)).reshape(a_local, local_irreps, BLK, width)
        ladder = ladder + jnp.einsum(
            "hrk,ahsk->hras", masked[:, :, s, :], moved, preferred_element_type=jnp.float32
        )
    a_global = lax.axis_index("virt") * a_local + jnp.arange(a_local, dtype=jnp.int32)
    a_irrep = a_global // BLK
    a_slot = a_global % BLK
    live_a = a_slot < pick_counts(a_irrep, virt_counts)
    eps_a = lax.dynamic_slice_in_dim(eps_virt, lax.axis_index("virt") * a_local, a_local)
    b_irrep = jnp.bitwise_xor(a_irrep[None, :], irrep_ids[:, None])
    b_onehot = (b_irrep[..., None] == jnp.arange(IRREPS, dtype=jnp.int32)).astype(jnp.float32)
    eps_table = eps_virt.reshape(IRREPS, BLK)
    eps_b = jnp.einsum("hag,gs->has", b_onehot, eps_table, precision=lax.Precision.HIGHEST)
    live_b = slots[None, None, :] < pick_counts(b_irrep, virt_counts)[..., None]
    occ_onehot = pair_list[..., None] == jnp.arange(eps_occ.shape[0], dtype=jnp.int32)
    occ_terms = jnp.sum(jnp.where(occ_onehot, eps_occ, 0.0), axis=-1)
    occ = occ_terms[:, :, 0] + occ_terms[:, :, 1]
    live_rows = (
        jnp.arange(rows, dtype=jnp.int32)[None, :] < pick_counts(irrep_ids, pair_counts)[:, None]
    )
    denom = (eps_a[None, :, None] + eps_b)[:, None, :, :] - occ[:, :, None, None]
    live = live_rows[:, :, None, None] & live_a[None, None, :, None] & live_b[:, None, :, :]
    ratio = jnp.where(live, ladder / denom, jnp.zeros_like(ladder))
    update = ratio.astype(jnp.bfloat16).reshape(local_irreps, rows, a_local * BLK)
    partial_value = jnp.sum(ratio * ladder, axis=(2, 3)) / (NV * BLK)
    energy = lax.psum_scatter(partial_value, "virt", scatter_dimension=1, tiled=True)
    return (update, energy)


def solution(mesh):
    placed = (
        P("pair", None, None, None),
        P(None, None, None, ("virt", "pair")),
        P(),
        P(),
        P("pair", None, None),
        P(),
        P(),
    )
    return jax.shard_map(
        shards,
        mesh=mesh,
        in_specs=placed,
        out_specs=(P("pair", None, "virt"), P("pair", "virt")),
        check_vma=False,
    )
```

profile of v0, /device:TPU:1, one launch (start us, length us, event | category | flops | bytes accessed | tf_op | source)
XLA Modules:
  0.0 343.2 jit_solution(5038746887808633869)
XLA Ops:
  7.2 3.8 %slice_bitcast_fusion.5 = (bf16[512,8,256]{2,1,0:T(8,128)(2,1)S(1)}, bf16[512,8,256]{2,1,0:T(8,128)(2,1)}) fusion(bf16[2,512,8,256]{3,2,1,0:T(8,128)(2,1)} %param.8), kind=kLoop, calls=%fused_computation.12 | loop fusion | bytes 8388608 | tf_op jit(solution)/shard_map/squeeze | solution.py:32
  11.0 64.1 %all_to_all.66 = bf16[512,8,256]{2,1,0:T(8,128)(2,1)} all-to-all(bf16[512,8,256]{2,1,0:T(8,128)(2,1)S(1)} %get-tuple-element.14), channel_id=1, replica_groups=mesh['virt'=64,'pair'=4] {'virt'}, dimensions={0} | all-to-all | bytes 4194304 | tf_op jit(solution)/shard_map/all_to_all | solution.py:34
  75.1 5.8 %all-to-all-start.2 = ((bf16[512,8,256]{2,1,0:T(8,128)(2,1)}), bf16[512,8,256]{2,1,0:T(8,128)(2,1)S(1)}, u32[]{:S(2)}, u32[]{:S(2)}) async-start(bf16[512,8,256]{2,1,0:T(8,128)(2,1)} %get-tuple-element.15), calls=%async_computation.2 | async-start | bytes 4194304 | tf_op jit(solution)/shard_map/all_to_all | solution.py:34
  80.9 4.1 %copy.58 = bf16[64,8,8,256]{3,0,2,1:T(8,128)(2,1)} copy(bf16[64,8,8,256]{3,2,1,0:T(8,128)(2,1)} %bitcast.73) | data formatting | bytes 4194304 | tf_op jit(solution)/shard_map/all_to_all | solution.py:34
  85.0 4.2 %all_to_all.51 = bf16[8,8,16384]{2,1,0:T(8,128)(2,1)} reshape(bf16[8,8,64,256]{3,2,1,0:T(8,128)(2,1)} %bitcast.74) | data formatting | bytes 4194304 | tf_op jit(solution)/shard_map/all_to_all | solution.py:34
  89.3 4.1 %copy.34 = bf16[8,8,16384]{2,0,1:T(8,128)(2,1)} copy(bf16[8,8,16384]{2,1,0:T(8,128)(2,1)} %all_to_all.51) | data formatting | bytes 4194304 | tf_op jit(solution)/shard_map/all_to_all | solution.py:34
  93.4 38.8 %all-to-all-done.2 = bf16[512,8,256]{2,1,0:T(8,128)(2,1)S(1)} async-done(((bf16[512,8,256]{2,1,0:T(8,128)(2,1)}), bf16[512,8,256]{2,1,0:T(8,128)(2,1)S(1)}, u32[]{:S(2)}, u32[]{:S(2)}) %all-to-all-start.2) | async-done | bytes 2097184 | tf_op jit(solution)/shard_map/all_to_all | solution.py:34
  132.2 1.3 copy-done.1
  133.5 4.2 %all-to-all-start.1 = ((bf16[8,8,16384]{2,0,1:T(8,128)(2,1)}), bf16[8,8,16384]{2,0,1:T(8,128)(2,1)S(1)}, u32[]{:S(2)}, u32[]{:S(2)}) async-start(bf16[8,8,16384]{2,0,1:T(8,128)(2,1)} %copy.34), calls=%async_computation.1 | async-start | bytes 4194304 | tf_op jit(solution)/shard_map/all_to_all | solution.py:33
  137.7 0.2 select_reduce_fusion.1
  137.9 0.2 select_reduce_fusion.3
  138.1 0.2 select_reduce_fusion
  138.4 0.9 fusion.4
  139.3 4.1 %copy.57 = bf16[64,8,8,256]{3,0,2,1:T(8,128)(2,1)} copy(bf16[64,8,8,256]{3,2,1,0:T(8,128)(2,1)} %bitcast.72) | data formatting | bytes 4194304 | tf_op jit(solution)/shard_map/all_to_all | solution.py:34
  143.4 4.2 %all_to_all.58 = bf16[8,8,16384]{2,1,0:T(8,128)(2,1)} reshape(bf16[8,8,64,256]{3,2,1,0:T(8,128)(2,1)} %bitcast.75) | data formatting | bytes 4194304 | tf_op jit(solution)/shard_map/all_to_all | solution.py:34
  147.6 4.1 %copy.38 = bf16[8,8,16384]{2,0,1:T(8,128)(2,1)} copy(bf16[8,8,16384]{2,1,0:T(8,128)(2,1)} %all_to_all.58) | data formatting | bytes 4194304 | tf_op jit(solution)/shard_map/all_to_all | solution.py:34
  151.7 11.7 %all-to-all-done.1 = bf16[8,8,16384]{2,0,1:T(8,128)(2,1)S(1)} async-done(((bf16[8,8,16384]{2,0,1:T(8,128)(2,1)}), bf16[8,8,16384]{2,0,1:T(8,128)(2,1)S(1)}, u32[]{:S(2)}, u32[]{:S(2)}) %all-to-all-start.1) | async-done | bytes 2097184 | tf_op jit(solution)/shard_map/all_to_all | solution.py:33
  163.4 4.5 %all-to-all-start.3 = ((bf16[8,8,16384]{2,0,1:T(8,128)(2,1)}), bf16[8,8,16384]{2,0,1:T(8,128)(2,1)}, u32[]{:S(2)}, u32[]{:S(2)}) async-start(bf16[8,8,16384]{2,0,1:T(8,128)(2,1)} %copy.38), calls=%async_computation.3 | async-start | bytes 4194304 | tf_op jit(solution)/shard_map/all_to_all | solution.py:33
  167.9 0.2 reduce-scatter.4.cloned.1.call-start
  168.5 0.2 convolution_add_fusion
  168.8 9.3 %copy_multiply_fusion = bf16[2,1024,2,1024]{3,1,0,2:T(8,128)(2,1)} fusion(bf16[2,1024,2,1024]{3,2,1,0:T(2,128)(2,1)} %param.7, bf16[2,1024]{1,0:T(2,128)(2,1)S(1)} %convert_element_type.16), kind=kLoop, calls=%fused_computation | loop fusion | flops 4194304 | bytes 16781312 | tf_op jit(solution)/shard_map/mul | solution.py:29
  178.2 1.8 copy.47
  180.1 12.7 %all-to-all-done.3 = bf16[8,8,16384]{2,0,1:T(8,128)(2,1)} async-done(((bf16[8,8,16384]{2,0,1:T(8,128)(2,1)}), bf16[8,8,16384]{2,0,1:T(8,128)(2,1)}, u32[]{:S(2)}, u32[]{:S(2)}) %all-to-all-start.3) | async-done | bytes 2097184 | tf_op jit(solution)/shard_map/all_to_all | solution.py:33
  192.8 1.9 copy.39
  194.7 0.5 copy.48
  195.2 1.6 copy-done
  196.8 2.4 fusion
  199.2 3.5 %multiply_reduce_fusion = (f32[2,1024]{1,0:T(2,128)S(1)}, bf16[2,1024,8,64]{1,3,2,0:T(8,128)(2,1)S(1)}) fusion(f32[2,1024]{1,0:T(2,128)S(1)} %bitcast.83, f32[2,8,64]{2,1,0:T(8,128)S(1)} %convolution_add_fusion, pred[2,8,64]{2,1,0:T(8,128)(4,1)S(1)} %iota_compare_fusion.2, pred[2,1024,8]{1,2,0:T(8,128)(4,1)S(1)} %broadcast_and_fusion, ...), kind=kOutput, calls=%fused_computation.5 | convolution fusion | flops 2155870208 | bytes 12625920 | tf_op jit(solution)/shard_map/hrk,ahsk->hras/dot_general | solution.py:42
  202.6 1.0 copy.44
  203.7 2.6 copy.41
  206.3 128.8 %reduce-scatter.4.cloned.1.call-done = f32[16,2]{1,0:T(8,128)} async-done(((f32[1024,2]{1,0:T(8,128)}), f32[16,2]{1,0:T(8,128)}) %reduce-scatter.4.cloned.1.call-update) | async-done | bytes 144
  335.1 1.3 copy.45
  (30 shorter events, 0.8 us)
Async XLA Ops:
  75.1 57.1 %all-to-all-start.2 = ((bf16[512,8,256]{2,1,0:T(8,128)(2,1)}), bf16[512,8,256]{2,1,0:T(8,128)(2,1)S(1)}, u32[]{:S(2)}, u32[]{:S(2)}) async-start(bf16[512,8,256]{2,1,0:T(8,128)(2,1)} %get-tuple-element.15), calls=%async_computation.2 | async-start | bytes 4194304 | tf_op jit(solution)/shard_map/all_to_all | solution.py:34
  93.3 44.3 %copy-start.5 = (s32[8]{0:T(128)S(1)}, s32[8]{0:T(128)}, u32[]{:S(2)}) copy-start(s32[8]{0:T(128)} %param.9) | copy-start | bytes 100
  93.4 44.5 %copy-start.7 = (s32[8]{0:T(128)S(1)}, s32[8]{0:T(128)}, u32[]{:S(2)}) copy-start(s32[8]{0:T(128)} %param.10) | copy-start | bytes 100
  93.4 45.0 %copy-start.3 = (s32[2,1024,2]{1,2,0:T(2,128)S(1)}, s32[2,1024,2]{1,2,0:T(2,128)}, u32[]{:S(2)}) copy-start(s32[2,1024,2]{1,2,0:T(2,128)} %param.11) | copy-start | bytes 49156
  93.4 45.0 %copy-start.6 = (f32[100]{0:T(128)S(1)}, f32[100]{0:T(128)}, u32[]{:S(2)}) copy-start(f32[100]{0:T(128)} %param.12) | copy-start | bytes 1204
  132.2 1.3 copy-start.1
  133.5 29.9 %all-to-all-start.1 = ((bf16[8,8,16384]{2,0,1:T(8,128)(2,1)}), bf16[8,8,16384]{2,0,1:T(8,128)(2,1)S(1)}, u32[]{:S(2)}, u32[]{:S(2)}) async-start(bf16[8,8,16384]{2,0,1:T(8,128)(2,1)} %copy.34), calls=%async_computation.1 | async-start | bytes 4194304 | tf_op jit(solution)/shard_map/all_to_all | solution.py:33
  151.7 16.5 %copy-start.4 = (f32[512]{0:T(512)S(1)}, f32[512]{0:T(512)}, u32[]{:S(2)}) copy-start(f32[512]{0:T(512)} %param.13) | copy-start | bytes 6148
  163.4 29.4 %all-to-all-start.3 = ((bf16[8,8,16384]{2,0,1:T(8,128)(2,1)}), bf16[8,8,16384]{2,0,1:T(8,128)(2,1)}, u32[]{:S(2)}, u32[]{:S(2)}) async-start(bf16[8,8,16384]{2,0,1:T(8,128)(2,1)} %copy.38), calls=%async_computation.3 | async-start | bytes 4194304 | tf_op jit(solution)/shard_map/all_to_all | solution.py:33
  167.9 167.2 %reduce-scatter.4.cloned.1.call-start = ((), (), s32[]{:S(2)}) async-start(), calls=%async_computation.5 | async-start | bytes 532480
  192.8 4.0 %copy-start = (bf16[2,1024,2,1024]{3,1,0,2:T(8,128)(2,1)S(1)}, bf16[2,1024,2,1024]{3,1,0,2:T(8,128)(2,1)}, u32[]{:S(2)}) copy-start(bf16[2,1024,2,1024]{3,1,0,2:T(8,128)(2,1)} %copy_multiply_fusion) | copy-start | bytes 25165828
  196.8 2.4 copy-start.2
Sparse Core Ops, SparseCore 0:
  203.8 131.2 reduce-scatter.3
where the time goes:
time: 348 us; the launch traced here: 343 us
  waiting for transfers between devices  192 us (55%)
  blocking collectives  64.1 us (18%)
  local copies, waits for them, and re-layouts  41.1 us (12%)
  starting transfers between devices  14.7 us (4%)
  between operations  14.2 us (4%)
  other arithmetic  11.1 us (3%)
  matrix products  6.02 us (2%)
    unnamed x2, waiting for transfers between devices  129 us
    all_to_all x1, blocking collectives, shards(): lax.all_to_all(piece, 'virt', split_axis=0, concat_axis=2, tiled=True)  64.1 us
    all_to_all x1, waiting for transfers between devices, shards(): lax.all_to_all(piece, 'virt', split_axis=0, concat_axis=2, tiled=True)  38.8 us
    all_to_all x6, local copies, waits for them, and re-layouts, shards(): lax.all_to_all(piece, 'virt', split_axis=0, concat_axis=2, tiled=True)  24.8 us
    all_to_all x2, waiting for transfers between devices, shards(): lax.all_to_all(lax.all_to_all(piece, 'virt', split_axis=0, concat_axis=2,...  24.4 us
    mul x1, other arithmetic, shards(): masked = amplitudes * dmask[:, None, None, :]  9.31 us
    all_to_all x2, starting transfers between devices, shards(): lax.all_to_all(lax.all_to_all(piece, 'virt', split_axis=0, concat_axis=2,...  8.66 us
    unnamed x20, local copies, waits for them, and re-layouts  7.88 us
  transfers between devices with their start and end apart: 4, of which 4 were waited for; matrix products, arithmetic and copies ran while one was open for 9% of the time, Pallas kernels for 0%

commit v1 on v0

v1 whole, which is shorter than its diff:
```python
import jax
import jax.numpy as jnp
from jax import lax
from jax.experimental import pallas as pl
from jax.experimental.pallas import tpu as pltpu
from jax.sharding import PartitionSpec as P

IRREPS = 8
NV = 512
BLK = 64
CS = 16
SLABS = 2
PCAP = 1024
KQ = 256
VMEM = 48 * 1024 * 1024
ABLK = 64
RBLK = 256


def regroup_kernel(pair_ref, x_ref, *refs):
    outs, (perm, held) = refs[:10], refs[10:]
    slab = pl.program_id(0)
    rows = ABLK * IRREPS

    @pl.when((slab == 0) & (pl.program_id(1) == 0))
    def _():
        to = lax.broadcasted_iota(jnp.int32, (rows, rows), 0)
        source = lax.broadcasted_iota(jnp.int32, (rows, rows), 1)
        perm[...] = jnp.where((to % ABLK) * IRREPS + to // ABLK == source, 1.0, 0.0).astype(jnp.bfloat16)

    moved = jnp.dot(perm[...], x_ref[0], preferred_element_type=jnp.float32)
    held[...] = moved.astype(jnp.bfloat16).reshape(IRREPS, ABLK, KQ)
    me = pair_ref[0]
    for parity in range(2):
        own, plus, minus, far0, far1 = outs[5 * parity : 5 * parity + 5]
        own[0] = held[2 * me + parity]
        plus[0] = held[2 * ((me + 1) % 4) + parity]
        minus[0] = held[2 * ((me + 3) % 4) + parity]
        far = 2 * ((me + 2) % 4) + parity

        @pl.when(slab == 0)
        def _():
            far0[...] = held[far]

        @pl.when(slab == 1)
        def _():
            far1[...] = held[far]


def regroup(pair_id, integrals):
    blocks = NV // ABLK
    both = jax.ShapeDtypeStruct((SLABS, NV, KQ), jnp.bfloat16)
    one = jax.ShapeDtypeStruct((NV, KQ), jnp.bfloat16)
    both_spec = pl.BlockSpec((1, ABLK, KQ), lambda s, i, me: (s, i, 0))
    far0_spec = pl.BlockSpec((ABLK, KQ), lambda s, i, me: (jnp.where(s == 0, i, blocks - 1), 0))
    far1_spec = pl.BlockSpec((ABLK, KQ), lambda s, i, me: (jnp.where(s == 1, i, 0), 0))
    flat = integrals.reshape(SLABS, NV * IRREPS, KQ)
    return pl.pallas_call(
        regroup_kernel,
        grid_spec=pltpu.PrefetchScalarGridSpec(
            num_scalar_prefetch=1,
            grid=(SLABS, blocks),
            in_specs=[pl.BlockSpec((1, ABLK * IRREPS, KQ), lambda s, i, me: (s, i, 0))],
            out_specs=[both_spec, both_spec, both_spec, far0_spec, far1_spec] * 2,
            scratch_shapes=[
                pltpu.VMEM((ABLK * IRREPS, ABLK * IRREPS), jnp.bfloat16),
                pltpu.VMEM((IRREPS, ABLK, KQ), jnp.bfloat16),
            ],
        ),
        out_shape=[both, both, both, one, one] * 2,
        compiler_params=pltpu.CompilerParams(vmem_limit_bytes=VMEM),
        name="regroup",
    )(pair_id, flat)


def ladder_kernel(pair_ref, own, left, right, far0, far1, amp, cols, rows, send, energy):
    me = pair_ref[0]

    def term(block, slab, source):
        at = pl.multiple_of(source * KQ, KQ)
        return lax.dot_general(
            block,
            amp[slab, :, pl.ds(at, KQ)],
            (((1,), (1,)), ((), ())),
            preferred_element_type=jnp.float32,
        )

    total = None
    for slab in range(SLABS):
        far = far0 if slab == 0 else far1
        for block, shift in ((own[slab], 0), (left[slab], 3), (right[slab], 1), (far[...], 2)):
            piece = term(block, slab, (me + shift) % 4)
            total = piece if total is None else total + piece
    denom = cols[:, 0:1] - rows[0:1, :]
    live = (cols[:, 1:2] * rows[1:2, :]) > 0.5
    ratio = jnp.where(live, total / denom, 0.0)
    send[...] = ratio.astype(jnp.bfloat16)
    energy[...] = jnp.sum(ratio * total, axis=0, keepdims=True) / (NV * BLK)


def ladder(pair_id, pieces, amp, cols, rows):
    whole = lambda *shape: pl.BlockSpec(shape, lambda i, me: (0,) * len(shape))
    return pl.pallas_call(
        ladder_kernel,
        grid_spec=pltpu.PrefetchScalarGridSpec(
            num_scalar_prefetch=1,
            grid=(PCAP // RBLK,),
            in_specs=[
                whole(SLABS, NV, KQ),
                whole(SLABS, NV, KQ),
                whole(SLABS, NV, KQ),
                whole(NV, KQ),
                whole(NV, KQ),
                pl.BlockSpec((SLABS, RBLK, 4 * KQ), lambda i, me: (0, i, 0)),
                whole(NV, 8),
                pl.BlockSpec((8, RBLK), lambda i, me: (0, i)),
            ],
            out_specs=[
                pl.BlockSpec((NV, RBLK), lambda i, me: (0, i)),
                pl.BlockSpec((1, RBLK), lambda i, me: (0, i)),
            ],
        ),
        out_shape=[
            jax.ShapeDtypeStruct((NV, PCAP), jnp.bfloat16),
            jax.ShapeDtypeStruct((1, PCAP), jnp.float32),
        ],
        compiler_params=pltpu.CompilerParams(vmem_limit_bytes=VMEM),
        cost_estimate=pl.CostEstimate(
            flops=2 * NV * PCAP * 2048, bytes_accessed=7 << 20, transcendentals=0
        ),
        name="ladder",
    )(pair_id, *pieces, amp, cols, rows)


def place_kernel(first, second, out, perm):
    @pl.when((pl.program_id(0) == 0) & (pl.program_id(1) == 0))
    def _():
        source = lax.broadcasted_iota(jnp.int32, (NV, NV), 0)
        to = lax.broadcasted_iota(jnp.int32, (NV, NV), 1)
        perm[...] = jnp.where((source % 8) * BLK + source // 8 == to, 1.0, 0.0).astype(jnp.bfloat16)

    def put(block):
        out[0] = lax.dot_general(
            block[...], perm[...], (((0,), (0,)), ((), ())), preferred_element_type=jnp.float32
        ).astype(jnp.bfloat16)

    @pl.when(pl.program_id(0) == 0)
    def _():
        put(first)

    @pl.when(pl.program_id(0) == 1)
    def _():
        put(second)


def place(first, second):
    steps = PCAP // RBLK
    return pl.pallas_call(
        place_kernel,
        grid=(2, steps),
        in_specs=[
            pl.BlockSpec((NV, RBLK), lambda h, i: (0, jnp.where(h == 0, i, steps - 1))),
            pl.BlockSpec((NV, RBLK), lambda h, i: (0, jnp.where(h == 1, i, 0))),
        ],
        out_specs=pl.BlockSpec((1, RBLK, NV), lambda h, i: (h, i, 0)),
        out_shape=jax.ShapeDtypeStruct((2, PCAP, NV), jnp.bfloat16),
        scratch_shapes=[pltpu.VMEM((NV, NV), jnp.bfloat16)],
        compiler_params=pltpu.CompilerParams(vmem_limit_bytes=VMEM),
        name="place",
    )(first, second)


def pick(ids, table):
    onehot = ids[..., None] == jnp.arange(table.shape[0], dtype=jnp.int32)
    return jnp.sum(jnp.where(onehot, table, 0), axis=-1)


def step(value, by):
    return lax.ppermute(value, "pair", [(i, (i + by) % 4) for i in range(4)])


def shards(amplitudes, integrals, virt_counts, pair_counts, pair_list, eps_occ, eps_virt):
    me = lax.axis_index("pair")
    virt = lax.axis_index("virt")
    pair_id = me.astype(jnp.int32)[None]
    irrep_ids = me * 2 + jnp.arange(2, dtype=jnp.int32)

    sends = regroup(pair_id, integrals)

    slots = jnp.arange(BLK, dtype=jnp.int32)
    live_d = slots[None, :] < pick(irrep_ids, virt_counts)[:, None]
    dmask = jnp.tile(live_d, (1, CS)).astype(jnp.bfloat16)

    a_irrep = jnp.arange(NV, dtype=jnp.int32) // BLK
    a_slot = jnp.arange(NV, dtype=jnp.int32) % BLK
    b_irrep = jnp.bitwise_xor(jnp.arange(IRREPS, dtype=jnp.int32)[None, :], irrep_ids[:, None])
    eps_at = lax.dynamic_slice_in_dim(eps_virt.reshape(IRREPS, BLK), virt, 1, axis=1)[:, 0]
    eps_b = jnp.repeat(pick(b_irrep, eps_at), BLK, axis=1)
    live_b = jnp.repeat(virt < pick(b_irrep, virt_counts), BLK, axis=1)
    live_a = a_slot < jnp.repeat(virt_counts, BLK)
    col_eps = eps_virt[None, :] + eps_b
    col_live = (live_a[None, :] & live_b).astype(jnp.float32)
    cols = jnp.pad(jnp.stack([col_eps, col_live], axis=-1), ((0, 0), (0, 0), (0, 6)))
    occ_terms = pick(pair_list, eps_occ)
    occ = occ_terms[:, :, 0] + occ_terms[:, :, 1]
    row_live = (
        jnp.arange(PCAP, dtype=jnp.int32)[None, :] < pick(irrep_ids, pair_counts)[:, None]
    ).astype(jnp.float32)
    rows = jnp.pad(jnp.stack([occ, row_live], axis=1), ((0, 0), (0, 6), (0, 0)))

    def exchange(own, plus, minus, far0, far1):
        far0, far1 = step(far0, 1), step(far1, -1)
        left, right = step(plus, 1), step(minus, -1)
        return own, left, right, step(far0, 1), step(far1, -1)

    def masked(parity):
        return jnp.transpose(amplitudes[parity] * dmask[parity][None, None, :], (1, 0, 2))

    even, odd = sends[:5], sends[5:]
    even = exchange(*even)
    even, odd = lax.optimization_barrier((even, odd))
    odd = exchange(*odd)
    send, energy0 = ladder(pair_id, even, masked(0), cols[0], rows[0])
    first = lax.all_to_all(send, "virt", 0, 0, tiled=True)
    first, odd = lax.optimization_barrier((first, odd))
    send, energy1 = ladder(pair_id, odd, masked(1), cols[1], rows[1])
    second = lax.all_to_all(send, "virt", 0, 0, tiled=True)
    terms = jnp.concatenate([energy0, energy1], axis=0).reshape(2, 64, 16)
    terms = jnp.transpose(terms, (1, 0, 2)).reshape(64, 32)
    terms = lax.all_to_all(terms, "virt", 0, 0, tiled=True)
    energy = jnp.sum(terms, axis=0).reshape(2, 16)
    return place(first, second), energy


def solution(mesh):
    placed = (
        P("pair", None, None, None),
        P(None, None, None, ("virt", "pair")),
        P(),
        P(),
        P("pair", None, None),
        P(),
        P(),
    )
    return jax.shard_map(
        shards,
        mesh=mesh,
        in_specs=placed,
        out_specs=(P("pair", None, "virt"), P("pair", "virt")),
        check_vma=False,
    )
```

time: 348 us -> 174 us (0.50); the launches traced: 343 us -> 173 us
  waiting for transfers between devices: 192 us -> 50.2 us
  blocking collectives: 64.1 us -> 21.4 us
  Pallas kernels: 0 us -> 28.2 us
  starting transfers between devices: 14.7 us -> 37.1 us
  local copies, waits for them, and re-layouts: 41.1 us -> 20.3 us
  between operations: 14.2 us -> 0.84 us
  matrix products: 6.02 us -> 0 us
  other arithmetic: 11.1 us -> 15 us
    unnamed x2 -> x0, waiting for transfers between devices: 129 us -> none
    all_to_all x1, blocking collectives: 64.1 us -> 21.4 us  [shards(): terms = lax.all_to_all(terms, 'virt', 0, 0, tiled=True)]
    all_to_all x3 -> x2, waiting for transfers between devices: 63.2 us -> 27.8 us  [the longest x1 27.8 us: shards(): second = lax.all_to_all(send, 'virt', 0, 0, tiled=True)]
    pallas_call x0 -> x4, Pallas kernels: none -> 28.2 us  [the longest x1 12 us: regroup(): pl.pallas_call(regroup_kernel, grid_spec=pltpu.PrefetchScalarGridSpec(num...]
    all_to_all x8 -> x1, local copies, waits for them, and re-layouts: 26.8 us -> 0.08 us  [shards(): terms = lax.all_to_all(terms, 'virt', 0, 0, tiled=True)]
    ppermute x0 -> x12, waiting for transfers between devices: none -> 22.4 us  [step(): return lax.ppermute(value, 'pair', [(i, (i + by) % 4) for i in range(4)])]
    ppermute x0 -> x12, starting transfers between devices: none -> 17.4 us  [step(): return lax.ppermute(value, 'pair', [(i, (i + by) % 4) for i in range(4)])]
    mul x1 -> x0, other arithmetic: 9.31 us -> none  [shards(): masked = amplitudes * dmask[:, None, None, :]]
  transfers between devices with their start and end apart: 4 -> 14, of which waited for: 4 -> 4; matrix products, arithmetic and copies ran while one was open for 9% -> 16% of each run, Pallas kernels for 0% -> 0%
where the time goes in v1:
time: 174 us; the launch traced here: 173 us
  waiting for transfers between devices  50.2 us (29%)
  starting transfers between devices  37.1 us (21%)
  Pallas kernels  28.2 us (16%)
  blocking collectives  21.4 us (12%)
  local copies, waits for them, and re-layouts  20.3 us (12%)
  other arithmetic  15 us (9%)
    all_to_all x1, waiting for transfers between devices, shards(): second = lax.all_to_all(send, 'virt', 0, 0, tiled=True)  27.8 us
    ppermute x12, waiting for transfers between devices, step(): return lax.ppermute(value, 'pair', [(i, (i + by) % 4) for i in range(4)])  22.4 us
    all_to_all x1, blocking collectives, shards(): terms = lax.all_to_all(terms, 'virt', 0, 0, tiled=True)  21.4 us
    ppermute x12, starting transfers between devices, step(): return lax.ppermute(value, 'pair', [(i, (i + by) % 4) for i in range(4)])  17.4 us
    all_to_all x1, starting transfers between devices, shards(): first = lax.all_to_all(send, 'virt', 0, 0, tiled=True)  15 us
    pallas_call x1, Pallas kernels, regroup(): pl.pallas_call(regroup_kernel, grid_spec=pltpu.PrefetchScalarGridSpec(num...  12 us
    pallas_call x2, Pallas kernels, ladder(): pl.pallas_call(ladder_kernel, grid_spec=pltpu.PrefetchScalarGridSpec(num_...  11.3 us
    slice x1, local copies, waits for them, and re-layouts, masked(): amplitudes[parity] * dmask[parity][None, None, :]  8.43 us
  transfers between devices with their start and end apart: 14, of which 4 were waited for; matrix products, arithmetic and copies ran while one was open for 16% of the time, Pallas kernels for 0%

profile of v1, /device:TPU:1, one launch (start us, length us, event | category | flops | bytes accessed | tf_op | source)
XLA Modules:
  0.0 173.1 jit_solution(3295468751215118070)
XLA Ops:
  0.6 12.0 %regroup.1 = (bf16[2,512,256]{2,1,0:T(8,128)(2,1)S(1)}, bf16[2,512,256]{2,1,0:T(8,128)(2,1)}, bf16[2,512,256]{2,1,0:T(8,128)(2,1)}, bf16[512,256]{1,0:T(8,128)(2...) custom-call(s32[1]{0:T(128)} %bitcast.pair_ref, ...), custom_call_target="tpu_custom_call" | custom-call | tf_op jit(solution)/shard_map/regroup/pallas_call | solution.py:58
  14.1 2.1 %collective-permute-start = (bf16[2,512,256]{2,1,0:T(8,128)(2,1)}, bf16[2,512,256]{2,1,0:T(8,128)(2,1)S(1)}, u32[]{:S(2)}, u32[]{:S(2)}) collective-permute-start(bf16[2,512,256]{2,1,0:T(8,128)(2,1)} %get-tuple-element.33), channel_id=1, source_target_pairs={{0,1},{1,2},{2,3},{3,0},{4,5},{5,6},{6,7},{7,4},{8,9},{9,10},{10,1... | collective-permute-start | bytes 1572872 | tf_op jit(solution)/shard_map/ppermute | solution.py:179
  16.2 1.4 collective-permute-start.1
  17.7 2.7 %collective-permute-start.4 = (bf16[512,256]{1,0:T(8,128)(2,1)S(1)}, bf16[512,256]{1,0:T(8,128)(2,1)}, u32[]{:S(2)}, u32[]{:S(2)}) collective-permute-start(bf16[512,256]{1,0:T(8,128)(2,1)S(1)} %get-tuple-element.36), channel_id=1, source_target_pairs={{0,3},{1,0},{2,1},{3,2},{4,7},{5,4},{6,5},{7,6},{8,11},{9,8},{10,9... | collective-permute-start | bytes 786440 | tf_op jit(solution)/shard_map/ppermute | solution.py:179
  20.3 8.4 %fusion.10 = (bf16[1,1024,2,1024]{3,2,1,0:T(2,128)(2,1)}, bf16[1,1024,2,1024]{3,2,1,0:T(2,128)(2,1)}) fusion(bf16[2,1024,2,1024]{3,2,1,0:T(2,128)(2,1)} %param.7), kind=kLoop, calls=%fused_computation.41 | loop fusion | bytes 16777216 | tf_op jit(solution)/shard_map/slice | solution.py:217
  28.8 0.8 select_reduce_fusion.2
  31.2 0.7 broadcast_in_dim.72
  32.6 1.2 fusion.6
  34.3 1.3 reshape.217
  35.5 1.2 broadcast_add_fusion
  36.7 0.7 compare_convert_fusion
  37.5 1.7 fusion.4
  39.9 8.0 %fusion.1 = (bf16[2,1024,1024]{2,1,0:T(8,128)(2,1)}, bf16[2,1024,1024]{2,1,0:T(8,128)(2,1)}) fusion(bf16[1,1024,2,1024]{3,2,1,0:T(2,128)(2,1)} %get-tuple-element.64, bf16[1024]{0:T(1024)(128)(2,1)S(1)} %mul.27, bf16[1024]{0:T(1024)(128)(2,1)} %mul.24, bf16[1,1024,2,1024]{3,2,1,0:T(2,128)(2,1)} %get-tuple-element.65), kind=kLoop, calls=%fused_computation.2 | loop fusion | flops 4194304 | bytes 16781312 | tf_op jit(solution)/shard_map/transpose | solution.py:217
  48.0 2.7 %collective-permute-start.5 = (bf16[512,256]{1,0:T(8,128)(2,1)}, bf16[512,256]{1,0:T(8,128)(2,1)S(1)}, u32[]{:S(2)}, u32[]{:S(2)}) collective-permute-start(bf16[512,256]{1,0:T(8,128)(2,1)} %collective-permute-done.4), channel_id=1, source_target_pairs={{0,3},{1,0},{2,1},{3,2},{4,7},{5,4},{6,5},{7,6},{8,11},{9,8},{10,9... | collective-permute-start | bytes 786440 | tf_op jit(solution)/shard_map/ppermute | solution.py:179
  51.0 3.7 %collective-permute-done.3.far0 = bf16[512,256]{1,0:T(8,128)(2,1)S(1)} collective-permute-done((bf16[512,256]{1,0:T(8,128)(2,1)}, bf16[512,256]{1,0:T(8,128)(2,1)S(1)}, u32[]{:S(2)}, u32[]{:S(2)}) %collective-permute-start.3) | collective-permute-done | bytes 262176 | tf_op jit(solution)/shard_map/ppermute | solution.py:179
  54.7 5.7 %ladder.2 = (bf16[512,1024]{1,0:T(8,128)(2,1)}, f32[1,1024]{1,0:T(1,128)S(1)}) custom-call(s32[1]{0:T(128)} %bitcast.pair_ref, bf16[2,512,256]{2,1,0:T(8,128)(2,1)S(1)} %get-tuple-element.42.own, bf16[2,512,256]{2,1,0:T(8,128)(2,1)S(1)} %collective-permute-done.left, bf16[2,512,256]{2,1,0:T(8,128)(2,1)S(1)} %collective-permute-done.1.right, ...), custom_call_target="tpu_custom_call" | custom-call | flops 2147483648 | bytes 7340032 | tf_op jit(solution)/shard_map/ladder/pallas_call | solution.py:103
  60.3 15.0 %all-to-all-start = ((bf16[64,8,1024]{2,1,0:T(8,128)(2,1)}), bf16[64,8,1024]{2,1,0:T(8,128)(2,1)S(1)}, u32[]{:S(2)}, u32[]{:S(2)}) async-start(bf16[64,8,1024]{2,1,0:T(8,128)(2,1)} %bitcast.8), calls=%async_computation | async-start | bytes 2097152 | tf_op jit(solution)/shard_map/all_to_all | solution.py:224
  75.6 2.8 %collective-permute-start.7 = (bf16[2,512,256]{2,1,0:T(8,128)(2,1)S(1)}, bf16[2,512,256]{2,1,0:T(8,128)(2,1)S(1)}, u32[]{:S(2)}, u32[]{:S(2)}) collective-permute-start(bf16[2,512,256]{2,1,0:T(8,128)(2,1)S(1)} %get-tuple-element.50), channel_id=1, source_target_pairs={{0,3},{1,0},{2,1},{3,2},{4,7},{5,4},{6,5},{7,6},{8,11},{9,8},{10,9... | collective-permute-start | bytes 1572872 | tf_op jit(solution)/shard_map/ppermute | solution.py:179
  78.3 2.7 %collective-permute-start.10 = (bf16[512,256]{1,0:T(8,128)(2,1)}, bf16[512,256]{1,0:T(8,128)(2,1)S(1)}, u32[]{:S(2)}, u32[]{:S(2)}) collective-permute-start(bf16[512,256]{1,0:T(8,128)(2,1)} %copy-done.2), channel_id=1, source_target_pairs={{0,3},{1,0},{2,1},{3,2},{4,7},{5,4},{6,5},{7,6},{8,11},{9,8},{10,9... | collective-permute-start | bytes 786440 | tf_op jit(solution)/shard_map/ppermute | solution.py:179
  81.0 14.4 %collective-permute-done.8 = bf16[512,256]{1,0:T(8,128)(2,1)S(1)} collective-permute-done((bf16[512,256]{1,0:T(8,128)(2,1)}, bf16[512,256]{1,0:T(8,128)(2,1)S(1)}, u32[]{:S(2)}, u32[]{:S(2)}) %collective-permute-start.8) | collective-permute-done | bytes 262176 | tf_op jit(solution)/shard_map/ppermute | solution.py:179
  95.5 2.7 %collective-permute-start.11 = (bf16[512,256]{1,0:T(8,128)(2,1)S(1)}, bf16[512,256]{1,0:T(8,128)(2,1)S(1)}, u32[]{:S(2)}, u32[]{:S(2)}) collective-permute-start(bf16[512,256]{1,0:T(8,128)(2,1)S(1)} %collective-permute-done.10), channel_id=1, source_target_pairs={{0,3},{1,0},{2,1},{3,2},{4,7},{5,4},{6,5},{7,6},{8,11},{9,8},{10,9... | collective-permute-start | bytes 786440 | tf_op jit(solution)/shard_map/ppermute | solution.py:179
  98.1 0.8 copy-done
  98.9 4.2 %collective-permute-done.9.far0 = bf16[512,256]{1,0:T(8,128)(2,1)S(1)} collective-permute-done((bf16[512,256]{1,0:T(8,128)(2,1)S(1)}, bf16[512,256]{1,0:T(8,128)(2,1)S(1)}, u32[]{:S(2)}, u32[]{:S(2)}) %collective-permute-start.9) | collective-permute-done | bytes 262176 | tf_op jit(solution)/shard_map/ppermute | solution.py:179
  103.2 0.7 copy-done.4
  104.6 1.0 copy-done.1
  105.7 0.9 copy-done.5
  106.6 0.9 copy-done.7
  107.6 5.7 %ladder.3 = (bf16[512,1024]{1,0:T(8,128)(2,1)}, f32[1,1024]{1,0:T(1,128)S(1)}) custom-call(s32[1]{0:T(128)} %bitcast.pair_ref, bf16[2,512,256]{2,1,0:T(8,128)(2,1)S(1)} %get-tuple-element.54.own, bf16[2,512,256]{2,1,0:T(8,128)(2,1)S(1)} %collective-permute-done.6.left, bf16[2,512,256]{2,1,0:T(8,128)(2,1)S(1)} %copy-done.1, bf16[512,256]{1,0:T(8,128)(2,1)S(1)} %copy-done.5, ...), custom_call_target="tpu_custom_call" | custom-call | flops 2147483648 | bytes 7340032 | tf_op jit(solution)/shard_map/ladder/pallas_call | solution.py:103
  113.5 21.4 %all_to_all.32 = f32[64,1,32]{2,1,0:T(1,128)S(1)} all-to-all(f32[64,1,32]{2,1,0:T(1,128)S(1)} %copy.45), channel_id=1, replica_groups=mesh['virt'=64,'pair'=4] {'virt'}, dimensions={0} | all-to-all | bytes 16384 | tf_op jit(solution)/shard_map/all_to_all | solution.py:230
  134.8 4.8 %all-to-all-start.1 = ((bf16[64,8,1024]{2,1,0:T(8,128)(2,1)}), bf16[64,8,1024]{2,1,0:T(8,128)(2,1)S(1)}, u32[]{:S(2)}, u32[]{:S(2)}) async-start(bf16[64,8,1024]{2,1,0:T(8,128)(2,1)} %bitcast.15), calls=%async_computation.1 | async-start | bytes 2097152 | tf_op jit(solution)/shard_map/all_to_all | solution.py:227
  140.3 27.8 %all-to-all-done.1 = bf16[64,8,1024]{2,1,0:T(8,128)(2,1)S(1)} async-done(((bf16[64,8,1024]{2,1,0:T(8,128)(2,1)}), bf16[64,8,1024]{2,1,0:T(8,128)(2,1)S(1)}, u32[]{:S(2)}, u32[]{:S(2)}) %all-to-all-start.1) | async-done | bytes 1048608 | tf_op jit(solution)/shard_map/all_to_all | solution.py:227
  168.2 4.9 %place.1 = bf16[2,1024,512]{2,1,0:T(8,128)(2,1)} custom-call(bf16[512,1024]{1,0:T(8,128)(2,1)S(1)} %bitcast.38, bf16[512,1024]{1,0:T(8,128)(2,1)S(1)} %bitcast.39), custom_call_target="tpu_custom_call" | custom-call | tf_op jit(solution)/shard_map/place/pallas_call | solution.py:158
  (60 shorter events, 7.3 us)
Async XLA Ops:
  12.6 0.7 copy-start.2
  13.4 0.7 copy-start.3
  14.1 36.9 %collective-permute-start = (bf16[2,512,256]{2,1,0:T(8,128)(2,1)}, bf16[2,512,256]{2,1,0:T(8,128)(2,1)S(1)}, u32[]{:S(2)}, u32[]{:S(2)}) collective-permute-start(bf16[2,512,256]{2,1,0:T(8,128)(2,1)} %get-tuple-element.33), channel_id=1, source_target_pairs={{0,1},{1,2},{2,3},{3,0},{4,5},{5,6},{6,7},{7,4},{8,9},{9,10},{10,1... | collective-permute-start | bytes 1572872 | tf_op jit(solution)/shard_map/ppermute | solution.py:179
  16.2 34.8 %collective-permute-start.1 = (bf16[2,512,256]{2,1,0:T(8,128)(2,1)}, bf16[2,512,256]{2,1,0:T(8,128)(2,1)S(1)}, u32[]{:S(2)}, u32[]{:S(2)}) collective-permute-start(bf16[2,512,256]{2,1,0:T(8,128)(2,1)} %get-tuple-element.34), channel_id=1, source_target_pairs={{0,3},{1,0},{2,1},{3,2},{4,7},{5,4},{6,5},{7,6},{8,11},{9,8},{10,9... | collective-permute-start | bytes 1572872 | tf_op jit(solution)/shard_map/ppermute | solution.py:179
  17.6 30.3 %collective-permute-start.2 = (bf16[512,256]{1,0:T(8,128)(2,1)}, bf16[512,256]{1,0:T(8,128)(2,1)}, u32[]{:S(2)}, u32[]{:S(2)}) collective-permute-start(bf16[512,256]{1,0:T(8,128)(2,1)} %get-tuple-element.35), channel_id=1, source_target_pairs={{0,1},{1,2},{2,3},{3,0},{4,5},{5,6},{6,7},{7,4},{8,9},{9,10},{10,1... | collective-permute-start | bytes 786440 | tf_op jit(solution)/shard_map/ppermute | solution.py:179
  17.7 11.1 %copy-start.9 = (s32[8]{0:T(128)S(1)}, s32[8]{0:T(128)}, u32[]{:S(2)}) copy-start(s32[8]{0:T(128)} %param.9) | copy-start | bytes 100
  17.7 11.1 %copy-start.10 = (s32[8]{0:T(128)S(1)}, s32[8]{0:T(128)}, u32[]{:S(2)}) copy-start(s32[8]{0:T(128)} %param.10) | copy-start | bytes 100
  17.7 16.1 %copy-start.8 = (f32[512]{0:T(512)S(1)}, f32[512]{0:T(512)}, u32[]{:S(2)}) copy-start(f32[512]{0:T(512)} %param.13) | copy-start | bytes 6148
  17.7 30.3 %collective-permute-start.4 = (bf16[512,256]{1,0:T(8,128)(2,1)S(1)}, bf16[512,256]{1,0:T(8,128)(2,1)}, u32[]{:S(2)}, u32[]{:S(2)}) collective-permute-start(bf16[512,256]{1,0:T(8,128)(2,1)S(1)} %get-tuple-element.36), channel_id=1, source_target_pairs={{0,3},{1,0},{2,1},{3,2},{4,7},{5,4},{6,5},{7,6},{8,11},{9,8},{10,9... | collective-permute-start | bytes 786440 | tf_op jit(solution)/shard_map/ppermute | solution.py:179
  47.9 6.7 %collective-permute-start.3 = (bf16[512,256]{1,0:T(8,128)(2,1)}, bf16[512,256]{1,0:T(8,128)(2,1)S(1)}, u32[]{:S(2)}, u32[]{:S(2)}) collective-permute-start(bf16[512,256]{1,0:T(8,128)(2,1)} %collective-permute-done.2), channel_id=1, source_target_pairs={{0,1},{1,2},{2,3},{3,0},{4,5},{5,6},{6,7},{7,4},{8,9},{9,10},{10,1... | collective-permute-start | bytes 786440 | tf_op jit(solution)/shard_map/ppermute | solution.py:179
  48.0 6.6 %collective-permute-start.5 = (bf16[512,256]{1,0:T(8,128)(2,1)}, bf16[512,256]{1,0:T(8,128)(2,1)S(1)}, u32[]{:S(2)}, u32[]{:S(2)}) collective-permute-start(bf16[512,256]{1,0:T(8,128)(2,1)} %collective-permute-done.4), channel_id=1, source_target_pairs={{0,3},{1,0},{2,1},{3,2},{4,7},{5,4},{6,5},{7,6},{8,11},{9,8},{10,9... | collective-permute-start | bytes 786440 | tf_op jit(solution)/shard_map/ppermute | solution.py:179
  60.3 44.3 %all-to-all-start = ((bf16[64,8,1024]{2,1,0:T(8,128)(2,1)}), bf16[64,8,1024]{2,1,0:T(8,128)(2,1)S(1)}, u32[]{:S(2)}, u32[]{:S(2)}) async-start(bf16[64,8,1024]{2,1,0:T(8,128)(2,1)} %bitcast.8), calls=%async_computation | async-start | bytes 2097152 | tf_op jit(solution)/shard_map/all_to_all | solution.py:224
  75.3 22.8 %collective-permute-start.6 = (bf16[2,512,256]{2,1,0:T(8,128)(2,1)S(1)}, bf16[2,512,256]{2,1,0:T(8,128)(2,1)S(1)}, u32[]{:S(2)}, u32[]{:S(2)}) collective-permute-start(bf16[2,512,256]{2,1,0:T(8,128)(2,1)S(1)} %get-tuple-element.49), channel_id=1, source_target_pairs={{0,1},{1,2},{2,3},{3,0},{4,5},{5,6},{6,7},{7,4},{8,9},{9,10},{10,1... | collective-permute-start | bytes 1572872 | tf_op jit(solution)/shard_map/ppermute | solution.py:179
  75.6 22.6 %collective-permute-start.7 = (bf16[2,512,256]{2,1,0:T(8,128)(2,1)S(1)}, bf16[2,512,256]{2,1,0:T(8,128)(2,1)S(1)}, u32[]{:S(2)}, u32[]{:S(2)}) collective-permute-start(bf16[2,512,256]{2,1,0:T(8,128)(2,1)S(1)} %get-tuple-element.50), channel_id=1, source_target_pairs={{0,3},{1,0},{2,1},{3,2},{4,7},{5,4},{6,5},{7,6},{8,11},{9,8},{10,9... | collective-permute-start | bytes 1572872 | tf_op jit(solution)/shard_map/ppermute | solution.py:179
  78.3 17.1 %collective-permute-start.8 = (bf16[512,256]{1,0:T(8,128)(2,1)}, bf16[512,256]{1,0:T(8,128)(2,1)S(1)}, u32[]{:S(2)}, u32[]{:S(2)}) collective-permute-start(bf16[512,256]{1,0:T(8,128)(2,1)} %copy-done.3), channel_id=1, source_target_pairs={{0,1},{1,2},{2,3},{3,0},{4,5},{5,6},{6,7},{7,4},{8,9},{9,10},{10,1... | collective-permute-start | bytes 786440 | tf_op jit(solution)/shard_map/ppermute | solution.py:179
  78.3 17.1 %collective-permute-start.10 = (bf16[512,256]{1,0:T(8,128)(2,1)}, bf16[512,256]{1,0:T(8,128)(2,1)S(1)}, u32[]{:S(2)}, u32[]{:S(2)}) collective-permute-start(bf16[512,256]{1,0:T(8,128)(2,1)} %copy-done.2), channel_id=1, source_target_pairs={{0,3},{1,0},{2,1},{3,2},{4,7},{5,4},{6,5},{7,6},{8,11},{9,8},{10,9... | collective-permute-start | bytes 786440 | tf_op jit(solution)/shard_map/ppermute | solution.py:179
  95.4 7.7 %collective-permute-start.9 = (bf16[512,256]{1,0:T(8,128)(2,1)S(1)}, bf16[512,256]{1,0:T(8,128)(2,1)S(1)}, u32[]{:S(2)}, u32[]{:S(2)}) collective-permute-start(bf16[512,256]{1,0:T(8,128)(2,1)S(1)} %collective-permute-done.8), channel_id=1, source_target_pairs={{0,1},{1,2},{2,3},{3,0},{4,5},{5,6},{6,7},{7,4},{8,9},{9,10},{10,1... | collective-permute-start | bytes 786440 | tf_op jit(solution)/shard_map/ppermute | solution.py:179
  95.5 8.4 %collective-permute-start.11 = (bf16[512,256]{1,0:T(8,128)(2,1)S(1)}, bf16[512,256]{1,0:T(8,128)(2,1)S(1)}, u32[]{:S(2)}, u32[]{:S(2)}) collective-permute-start(bf16[512,256]{1,0:T(8,128)(2,1)S(1)} %collective-permute-done.10), channel_id=1, source_target_pairs={{0,3},{1,0},{2,1},{3,2},{4,7},{5,4},{6,5},{7,6},{8,11},{9,8},{10,9... | collective-permute-start | bytes 786440 | tf_op jit(solution)/shard_map/ppermute | solution.py:179
  98.1 0.8 copy-start
  103.2 0.7 copy-start.4
  103.9 0.7 copy-start.6
  104.6 1.0 copy-start.1
  105.7 0.9 copy-start.5
  106.6 0.9 copy-start.7
  134.8 33.3 %all-to-all-start.1 = ((bf16[64,8,1024]{2,1,0:T(8,128)(2,1)}), bf16[64,8,1024]{2,1,0:T(8,128)(2,1)S(1)}, u32[]{:S(2)}, u32[]{:S(2)}) async-start(bf16[64,8,1024]{2,1,0:T(8,128)(2,1)} %bitcast.15), calls=%async_computation.1 | async-start | bytes 2097152 | tf_op jit(solution)/shard_map/all_to_all | solution.py:227

commit v2 on v0

v2 whole, which is shorter than its diff:
```python
import jax
import jax.numpy as jnp
from jax import lax
from jax.experimental import pallas as pl
from jax.experimental.pallas import tpu as pltpu
from jax.sharding import PartitionSpec as P

IRREPS = 8
NV = 512
BLK = 64
SLABS = 2
PCAP = 1024
KQ = 256
KS = 1024
VIRTS = 64
OWN = NV // VIRTS
MINE = PCAP // VIRTS
VMEM = 48 * 1024 * 1024
ABLK = 256
SUB = 32
RBLK = 256
EXTRA = 128


def iota(shape, axis):
    return lax.broadcasted_iota(jnp.int32, shape, axis)


def regroup_kernel(pair_ref, x_ref, even, own, plus, far, minus, perm, held):
    rows = SUB * IRREPS

    @pl.when((pl.program_id(0) == 0) & (pl.program_id(1) == 0))
    def _():
        to, source = iota((rows, rows), 0), iota((rows, rows), 1)
        at = (to & (SUB - 1)) * IRREPS + (to >> 5)
        perm[...] = jnp.where(at == source, 1.0, 0.0).astype(jnp.bfloat16)

    for sub in range(ABLK // SUB):
        block = x_ref[0, sub * rows : (sub + 1) * rows, :]
        moved = jnp.dot(perm[...], block, preferred_element_type=jnp.float32).astype(jnp.bfloat16)
        at = slice(sub * SUB, (sub + 1) * SUB)
        for pair in range(4):
            even[pair, 0, at, :] = moved[(2 * pair) * SUB : (2 * pair + 1) * SUB]
            held[pair, at, :] = moved[(2 * pair + 1) * SUB : (2 * pair + 2) * SUB]
    me = pair_ref[0]
    own[0] = held[me]
    plus[0] = held[(me + 1) % 4]
    far[0] = held[(me + 2) % 4]
    minus[0] = held[(me + 3) % 4]


def regroup(pair_id, integrals):
    each = jax.ShapeDtypeStruct((SLABS, NV, KQ), jnp.bfloat16)
    spec = pl.BlockSpec((1, ABLK, KQ), lambda s, i, me: (s, i, 0))
    return pl.pallas_call(
        regroup_kernel,
        grid_spec=pltpu.PrefetchScalarGridSpec(
            num_scalar_prefetch=1,
            grid=(SLABS, NV // ABLK),
            in_specs=[pl.BlockSpec((1, ABLK * IRREPS, KQ), lambda s, i, me: (s, i, 0))],
            out_specs=[pl.BlockSpec((4, 1, ABLK, KQ), lambda s, i, me: (0, s, i, 0))] + [spec] * 4,
            scratch_shapes=[
                pltpu.VMEM((SUB * IRREPS, SUB * IRREPS), jnp.bfloat16),
                pltpu.VMEM((4, ABLK, KQ), jnp.bfloat16),
            ],
        ),
        out_shape=[jax.ShapeDtypeStruct((4, SLABS, NV, KQ), jnp.bfloat16)] + [each] * 4,
        compiler_params=pltpu.CompilerParams(vmem_limit_bytes=VMEM),
        name="regroup",
    )(pair_id, integrals.reshape(SLABS, NV * IRREPS, KQ))


def ladder_kernel(parity, ids, virt_counts, pair_counts, eps, *refs):
    if parity == 0:
        moved, amp, eps_a, occ, send, energy, held = refs
    else:
        own, left, far, right, amp, eps_a, occ, energy0, send, held, energies = refs
    me, virt = ids[0], ids[1]
    h = 2 * me + parity
    at_row = pl.program_id(0)

    @pl.when(at_row == 0)
    def _():
        mask = jnp.where((iota((1, KQ), 1) & (BLK - 1)) < virt_counts[h], 1.0, 0.0).astype(jnp.bfloat16)
        for slab in range(SLABS):
            if parity == 0:
                for source in range(4):
                    to = slab * KS + source * KQ
                    held[:, to : to + KQ] = moved[source, slab] * mask
            else:
                for shift, piece in ((0, own), (3, left), (2, far), (1, right)):
                    to = pl.multiple_of(slab * KS + ((me + shift) % 4) * KQ, KQ)
                    held[:, pl.ds(to, KQ)] = piece[slab] * mask

    total = None
    for slab in range(SLABS):
        term = lax.dot_general(
            held[:, slab * KS : (slab + 1) * KS],
            amp[slab, 0],
            (((1,), (1,)), ((), ())),
            preferred_element_type=jnp.float32,
        )
        total = term if total is None else total + term
    columns = pl.ds(pl.multiple_of(at_row * RBLK, RBLK), RBLK)
    occ_row = occ[parity : parity + 1, :]
    slot = iota((BLK, RBLK), 0)
    live_row = at_row * RBLK + iota((BLK, RBLK), 1) < pair_counts[h]
    summed = jnp.zeros((1, RBLK), jnp.float32)
    for ha in range(IRREPS):
        hb = jnp.bitwise_xor(h, ha)
        part = total[ha * BLK : (ha + 1) * BLK]
        denom = (eps_a[ha * BLK : (ha + 1) * BLK, :] + eps[hb * BLK + virt]) - occ_row
        live_a = jnp.where(virt < virt_counts[hb], virt_counts[ha], 0)
        ratio = jnp.where((slot < live_a) & live_row, part / denom, 0.0)
        summed = summed + jnp.sum(ratio * part, axis=0, keepdims=True)
        ratio = ratio.astype(jnp.bfloat16)
        if parity == 0:
            send[ha * BLK : (ha + 1) * BLK, :] = ratio
        else:
            send[ha * BLK : (ha + 1) * BLK, columns] = ratio
    summed = summed / (NV * BLK)
    if parity == 0:
        energy[...] = summed
        return
    energies[1:2, columns] = summed

    @pl.when(at_row == PCAP // RBLK - 1)
    def _():
        energies[0:1, :] = energy0[...]
        value = energies[0:2, :]
        high = value.astype(jnp.bfloat16).astype(jnp.float32)
        rest = value - high
        middle = rest.astype(jnp.bfloat16).astype(jnp.float32)
        low = rest - middle
        pieces = jnp.concatenate([high, middle, low, jnp.zeros((2, PCAP), jnp.float32)], axis=0)
        spread = jnp.broadcast_to(pieces[None], (VIRTS, OWN, PCAP)).reshape(NV, PCAP)
        owner = (iota((NV, PCAP), 1) // MINE) == (iota((NV, PCAP), 0) // OWN)
        spread = jnp.where(owner, spread, 0.0).astype(jnp.bfloat16)
        lane = (iota((PCAP, EXTRA), 0) & (MINE - 1)) == iota((PCAP, EXTRA), 1)
        select = jnp.where(lane, 1.0, 0.0).astype(jnp.bfloat16)
        send[:, PCAP : PCAP + EXTRA] = jnp.dot(
            spread, select, preferred_element_type=jnp.float32
        ).astype(jnp.bfloat16)


def ladder(parity, scalars, pieces, amp, eps_a, occ, energy0=None):
    whole = lambda *shape: pl.BlockSpec(shape, lambda i, *_: (0,) * len(shape))
    in_specs = [whole(*piece.shape) for piece in pieces] + [
        pl.BlockSpec((SLABS, 1, RBLK, KS), lambda i, *_: (0, parity, i, 0)),
        whole(NV, 1),
        pl.BlockSpec((2, RBLK), lambda i, *_: (0, i)),
    ]
    args = [*scalars, *pieces, amp, eps_a, occ]
    scratch = [pltpu.VMEM((NV, SLABS * KS), jnp.bfloat16)]
    if parity == 0:
        out_specs = [
            pl.BlockSpec((NV, RBLK), lambda i, *_: (0, i)),
            pl.BlockSpec((1, RBLK), lambda i, *_: (0, i)),
        ]
        out_shape = [
            jax.ShapeDtypeStruct((NV, PCAP), jnp.bfloat16),
            jax.ShapeDtypeStruct((1, PCAP), jnp.float32),
        ]
    else:
        in_specs.append(whole(1, PCAP))
        args.append(energy0)
        out_specs = whole(NV, PCAP + EXTRA)
        out_shape = jax.ShapeDtypeStruct((NV, PCAP + EXTRA), jnp.bfloat16)
        scratch.append(pltpu.VMEM((8, PCAP), jnp.float32))
    return pl.pallas_call(
        lambda *refs: ladder_kernel(parity, *refs),
        grid_spec=pltpu.PrefetchScalarGridSpec(
            num_scalar_prefetch=4,
            grid=(PCAP // RBLK,),
            in_specs=in_specs,
            out_specs=out_specs,
            scratch_shapes=scratch,
        ),
        out_shape=out_shape,
        compiler_params=pltpu.CompilerParams(vmem_limit_bytes=VMEM),
        cost_estimate=pl.CostEstimate(
            flops=2 * NV * PCAP * SLABS * KS, bytes_accessed=7 << 20, transcendentals=0
        ),
        name="ladder",
    )(*args)


def put(block, out, perm):
    @pl.when(pl.program_id(0) == 0)
    def _():
        source, to = iota((NV, NV), 0), iota((NV, NV), 1)
        at = (source & (OWN - 1)) * BLK + (source >> 3)
        perm[...] = jnp.where(at == to, 1.0, 0.0).astype(jnp.bfloat16)

    out[0] = lax.dot_general(
        block[...], perm[...], (((0,), (0,)), ((), ())), preferred_element_type=jnp.float32
    ).astype(jnp.bfloat16)


def place_even_kernel(block, out, perm):
    put(block, out, perm)


def place_odd_kernel(block, extra, before, out, energy, perm):
    put(block, out, perm)

    @pl.when(pl.program_id(0) == 0)
    def _():
        values = extra[...].astype(jnp.float32)
        kind = iota((NV, EXTRA), 0) & (OWN - 1)
        for parity in range(2):
            mine = (kind < 6) & ((kind & 1) == parity)
            summed = jnp.sum(jnp.where(mine, values, 0.0), axis=0, keepdims=True)
            energy[parity : parity + 1, :] = summed[:, :MINE]


def place(parity, block, before=None):
    in_specs = [pl.BlockSpec((NV, RBLK), lambda i: (0, i))]
    out_spec = pl.BlockSpec((1, RBLK, NV), lambda i: (parity, i, 0))
    out = jax.ShapeDtypeStruct((2, PCAP, NV), jnp.bfloat16)
    common = dict(
        grid=(PCAP // RBLK,),
        scratch_shapes=[pltpu.VMEM((NV, NV), jnp.bfloat16)],
        compiler_params=pltpu.CompilerParams(vmem_limit_bytes=VMEM),
        cost_estimate=pl.CostEstimate(flops=2 * NV * NV * PCAP, bytes_accessed=2 << 20, transcendentals=0),
        name="place",
    )
    if parity == 0:
        return pl.pallas_call(place_even_kernel, in_specs=in_specs, out_specs=out_spec, out_shape=out, **common)(block)
    in_specs += [
        pl.BlockSpec((NV, EXTRA), lambda i: (0, PCAP // EXTRA)),
        pl.BlockSpec(memory_space=pl.ANY),
    ]
    return pl.pallas_call(
        place_odd_kernel,
        in_specs=in_specs,
        out_specs=[out_spec, pl.BlockSpec((2, MINE), lambda i: (0, 0))],
        out_shape=[out, jax.ShapeDtypeStruct((2, MINE), jnp.float32)],
        input_output_aliases={2: 0},
        **common,
    )(block, block, before)


def pick(ids, table):
    onehot = ids[..., None] == jnp.arange(table.shape[0], dtype=jnp.int32)
    return jnp.sum(jnp.where(onehot, table, 0), axis=-1)


def step(value, by):
    return lax.ppermute(value, "pair", [(i, (i + by) % 4) for i in range(4)])


def across(value):
    return lax.all_to_all(value, "virt", 0, 0, tiled=True)


def shards(amplitudes, integrals, virt_counts, pair_counts, pair_list, eps_occ, eps_virt):
    me = lax.axis_index("pair").astype(jnp.int32)
    virt = lax.axis_index("virt").astype(jnp.int32)
    even, own, plus, far, minus = regroup(me[None], integrals)
    even = lax.all_to_all(even, "pair", 0, 0, tiled=True)

    amp = jnp.transpose(amplitudes, (2, 0, 1, 3))
    occ_terms = pick(pair_list, eps_occ)
    occ = occ_terms[:, :, 0] + occ_terms[:, :, 1]
    eps_a = eps_virt[:, None]
    scalars = (jnp.stack([me, virt]), virt_counts, pair_counts, eps_virt)

    even, plus, far, minus = lax.optimization_barrier((even, plus, far, minus))
    left, far, right = step(plus, 1), step(far, 2), step(minus, 3)
    send, energy0 = ladder(0, scalars, (even,), amp, eps_a, occ)
    first = across(send)
    send = ladder(1, scalars, (own, left, far, right), amp, eps_a, occ, energy0)
    first, send = lax.optimization_barrier((first, send))
    second = across(send)
    out = place(0, first)
    return tuple(place(1, second, out))


def solution(mesh):
    placed = (
        P("pair", None, None, None),
        P(None, None, None, ("virt", "pair")),
        P(),
        P(),
        P("pair", None, None),
        P(),
        P(),
    )
    return jax.shard_map(
        shards,
        mesh=mesh,
        in_specs=placed,
        out_specs=(P("pair", None, "virt"), P("pair", "virt")),
        check_vma=False,
    )
```

time: 348 us -> 138 us (0.40); the launches traced: 343 us -> 137 us
  waiting for transfers between devices: 192 us -> 65.7 us
  blocking collectives: 64.1 us -> 0 us
  local copies, waits for them, and re-layouts: 41.1 us -> 12.5 us
  Pallas kernels: 0 us -> 23.5 us
  starting transfers between devices: 14.7 us -> 33.9 us
  between operations: 14.2 us -> 0.75 us
  other arithmetic: 11.1 us -> 1 us
  matrix products: 6.02 us -> 0 us
    unnamed x2 -> x0, waiting for transfers between devices: 129 us -> none
    all_to_all x1 -> x0, blocking collectives: 64.1 us -> none  [shards(): lax.all_to_all(piece, 'virt', split_axis=0, concat_axis=2, tiled=True)]
    all_to_all x8 -> x0, local copies, waits for them, and re-layouts: 26.8 us -> none  [the longest x6 24.8 us: shards(): lax.all_to_all(piece, 'virt', split_axis=0, concat_axis=2, tiled=True)]
    pallas_call x0 -> x5, Pallas kernels: none -> 23.5 us  [the longest x2 13.9 us: ladder(): pl.pallas_call(lambda *refs: ladder_kernel(parity, *refs), grid_spec=pltp...]
    ppermute x0 -> x3, waiting for transfers between devices: none -> 23 us  [step(): return lax.ppermute(value, 'pair', [(i, (i + by) % 4) for i in range(4)])]
    all_to_all x3, waiting for transfers between devices: 63.2 us -> 42.7 us  [the longest x2 28.7 us: across(): return lax.all_to_all(value, 'virt', 0, 0, tiled=True)]
    all_to_all x3, starting transfers between devices: 14.5 us -> 31 us  [the longest x2 25.9 us: across(): return lax.all_to_all(value, 'virt', 0, 0, tiled=True)]
    mul x1 -> x0, other arithmetic: 9.31 us -> none  [shards(): masked = amplitudes * dmask[:, None, None, :]]
  transfers between devices with their start and end apart: 4 -> 6, of which waited for: 4 -> 5; matrix products, arithmetic and copies ran while one was open for 9% -> 8% of each run, Pallas kernels for 0% -> 7%
where the time goes in v2:
time: 138 us; the launch traced here: 137 us
  waiting for transfers between devices  65.7 us (48%)
  starting transfers between devices  33.9 us (25%)
  Pallas kernels  23.5 us (17%)
  local copies, waits for them, and re-layouts  12.5 us (9%)
    all_to_all x2, waiting for transfers between devices, across(): return lax.all_to_all(value, 'virt', 0, 0, tiled=True)  28.7 us
    all_to_all x2, starting transfers between devices, across(): return lax.all_to_all(value, 'virt', 0, 0, tiled=True)  25.9 us
    ppermute x3, waiting for transfers between devices, step(): return lax.ppermute(value, 'pair', [(i, (i + by) % 4) for i in range(4)])  23 us
    all_to_all x1, waiting for transfers between devices, shards(): even = lax.all_to_all(even, 'pair', 0, 0, tiled=True)  14 us
    pallas_call x2, Pallas kernels, ladder(): pl.pallas_call(lambda *refs: ladder_kernel(parity, *refs), grid_spec=pltp...  13.9 us
    unnamed x21, local copies, waits for them, and re-layouts  12.4 us
    all_to_all x1, starting transfers between devices, shards(): even = lax.all_to_all(even, 'pair', 0, 0, tiled=True)  5.14 us
    pallas_call x1, Pallas kernels, regroup(): pl.pallas_call(regroup_kernel, grid_spec=pltpu.PrefetchScalarGridSpec(num...  4.18 us
  transfers between devices with their start and end apart: 6, of which 5 were waited for; matrix products, arithmetic and copies ran while one was open for 8% of the time, Pallas kernels for 7%

profile of v2, /device:TPU:1, one launch (start us, length us, event | category | flops | bytes accessed | tf_op | source)
XLA Modules:
  0.0 137.4 jit_solution(8852834890383856885)
XLA Ops:
  0.6 4.2 %regroup.1 = (bf16[4,2,512,256]{3,2,1,0:T(8,128)(2,1)S(1)}, bf16[2,512,256]{2,1,0:T(8,128)(2,1)S(1)}, bf16[2,512,256]{2,1,0:T(8,128)(2,1)S(1)}, bf16[2,512,256]{2,1,0:T(8,128)(2,1)S(1)}, bf16[2,512,256]{2,1,0:T(8,128)(2,1)S(1)}) custom-call(s32[1]{0:T(128)} %bitcast.pair_ref, bf16[2,4096,256]{2,1,0:T(8,128)(2,1)} %bitcast.19), custom_call_target="tpu_custom_call" | custom-call | tf_op jit(solution)/shard_map/regroup/pallas_call | solution.py:55
  4.8 0.0 copy-start
  4.8 1.3 copy-done
  6.1 0.8 copy-done.4
  7.0 0.8 copy-done.6
  7.8 5.1 %all-to-all-start = ((bf16[4,2,512,256]{3,2,1,0:T(8,128)(2,1)}), bf16[4,2,512,256]{3,2,1,0:T(8,128)(2,1)S(1)}, u32[]{:S(2)}, u32[]{:S(2)}) async-start(bf16[4,2,512,256]{3,2,1,0:T(8,128)(2,1)} %copy-done), calls=%async_computation | async-start | bytes 4194304 | tf_op jit(solution)/shard_map/all_to_all | solution.py:261
  12.9 0.0 copy-done.1
  13.0 0.1 copy.19.refs_6_.refs_9_
  13.1 0.0 copy-start.8
  13.1 0.0 copy-start.9
  13.1 0.0 copy-start.2
  13.1 0.0 copy-start.3
  13.2 9.3 %copy.28 = bf16[2,1024,2,1024]{3,1,0,2:T(8,128)(2,1)} copy(bf16[2,1024,2,1024]{3,2,1,0:T(2,128)(2,1)} %param.7) | data formatting | bytes 16777216 | tf_op args[0]
  22.5 0.1 pad_add_fusion.refs_0_
  22.6 0.9 fusion
  23.5 14.0 %all-to-all-done.refs_4_ = bf16[4,2,512,256]{3,2,1,0:T(8,128)(2,1)S(1)} async-done(((bf16[4,2,512,256]{3,2,1,0:T(8,128)(2,1)}), bf16[4,2,512,256]{3,2,1,0:T(8,128)(2,1)S(1)}, u32[]{:S(2)}, u32[]{:S(2)}) %all-to-all-start) | async-done | bytes 2097184 | tf_op jit(solution)/shard_map/all_to_all | solution.py:261
  37.5 0.0 copy-done.3
  37.5 6.5 %ladder.2 = (bf16[512,1024]{1,0:T(8,128)(2,1)}, f32[1,1024]{1,0:T(1,128)S(1)}) custom-call(s32[2]{0:T(128)S(1)} %pad_add_fusion.refs_0_, s32[8]{0:T(128)S(1)} %copy-done.2, s32[8]{0:T(128)S(1)} %copy-done.3, f32[512]{0:T(512)S(1)} %copy-done.1, bf16[4,2,512,256]{3,2,1,0:T(8,128)(2,1)S(1)} %all-to-all-done.refs_4_, bf16[2,2,1024,1024]{3,2,1,0:T(8,128)(2,1)} %bitcast.17, ...), custom_call_target="tpu_custom_call" | custom-call | flops 2147483648 | bytes 7340032 | tf_op jit(solution)/shard_map/ladder/pallas_call | solution.py:170
  44.0 14.3 %all-to-all-start.1 = ((bf16[64,8,1024]{2,1,0:T(8,128)(2,1)}), bf16[64,8,1024]{2,1,0:T(8,128)(2,1)S(1)}, u32[]{:S(2)}, u32[]{:S(2)}) async-start(bf16[64,8,1024]{2,1,0:T(8,128)(2,1)} %bitcast.6), calls=%async_computation.1 | async-start | bytes 2097152 | tf_op jit(solution)/shard_map/all_to_all | solution.py:254
  58.4 0.0 copy-done.7
  58.4 0.4 collective-permute-start
  58.8 1.8 %collective-permute-start.1 = (bf16[2,512,256]{2,1,0:T(8,128)(2,1)S(1)}, bf16[2,512,256]{2,1,0:T(8,128)(2,1)S(1)}, u32[]{:S(2)}, u32[]{:S(2)}) collective-permute-start(bf16[2,512,256]{2,1,0:T(8,128)(2,1)S(1)} %copy-done.5), channel_id=1, source_target_pairs={{0,2},{1,3},{2,0},{3,1},{4,6},{5,7},{6,4},{7,5},{8,10},{9,11},{10,... | collective-permute-start | bytes 1572872 | tf_op jit(solution)/shard_map/ppermute | solution.py:250
  60.6 0.7 collective-permute-start.2
  61.3 12.1 %collective-permute-done.refs_5_ = bf16[2,512,256]{2,1,0:T(8,128)(2,1)S(1)} collective-permute-done((bf16[2,512,256]{2,1,0:T(8,128)(2,1)S(1)}, bf16[2,512,256]{2,1,0:T(8,128)(2,1)S(1)}, u32[]{:S(2)}, u32[]{:S(2)}) %collective-permute-start) | collective-permute-done | bytes 524320 | tf_op jit(solution)/shard_map/ppermute | solution.py:250
  73.3 10.1 %collective-permute-done.1.refs_6_ = bf16[2,512,256]{2,1,0:T(8,128)(2,1)S(1)} collective-permute-done((bf16[2,512,256]{2,1,0:T(8,128)(2,1)S(1)}, bf16[2,512,256]{2,1,0:T(8,128)(2,1)S(1)}, u32[]{:S(2)}, u32[]{:S(2)}) %collective-permute-start.1) | collective-permute-done | bytes 524320 | tf_op jit(solution)/shard_map/ppermute | solution.py:250
  83.4 0.9 collective-permute-done.2.refs_7_
  84.3 7.3 %ladder.3 = bf16[512,1152]{1,0:T(8,128)(2,1)} custom-call(s32[2]{0:T(128)S(1)} %pad_add_fusion.refs_0_, s32[8]{0:T(128)S(1)} %copy-done.2, s32[8]{0:T(128)S(1)} %copy-done.3, f32[512]{0:T(512)S(1)} %copy-done.1, bf16[2,512,256]{2,1,0:T(8,128)(2,1)S(1)} %get-tuple-element.21.refs_4_, bf16[2,512,256]{2,1,0:T(8,128)(2,1)S(1)} %collective-permute-done.refs_5_, ...), custom_call_target="tpu_custom_call" | custom-call | flops 2147483648 | bytes 7340032 | tf_op jit(solution)/shard_map/ladder/pallas_call | solution.py:170
  91.6 0.0 all-to-all-done.1
  91.6 11.5 %all-to-all-start.2 = ((bf16[64,8,1152]{2,1,0:T(8,128)(2,1)}), bf16[64,8,1152]{2,1,0:T(8,128)(2,1)S(1)}, u32[]{:S(2)}, u32[]{:S(2)}) async-start(bf16[64,8,1152]{2,1,0:T(8,128)(2,1)} %bitcast.8), calls=%async_computation.2 | async-start | bytes 2359296 | tf_op jit(solution)/shard_map/all_to_all | solution.py:254
  103.2 2.7 %place.2.before = bf16[2,1024,512]{2,1,0:T(8,128)(2,1)} custom-call(bf16[512,1024]{1,0:T(8,128)(2,1)S(1)} %bitcast.15), custom_call_target="tpu_custom_call" | custom-call | flops 536870912 | bytes 2097152 | tf_op jit(solution)/shard_map/place/pallas_call | solution.py:229
  105.8 28.7 %all-to-all-done.2 = bf16[64,8,1152]{2,1,0:T(8,128)(2,1)S(1)} async-done(((bf16[64,8,1152]{2,1,0:T(8,128)(2,1)}), bf16[64,8,1152]{2,1,0:T(8,128)(2,1)S(1)}, u32[]{:S(2)}, u32[]{:S(2)}) %all-to-all-start.2) | async-done | bytes 1179680 | tf_op jit(solution)/shard_map/all_to_all | solution.py:254
  134.5 2.8 %place.3 = (bf16[2,1024,512]{2,1,0:T(8,128)(2,1)}, f32[2,16]{1,0:T(2,128)}) custom-call(bf16[512,1152]{1,0:T(8,128)(2,1)S(1)} %bitcast.13, bf16[512,1152]{1,0:T(8,128)(2,1)S(1)} %bitcast.14, bf16[2,1024,512]{2,1,0:T(8,128)(2,1)} %place.2.before), custom_call_target="tpu_custom_call", output_to_operand_aliasing={{0}: (2, {})} | custom-call | flops 536870912 | bytes 2097152 | tf_op jit(solution)/shard_map/place/pallas_call | solution.py:234
  (11 shorter events, 0.0 us)
Async XLA Ops:
  4.8 1.3 copy-start
  6.1 0.8 copy-start.4
  7.0 0.8 copy-start.6
  7.8 5.1 %copy-start.1 = (f32[512]{0:T(512)S(1)}, f32[512]{0:T(512)}, u32[]{:S(2)}) copy-start(f32[512]{0:T(512)} %refs_3_.3) | copy-start | bytes 6148
  7.8 29.7 %all-to-all-start = ((bf16[4,2,512,256]{3,2,1,0:T(8,128)(2,1)}), bf16[4,2,512,256]{3,2,1,0:T(8,128)(2,1)S(1)}, u32[]{:S(2)}, u32[]{:S(2)}) async-start(bf16[4,2,512,256]{3,2,1,0:T(8,128)(2,1)} %copy-done), calls=%async_computation | async-start | bytes 4194304 | tf_op jit(solution)/shard_map/all_to_all | solution.py:261
  13.1 9.5 %copy-start.8 = (s32[2,1024,2]{1,2,0:T(2,128)S(1)}, s32[2,1024,2]{1,2,0:T(2,128)}, u32[]{:S(2)}) copy-start(s32[2,1024,2]{1,2,0:T(2,128)} %param.11) | copy-start | bytes 49156
  13.1 9.5 %copy-start.9 = (f32[100]{0:T(128)S(1)}, f32[100]{0:T(128)}, u32[]{:S(2)}) copy-start(f32[100]{0:T(128)} %param.12) | copy-start | bytes 1204
  13.1 24.4 %copy-start.2 = (s32[8]{0:T(128)S(1)}, s32[8]{0:T(128)}, u32[]{:S(2)}) copy-start(s32[8]{0:T(128)} %refs_1_.3) | copy-start | bytes 100
  13.1 24.4 %copy-start.3 = (s32[8]{0:T(128)S(1)}, s32[8]{0:T(128)}, u32[]{:S(2)}) copy-start(s32[8]{0:T(128)} %refs_2_.3) | copy-start | bytes 100
  44.0 14.4 %copy-start.7 = (bf16[2,512,256]{2,1,0:T(8,128)(2,1)S(1)}, bf16[2,512,256]{2,1,0:T(8,128)(2,1)}, u32[]{:S(2)}) copy-start(bf16[2,512,256]{2,1,0:T(8,128)(2,1)} %copy-done.6) | copy-start | bytes 1572868
  44.0 14.7 %copy-start.5 = (bf16[2,512,256]{2,1,0:T(8,128)(2,1)S(1)}, bf16[2,512,256]{2,1,0:T(8,128)(2,1)}, u32[]{:S(2)}) copy-start(bf16[2,512,256]{2,1,0:T(8,128)(2,1)} %copy-done.4) | copy-start | bytes 1572868
  44.0 47.6 %all-to-all-start.1 = ((bf16[64,8,1024]{2,1,0:T(8,128)(2,1)}), bf16[64,8,1024]{2,1,0:T(8,128)(2,1)S(1)}, u32[]{:S(2)}, u32[]{:S(2)}) async-start(bf16[64,8,1024]{2,1,0:T(8,128)(2,1)} %bitcast.6), calls=%async_computation.1 | async-start | bytes 2097152 | tf_op jit(solution)/shard_map/all_to_all | solution.py:254
  58.4 14.9 %collective-permute-start = (bf16[2,512,256]{2,1,0:T(8,128)(2,1)S(1)}, bf16[2,512,256]{2,1,0:T(8,128)(2,1)S(1)}, u32[]{:S(2)}, u32[]{:S(2)}) collective-permute-start(bf16[2,512,256]{2,1,0:T(8,128)(2,1)S(1)} %copy-done.7), channel_id=1, source_target_pairs={{0,1},{1,2},{2,3},{3,0},{4,5},{5,6},{6,7},{7,4},{8,9},{9,10},{10,1... | collective-permute-start | bytes 1572872 | tf_op jit(solution)/shard_map/ppermute | solution.py:250
  58.8 24.6 %collective-permute-start.1 = (bf16[2,512,256]{2,1,0:T(8,128)(2,1)S(1)}, bf16[2,512,256]{2,1,0:T(8,128)(2,1)S(1)}, u32[]{:S(2)}, u32[]{:S(2)}) collective-permute-start(bf16[2,512,256]{2,1,0:T(8,128)(2,1)S(1)} %copy-done.5), channel_id=1, source_target_pairs={{0,2},{1,3},{2,0},{3,1},{4,6},{5,7},{6,4},{7,5},{8,10},{9,11},{10,... | collective-permute-start | bytes 1572872 | tf_op jit(solution)/shard_map/ppermute | solution.py:250
  60.6 23.8 %collective-permute-start.2 = (bf16[2,512,256]{2,1,0:T(8,128)(2,1)S(1)}, bf16[2,512,256]{2,1,0:T(8,128)(2,1)S(1)}, u32[]{:S(2)}, u32[]{:S(2)}) collective-permute-start(bf16[2,512,256]{2,1,0:T(8,128)(2,1)S(1)} %get-tuple-element.24), channel_id=1, source_target_pairs={{0,3},{1,0},{2,1},{3,2},{4,7},{5,4},{6,5},{7,6},{8,11},{9,8},{10,9... | collective-permute-start | bytes 1572872 | tf_op jit(solution)/shard_map/ppermute | solution.py:250
  91.6 42.9 %all-to-all-start.2 = ((bf16[64,8,1152]{2,1,0:T(8,128)(2,1)}), bf16[64,8,1152]{2,1,0:T(8,128)(2,1)S(1)}, u32[]{:S(2)}, u32[]{:S(2)}) async-start(bf16[64,8,1152]{2,1,0:T(8,128)(2,1)} %bitcast.8), calls=%async_computation.2 | async-start | bytes 2359296 | tf_op jit(solution)/shard_map/all_to_all | solution.py:254

commit v3 on v2

v3 whole, which is shorter than its diff:
```python
import jax
import jax.numpy as jnp
from jax import lax
from jax.experimental import pallas as pl
from jax.experimental.pallas import tpu as pltpu
from jax.sharding import PartitionSpec as P

IRREPS = 8
NV = 512
BLK = 64
SLABS = 2
PCAP = 1024
KQ = 256
KS = 1024
VIRTS = 64
OWN = NV // VIRTS
MINE = PCAP // VIRTS
VMEM = 20 * 1024 * 1024
ABLK = 256
SUB = 32
RBLK = 256


def iota(shape, axis):
    return lax.broadcasted_iota(jnp.int32, shape, axis)


def regroup_kernel(pair_ref, x_ref, even, own, plus, far, minus, perm, held):
    rows = SUB * IRREPS

    @pl.when((pl.program_id(0) == 0) & (pl.program_id(1) == 0))
    def _():
        to, source = iota((rows, rows), 0), iota((rows, rows), 1)
        at = (to & (SUB - 1)) * IRREPS + (to >> 5)
        perm[...] = jnp.where(at == source, 1.0, 0.0).astype(jnp.bfloat16)

    for sub in range(ABLK // SUB):
        block = x_ref[0, sub * rows : (sub + 1) * rows, :]
        moved = jnp.dot(perm[...], block, preferred_element_type=jnp.float32).astype(jnp.bfloat16)
        at = slice(sub * SUB, (sub + 1) * SUB)
        for pair in range(4):
            even[pair, 0, at, :] = moved[(2 * pair) * SUB : (2 * pair + 1) * SUB]
            held[pair, at, :] = moved[(2 * pair + 1) * SUB : (2 * pair + 2) * SUB]
    me = pair_ref[0]
    own[0] = held[me]
    plus[0] = held[(me + 1) % 4]
    far[0] = held[(me + 2) % 4]
    minus[0] = held[(me + 3) % 4]


def regroup(pair_id, integrals):
    each = pltpu.HBM((SLABS, NV, KQ), jnp.bfloat16)
    spec = pl.BlockSpec((1, ABLK, KQ), lambda s, i, me: (s, i, 0))
    return pl.pallas_call(
        regroup_kernel,
        grid_spec=pltpu.PrefetchScalarGridSpec(
            num_scalar_prefetch=1,
            grid=(SLABS, NV // ABLK),
            in_specs=[pl.BlockSpec((1, ABLK * IRREPS, KQ), lambda s, i, me: (s, i, 0))],
            out_specs=[pl.BlockSpec((4, 1, ABLK, KQ), lambda s, i, me: (0, s, i, 0))] + [spec] * 4,
            scratch_shapes=[
                pltpu.VMEM((SUB * IRREPS, SUB * IRREPS), jnp.bfloat16),
                pltpu.VMEM((4, ABLK, KQ), jnp.bfloat16),
            ],
        ),
        out_shape=[pltpu.HBM((4, SLABS, NV, KQ), jnp.bfloat16)] + [each] * 4,
        compiler_params=pltpu.CompilerParams(vmem_limit_bytes=3 * VMEM),
        name="regroup",
    )(pair_id, integrals.reshape(SLABS, NV * IRREPS, KQ))


def ladder_kernel(parity, ids, virt_counts, pair_counts, eps, *refs):
    pieces, (amp, eps_a, occ, send, energy, held, stage, sems) = refs[:-8], refs[-8:]
    me, virt = ids[0], ids[1]
    h = 2 * me + parity
    mask = jnp.where((iota((1, KQ), 1) & (BLK - 1)) < virt_counts[h], 1.0, 0.0).astype(jnp.bfloat16)
    for slab in range(SLABS):
        if parity == 0:
            for source in range(4):
                to = slab * KS + source * KQ
                held[:, to : to + KQ] = pieces[0][source, slab] * mask
        else:
            for shift, piece in zip((0, 3, 2, 1), pieces):
                to = pl.multiple_of(slab * KS + ((me + shift) % 4) * KQ, KQ)
                held[:, pl.ds(to, KQ)] = piece[slab] * mask
    slot = iota((BLK, RBLK), 0)
    column = iota((BLK, RBLK), 1)
    copies = []
    for block in range(PCAP // RBLK):
        at = slice(block * RBLK, (block + 1) * RBLK)
        total = None
        for slab in range(SLABS):
            term = lax.dot_general(
                held[:, slab * KS : (slab + 1) * KS],
                amp[slab, at, :],
                (((1,), (1,)), ((), ())),
                preferred_element_type=jnp.float32,
            )
            total = term if total is None else total + term
        occ_row = occ[parity : parity + 1, at]
        live_row = block * RBLK + column < pair_counts[h]
        summed = jnp.zeros((1, RBLK), jnp.float32)
        for ha in range(IRREPS):
            rows = slice(ha * BLK, (ha + 1) * BLK)
            hb = jnp.bitwise_xor(h, ha)
            part = total[rows]
            denom = (eps_a[rows, :] + eps[hb * BLK + virt]) - occ_row
            live_a = jnp.where(virt < virt_counts[hb], virt_counts[ha], 0)
            ratio = jnp.where((slot < live_a) & live_row, part / denom, 0.0)
            summed = summed + jnp.sum(ratio * part, axis=0, keepdims=True)
            stage[block, rows, :] = ratio.astype(jnp.bfloat16)
        energy[:, at] = summed / (NV * BLK)
        copy = pltpu.make_async_copy(stage.at[block], send.at[:, pl.ds(block * RBLK, RBLK)], sems.at[block])
        copy.start()
        copies.append(copy)
    for copy in copies:
        copy.wait()


def ladder(parity, scalars, pieces, amp, eps_a, occ):
    vmem = pl.BlockSpec(memory_space=pltpu.VMEM)
    return pl.pallas_call(
        lambda *refs: ladder_kernel(parity, *refs),
        in_specs=[pl.BlockSpec(memory_space=pltpu.SMEM)] * 4 + [vmem] * (len(pieces) + 3),
        out_specs=[pl.BlockSpec(memory_space=pl.ANY), vmem],
        out_shape=[
            jax.ShapeDtypeStruct((NV, PCAP), jnp.bfloat16),
            jax.ShapeDtypeStruct((1, PCAP), jnp.float32),
        ],
        scratch_shapes=[
            pltpu.VMEM((NV, SLABS * KS), jnp.bfloat16),
            pltpu.VMEM((PCAP // RBLK, NV, RBLK), jnp.bfloat16),
            pltpu.SemaphoreType.DMA((PCAP // RBLK,)),
        ],
        compiler_params=pltpu.CompilerParams(vmem_limit_bytes=VMEM),
        cost_estimate=pl.CostEstimate(
            flops=2 * NV * PCAP * SLABS * KS, bytes_accessed=7 << 20, transcendentals=0
        ),
        name="ladder",
    )(*scalars, *pieces, amp, eps_a, occ)


def put(block, out, perm):
    @pl.when(pl.program_id(0) == 0)
    def _():
        source, to = iota((NV, NV), 0), iota((NV, NV), 1)
        at = (source & (OWN - 1)) * BLK + (source >> 3)
        perm[...] = jnp.where(at == to, 1.0, 0.0).astype(jnp.bfloat16)

    out[0] = lax.dot_general(
        block[...], perm[...], (((0,), (0,)), ((), ())), preferred_element_type=jnp.float32
    ).astype(jnp.bfloat16)


def place_even_kernel(block, out, perm):
    put(block, out, perm)


def place_odd_kernel(block, before, out, perm):
    put(block, out, perm)


def place(parity, block, before=None):
    in_specs = [pl.BlockSpec((NV, RBLK), lambda i: (0, i))]
    common = dict(
        grid=(PCAP // RBLK,),
        out_specs=pl.BlockSpec((1, RBLK, NV), lambda i: (parity, i, 0)),
        out_shape=jax.ShapeDtypeStruct((2, PCAP, NV), jnp.bfloat16),
        scratch_shapes=[pltpu.VMEM((NV, NV), jnp.bfloat16)],
        compiler_params=pltpu.CompilerParams(vmem_limit_bytes=VMEM),
        cost_estimate=pl.CostEstimate(flops=2 * NV * NV * PCAP, bytes_accessed=2 << 20, transcendentals=0),
        name="place",
    )
    if parity == 0:
        return pl.pallas_call(place_even_kernel, in_specs=in_specs, **common)(block)
    in_specs.append(pl.BlockSpec(memory_space=pl.ANY))
    return pl.pallas_call(
        place_odd_kernel, in_specs=in_specs, input_output_aliases={1: 0}, **common
    )(block, before)


def pick(ids, table):
    onehot = ids[..., None] == jnp.arange(table.shape[0], dtype=jnp.int32)
    return jnp.sum(jnp.where(onehot, table, 0), axis=-1)


def step(value, by):
    return lax.ppermute(value, "pair", [(i, (i + by) % 4) for i in range(4)])


def across(value):
    return lax.all_to_all(value, "virt", 0, 0, tiled=True)


def shards(amplitudes, integrals, virt_counts, pair_counts, pair_list, eps_occ, eps_virt):
    me = lax.axis_index("pair").astype(jnp.int32)
    virt = lax.axis_index("virt").astype(jnp.int32)
    even, own, plus, far, minus = regroup(me[None], integrals)
    even = lax.all_to_all(even, "pair", 0, 0, tiled=True)

    amp = [jnp.transpose(amplitudes[parity], (1, 0, 2)) for parity in range(2)]
    occ_terms = pick(pair_list, eps_occ)
    occ = occ_terms[:, :, 0] + occ_terms[:, :, 1]
    eps_a = eps_virt[:, None]
    scalars = (jnp.stack([me, virt]), virt_counts, pair_counts, eps_virt)

    even, plus, far, minus = lax.optimization_barrier((even, plus, far, minus))
    left, far, right = step(plus, 1), step(far, 2), step(minus, 3)
    send, energy0 = ladder(0, scalars, (even,), amp[0], eps_a, occ)
    first = across(send)
    send, energy1 = ladder(1, scalars, (own, left, far, right), amp[1], eps_a, occ)
    first, send = lax.optimization_barrier((first, send))
    second = across(send)
    energy = jnp.concatenate([energy0, energy1], axis=0)
    for bit in range(6):
        energy = energy + lax.ppermute(energy, "virt", [(i, i ^ (1 << bit)) for i in range(VIRTS)])
    energy = lax.dynamic_slice_in_dim(energy, virt * MINE, MINE, axis=1)
    out = place(0, first)
    return place(1, second, out), energy


def solution(mesh):
    placed = (
        P("pair", None, None, None),
        P(None, None, None, ("virt", "pair")),
        P(),
        P(),
        P("pair", None, None),
        P(),
        P(),
    )
    return jax.shard_map(
        shards,
        mesh=mesh,
        in_specs=placed,
        out_specs=(P("pair", None, "virt"), P("pair", "virt")),
        check_vma=False,
    )
```

time: 138 us -> 150 us (1.087)
  the two profiles are of different devices: /device:TPU:1 before, /device:TPU:6 now
where the time goes in v3:
time: 150 us
  waiting for transfers between devices  71.3 us (48%)
  starting transfers between devices  39.3 us (26%)
  Pallas kernels  19.4 us (13%)
  local copies, waits for them, and re-layouts  17.2 us (11%)
  other arithmetic  1.7 us (1%)
    ppermute x6, waiting for transfers between devices, shards(): lax.ppermute(energy, 'virt', [(i, i ^ 1 << bit) for i in range(VIRTS)])  37 us
    all_to_all x2, starting transfers between devices, across(): return lax.all_to_all(value, 'virt', 0, 0, tiled=True)  22.5 us
    ppermute x3, waiting for transfers between devices, step(): return lax.ppermute(value, 'pair', [(i, (i + by) % 4) for i in range(4)])  20.4 us
    all_to_all x1, waiting for transfers between devices, shards(): even = lax.all_to_all(even, 'pair', 0, 0, tiled=True)  13.9 us
    unnamed x16, local copies, waits for them, and re-layouts  9.07 us
    ppermute x6, starting transfers between devices, shards(): lax.ppermute(energy, 'virt', [(i, i ^ 1 << bit) for i in range(VIRTS)])  8.88 us
    pallas_call x2, Pallas kernels, ladder(): pl.pallas_call(lambda *refs: ladder_kernel(parity, *refs), in_specs=[pl.B...  8.39 us
    slice x1, local copies, waits for them, and re-layouts, shards(): amp = [jnp.transpose(amplitudes[parity], (1, 0, 2)) for parity in range(2)]  7.92 us
  transfers between devices with their start and end apart: 12, of which 9 were waited for; matrix products, arithmetic and copies ran while one was open for 11% of the time, Pallas kernels for 5%

profile of v3, /device:TPU:6, one launch (start us, length us, event | category | flops | bytes accessed | tf_op | source)
XLA Modules:
  0.0 149.6 jit_solution(7006326738239424025)
XLA Ops:
  0.6 5.7 %regroup.1 = (bf16[4,2,512,256]{3,2,1,0:T(8,128)(2,1)}, bf16[2,512,256]{2,1,0:T(8,128)(2,1)}, bf16[2,512,256]{2,1,0:T(8,128)(2,1)}, bf16[2,512,256]{2,1,0:T(8,128)(2,1)}, bf16[2,512,256]{2,1,0:T(8,128)(2,1)}) custom-call(s32[1]{0:T(128)} %bitcast.pair_ref, bf16[2,4096,256]{2,1,0:T(8,128)(2,1)} %bitcast.25), custom_call_target="tpu_custom_call" | custom-call | tf_op jit(solution)/shard_map/regroup/pallas_call | solution.py:54
  6.4 4.5 %all-to-all-start = ((bf16[4,2,512,256]{3,2,1,0:T(8,128)(2,1)}), bf16[4,2,512,256]{3,2,1,0:T(8,128)(2,1)S(1)}, u32[]{:S(2)}, u32[]{:S(2)}) async-start(bf16[4,2,512,256]{3,2,1,0:T(8,128)(2,1)} %get-tuple-element.17), calls=%async_computation | async-start | bytes 4194304 | tf_op jit(solution)/shard_map/all_to_all | solution.py:199
  10.8 7.9 %fusion.3 = (bf16[1,1024,2,1024]{3,2,1,0:T(2,128)(2,1)}, bf16[1,1024,2,1024]{3,2,1,0:T(2,128)(2,1)S(1)}) fusion(bf16[2,1024,2,1024]{3,2,1,0:T(2,128)(2,1)} %param.7), kind=kLoop, calls=%fused_computation.10 | loop fusion | bytes 16777216 | tf_op jit(solution)/shard_map/slice | solution.py:201
  18.8 3.3 %copy.35 = bf16[1,1024,2,1024]{3,1,2,0:T(8,128)(2,1)} copy(bf16[1,1024,2,1024]{3,2,1,0:T(2,128)(2,1)S(1)} %get-tuple-element.33) | data formatting | bytes 8388608
  22.3 0.9 fusion
  23.3 13.9 %all-to-all-done.refs_4_ = bf16[4,2,512,256]{3,2,1,0:T(8,128)(2,1)S(1)} async-done(((bf16[4,2,512,256]{3,2,1,0:T(8,128)(2,1)}), bf16[4,2,512,256]{3,2,1,0:T(8,128)(2,1)S(1)}, u32[]{:S(2)}, u32[]{:S(2)}) %all-to-all-start) | async-done | bytes 2097184 | tf_op jit(solution)/shard_map/all_to_all | solution.py:199
  37.2 2.2 %copy-done = bf16[1,1024,2,1024]{3,1,2,0:T(8,128)(2,1)S(1)} copy-done((bf16[1,1024,2,1024]{3,1,2,0:T(8,128)(2,1)S(1)}, bf16[1,1024,2,1024]{3,1,2,0:T(8,128)(2,1)}, u32[]{:S(2)}) %copy-start) | copy-done | bytes 4194328
  39.4 4.1 %ladder.2 = (bf16[512,1024]{1,0:T(8,128)(2,1)}, f32[1,1024]{1,0:T(1,128)S(1)}) custom-call(s32[2]{0:T(128)S(1)} %pad_add_fusion.refs_0_, s32[8]{0:T(128)S(1)} %copy-done.3, s32[8]{0:T(128)S(1)} %copy-done.4, f32[512]{0:T(512)S(1)} %copy-done.1, bf16[4,2,512,256]{3,2,1,0:T(8,128)(2,1)S(1)} %all-to-all-done.refs_4_, bf16[2,1024,1024]{2,1,0:T(8,128)(2,1)S(1)} %bitcast.23, ...), custom_call_target="tpu_custom_call" | custom-call | flops 2147483648 | bytes 7340032 | tf_op jit(solution)/shard_map/ladder/pallas_call | solution.py:122
  43.4 12.2 %all-to-all-start.1 = ((bf16[64,8,1024]{2,1,0:T(8,128)(2,1)}), bf16[64,8,1024]{2,1,0:T(8,128)(2,1)S(1)}, u32[]{:S(2)}, u32[]{:S(2)}) async-start(bf16[64,8,1024]{2,1,0:T(8,128)(2,1)} %bitcast.7), calls=%async_computation.1 | async-start | bytes 2097152 | tf_op jit(solution)/shard_map/all_to_all | solution.py:192
  55.6 0.6 collective-permute-start
  56.2 2.1 %collective-permute-start.1 = (bf16[2,512,256]{2,1,0:T(8,128)(2,1)}, bf16[2,512,256]{2,1,0:T(8,128)(2,1)S(1)}, u32[]{:S(2)}, u32[]{:S(2)}) collective-permute-start(bf16[2,512,256]{2,1,0:T(8,128)(2,1)} %get-tuple-element.25), channel_id=1, source_target_pairs={{0,2},{1,3},{2,0},{3,1},{4,6},{5,7},{6,4},{7,5},{8,10},{9,11},{10,... | collective-permute-start | bytes 1572872 | tf_op jit(solution)/shard_map/ppermute | solution.py:188
  58.3 0.7 collective-permute-start.2
  59.0 3.5 %copy.34 = bf16[1,1024,2,1024]{3,1,2,0:T(8,128)(2,1)S(1)} copy(bf16[1,1024,2,1024]{3,2,1,0:T(2,128)(2,1)} %get-tuple-element.32) | data formatting | bytes 8388608
  62.6 19.7 %collective-permute-done.refs_5_ = bf16[2,512,256]{2,1,0:T(8,128)(2,1)S(1)} collective-permute-done((bf16[2,512,256]{2,1,0:T(8,128)(2,1)}, bf16[2,512,256]{2,1,0:T(8,128)(2,1)S(1)}, u32[]{:S(2)}, u32[]{:S(2)}) %collective-permute-start) | collective-permute-done | bytes 524320 | tf_op jit(solution)/shard_map/ppermute | solution.py:188
  82.3 0.6 collective-permute-done.2.refs_7_
  82.9 4.3 %ladder.3 = (bf16[512,1024]{1,0:T(8,128)(2,1)}, f32[1,1024]{1,0:T(1,128)S(1)}) custom-call(s32[2]{0:T(128)S(1)} %pad_add_fusion.refs_0_, s32[8]{0:T(128)S(1)} %copy-done.3, s32[8]{0:T(128)S(1)} %copy-done.4, f32[512]{0:T(512)S(1)} %copy-done.1, bf16[2,512,256]{2,1,0:T(8,128)(2,1)S(1)} %copy-done.2, bf16[2,512,256]{2,1,0:T(8,128)(2,1)S(1)} %collective-permute-done.refs_5_, ...), custom_call_target="tpu_custom_call" | custom-call | flops 2147483648 | bytes 7340032 | tf_op jit(solution)/shard_map/ladder/pallas_call | solution.py:122
  87.3 10.3 %all-to-all-start.2 = ((bf16[64,8,1024]{2,1,0:T(8,128)(2,1)}), bf16[64,8,1024]{2,1,0:T(8,128)(2,1)S(1)}, u32[]{:S(2)}, u32[]{:S(2)}) async-start(bf16[64,8,1024]{2,1,0:T(8,128)(2,1)} %bitcast.11), calls=%async_computation.2 | async-start | bytes 2097152 | tf_op jit(solution)/shard_map/all_to_all | solution.py:192
  97.7 0.2 collective-permute-start.3
  97.9 1.0 collective-permute-done.3
  98.9 1.6 %collective-permute-start.4 = (f32[2,1024]{1,0:T(2,128)S(1)}, f32[2,1024]{1,0:T(2,128)S(1)}, u32[]{:S(2)}, u32[]{:S(2)}) collective-permute-start(f32[2,1024]{1,0:T(2,128)S(1)} %fusion.2), channel_id=1, source_target_pairs={{0,8},{4,12},{8,0},{12,4},{16,24},{20,28},{24,16},{28,20},{32,40},... | collective-permute-start | bytes 24584 | tf_op jit(solution)/shard_map/ppermute | solution.py:216
  100.5 22.1 %collective-permute-done.4 = f32[2,1024]{1,0:T(2,128)S(1)} collective-permute-done((f32[2,1024]{1,0:T(2,128)S(1)}, f32[2,1024]{1,0:T(2,128)S(1)}, u32[]{:S(2)}, u32[]{:S(2)}) %collective-permute-start.4) | collective-permute-done | bytes 8224 | tf_op jit(solution)/shard_map/ppermute | solution.py:216
  122.6 0.6 collective-permute-start.5
  123.2 4.1 %collective-permute-done.5 = f32[2,1024]{1,0:T(2,128)S(1)} collective-permute-done((f32[2,1024]{1,0:T(2,128)S(1)}, f32[2,1024]{1,0:T(2,128)S(1)}, u32[]{:S(2)}, u32[]{:S(2)}) %collective-permute-start.5) | collective-permute-done | bytes 8224 | tf_op jit(solution)/shard_map/ppermute | solution.py:216
  127.3 4.5 %collective-permute-start.6 = (f32[2,1024]{1,0:T(2,128)S(1)}, f32[2,1024]{1,0:T(2,128)S(1)}, u32[]{:S(2)}, u32[]{:S(2)}) collective-permute-start(f32[2,1024]{1,0:T(2,128)S(1)} %add.30), channel_id=1, source_target_pairs={{0,32},{4,36},{8,40},{12,44},{16,48},{20,52},{24,56},{28,60},{32,0... | collective-permute-start | bytes 24584 | tf_op jit(solution)/shard_map/ppermute | solution.py:216
  131.8 3.0 %collective-permute-done.6 = f32[2,1024]{1,0:T(2,128)S(1)} collective-permute-done((f32[2,1024]{1,0:T(2,128)S(1)}, f32[2,1024]{1,0:T(2,128)S(1)}, u32[]{:S(2)}, u32[]{:S(2)}) %collective-permute-start.6) | collective-permute-done | bytes 8224 | tf_op jit(solution)/shard_map/ppermute | solution.py:216
  134.8 0.7 collective-permute-start.7
  135.6 2.9 %collective-permute-done.7 = f32[2,1024]{1,0:T(2,128)S(1)} collective-permute-done((f32[2,1024]{1,0:T(2,128)S(1)}, f32[2,1024]{1,0:T(2,128)S(1)}, u32[]{:S(2)}, u32[]{:S(2)}) %collective-permute-start.7) | collective-permute-done | bytes 8224 | tf_op jit(solution)/shard_map/ppermute | solution.py:216
  138.5 1.2 collective-permute-start.8
  139.7 3.9 %collective-permute-done.8 = f32[2,1024]{1,0:T(2,128)S(1)} collective-permute-done((f32[2,1024]{1,0:T(2,128)S(1)}, f32[2,1024]{1,0:T(2,128)S(1)}, u32[]{:S(2)}, u32[]{:S(2)}) %collective-permute-start.8) | collective-permute-done | bytes 8224 | tf_op jit(solution)/shard_map/ppermute | solution.py:216
  143.6 0.6 dynamic-slice_add_fusion
  144.3 2.6 %place.2.before = bf16[2,1024,512]{2,1,0:T(8,128)(2,1)} custom-call(bf16[512,1024]{1,0:T(8,128)(2,1)S(1)} %bitcast.20), custom_call_target="tpu_custom_call" | custom-call | flops 536870912 | bytes 2097152 | tf_op jit(solution)/shard_map/place/pallas_call | solution.py:175
  146.9 2.6 %place.3 = bf16[2,1024,512]{2,1,0:T(8,128)(2,1)} custom-call(bf16[512,1024]{1,0:T(8,128)(2,1)S(1)} %bitcast.21, bf16[2,1024,512]{2,1,0:T(8,128)(2,1)} %place.2.before), custom_call_target="tpu_custom_call", output_to_operand_aliasing={{}: (1, {})} | custom-call | flops 536870912 | bytes 2097152 | tf_op jit(solution)/shard_map/place/pallas_call | solution.py:177
  (26 shorter events, 0.3 us)
Async XLA Ops:
  6.4 30.8 %all-to-all-start = ((bf16[4,2,512,256]{3,2,1,0:T(8,128)(2,1)}), bf16[4,2,512,256]{3,2,1,0:T(8,128)(2,1)S(1)}, u32[]{:S(2)}, u32[]{:S(2)}) async-start(bf16[4,2,512,256]{3,2,1,0:T(8,128)(2,1)} %get-tuple-element.17), calls=%async_computation | async-start | bytes 4194304 | tf_op jit(solution)/shard_map/all_to_all | solution.py:199
  18.8 3.4 %copy-start.1 = (f32[512]{0:T(512)S(1)}, f32[512]{0:T(512)}, u32[]{:S(2)}) copy-start(f32[512]{0:T(512)} %refs_3_.3) | copy-start | bytes 6148
  18.8 3.6 %copy-start.5 = (s32[2,1024,2]{1,2,0:T(2,128)S(1)}, s32[2,1024,2]{1,2,0:T(2,128)}, u32[]{:S(2)}) copy-start(s32[2,1024,2]{1,2,0:T(2,128)} %param.11) | copy-start | bytes 49156
  18.8 3.6 %copy-start.6 = (f32[100]{0:T(128)S(1)}, f32[100]{0:T(128)}, u32[]{:S(2)}) copy-start(f32[100]{0:T(128)} %param.12) | copy-start | bytes 1204
  18.8 18.4 %copy-start.3 = (s32[8]{0:T(128)S(1)}, s32[8]{0:T(128)}, u32[]{:S(2)}) copy-start(s32[8]{0:T(128)} %refs_1_.3) | copy-start | bytes 100
  18.8 18.4 %copy-start.4 = (s32[8]{0:T(128)S(1)}, s32[8]{0:T(128)}, u32[]{:S(2)}) copy-start(s32[8]{0:T(128)} %refs_2_.3) | copy-start | bytes 100
  37.2 2.2 %copy-start = (bf16[1,1024,2,1024]{3,1,2,0:T(8,128)(2,1)S(1)}, bf16[1,1024,2,1024]{3,1,2,0:T(8,128)(2,1)}, u32[]{:S(2)}) copy-start(bf16[1,1024,2,1024]{3,1,2,0:T(8,128)(2,1)} %copy.35) | copy-start | bytes 12582916
  43.4 43.9 %all-to-all-start.1 = ((bf16[64,8,1024]{2,1,0:T(8,128)(2,1)}), bf16[64,8,1024]{2,1,0:T(8,128)(2,1)S(1)}, u32[]{:S(2)}, u32[]{:S(2)}) async-start(bf16[64,8,1024]{2,1,0:T(8,128)(2,1)} %bitcast.7), calls=%async_computation.1 | async-start | bytes 2097152 | tf_op jit(solution)/shard_map/all_to_all | solution.py:192
  55.6 26.7 %collective-permute-start = (bf16[2,512,256]{2,1,0:T(8,128)(2,1)}, bf16[2,512,256]{2,1,0:T(8,128)(2,1)S(1)}, u32[]{:S(2)}, u32[]{:S(2)}) collective-permute-start(bf16[2,512,256]{2,1,0:T(8,128)(2,1)} %get-tuple-element.24), channel_id=1, source_target_pairs={{0,1},{1,2},{2,3},{3,0},{4,5},{5,6},{6,7},{7,4},{8,9},{9,10},{10,1... | collective-permute-start | bytes 1572872 | tf_op jit(solution)/shard_map/ppermute | solution.py:188
  56.2 26.1 %collective-permute-start.1 = (bf16[2,512,256]{2,1,0:T(8,128)(2,1)}, bf16[2,512,256]{2,1,0:T(8,128)(2,1)S(1)}, u32[]{:S(2)}, u32[]{:S(2)}) collective-permute-start(bf16[2,512,256]{2,1,0:T(8,128)(2,1)} %get-tuple-element.25), channel_id=1, source_target_pairs={{0,2},{1,3},{2,0},{3,1},{4,6},{5,7},{6,4},{7,5},{8,10},{9,11},{10,... | collective-permute-start | bytes 1572872 | tf_op jit(solution)/shard_map/ppermute | solution.py:188
  58.3 24.6 %collective-permute-start.2 = (bf16[2,512,256]{2,1,0:T(8,128)(2,1)}, bf16[2,512,256]{2,1,0:T(8,128)(2,1)S(1)}, u32[]{:S(2)}, u32[]{:S(2)}) collective-permute-start(bf16[2,512,256]{2,1,0:T(8,128)(2,1)} %get-tuple-element.26), channel_id=1, source_target_pairs={{0,3},{1,0},{2,1},{3,2},{4,7},{5,4},{6,5},{7,6},{8,11},{9,8},{10,9... | collective-permute-start | bytes 1572872 | tf_op jit(solution)/shard_map/ppermute | solution.py:188
  59.0 23.9 %copy-start.2 = (bf16[2,512,256]{2,1,0:T(8,128)(2,1)S(1)}, bf16[2,512,256]{2,1,0:T(8,128)(2,1)}, u32[]{:S(2)}) copy-start(bf16[2,512,256]{2,1,0:T(8,128)(2,1)} %get-tuple-element.23.refs_4_) | copy-start | bytes 1572868
  87.3 59.6 %all-to-all-start.2 = ((bf16[64,8,1024]{2,1,0:T(8,128)(2,1)}), bf16[64,8,1024]{2,1,0:T(8,128)(2,1)S(1)}, u32[]{:S(2)}, u32[]{:S(2)}) async-start(bf16[64,8,1024]{2,1,0:T(8,128)(2,1)} %bitcast.11), calls=%async_computation.2 | async-start | bytes 2097152 | tf_op jit(solution)/shard_map/all_to_all | solution.py:192
  97.7 1.3 collective-permute-start.3
  98.9 23.7 %collective-permute-start.4 = (f32[2,1024]{1,0:T(2,128)S(1)}, f32[2,1024]{1,0:T(2,128)S(1)}, u32[]{:S(2)}, u32[]{:S(2)}) collective-permute-start(f32[2,1024]{1,0:T(2,128)S(1)} %fusion.2), channel_id=1, source_target_pairs={{0,8},{4,12},{8,0},{12,4},{16,24},{20,28},{24,16},{28,20},{32,40},... | collective-permute-start | bytes 24584 | tf_op jit(solution)/shard_map/ppermute | solution.py:216
  122.6 4.6 %collective-permute-start.5 = (f32[2,1024]{1,0:T(2,128)S(1)}, f32[2,1024]{1,0:T(2,128)S(1)}, u32[]{:S(2)}, u32[]{:S(2)}) collective-permute-start(f32[2,1024]{1,0:T(2,128)S(1)} %fusion.5), channel_id=1, source_target_pairs={{0,16},{4,20},{8,24},{12,28},{16,0},{20,4},{24,8},{28,12},{32,48},... | collective-permute-start | bytes 24584 | tf_op jit(solution)/shard_map/ppermute | solution.py:216
  127.3 7.6 %collective-permute-start.6 = (f32[2,1024]{1,0:T(2,128)S(1)}, f32[2,1024]{1,0:T(2,128)S(1)}, u32[]{:S(2)}, u32[]{:S(2)}) collective-permute-start(f32[2,1024]{1,0:T(2,128)S(1)} %add.30), channel_id=1, source_target_pairs={{0,32},{4,36},{8,40},{12,44},{16,48},{20,52},{24,56},{28,60},{32,0... | collective-permute-start | bytes 24584 | tf_op jit(solution)/shard_map/ppermute | solution.py:216
  134.8 3.7 %collective-permute-start.7 = (f32[2,1024]{1,0:T(2,128)S(1)}, f32[2,1024]{1,0:T(2,128)S(1)}, u32[]{:S(2)}, u32[]{:S(2)}) collective-permute-start(f32[2,1024]{1,0:T(2,128)S(1)} %add.31), channel_id=1, source_target_pairs={{0,64},{4,68},{8,72},{12,76},{16,80},{20,84},{24,88},{28,92},{32,9... | collective-permute-start | bytes 24584 | tf_op jit(solution)/shard_map/ppermute | solution.py:216
  138.5 5.2 %collective-permute-start.8 = (f32[2,1024]{1,0:T(2,128)S(1)}, f32[2,1024]{1,0:T(2,128)S(1)}, u32[]{:S(2)}, u32[]{:S(2)}) collective-permute-start(f32[2,1024]{1,0:T(2,128)S(1)} %add.32), channel_id=1, source_target_pairs={{0,128},{4,132},{8,136},{12,140},{16,144},{20,148},{24,152},{28,15... | collective-permute-start | bytes 24584 | tf_op jit(solution)/shard_map/ppermute | solution.py:216

commit v4 on v3

--- a/solution.py
+++ b/solution.py
@@ -19,6 +19,7 @@
 ABLK = 256
 SUB = 32
 RBLK = 256
+EXTRA = 128
 
 
 def iota(shape, axis):
@@ -70,7 +71,10 @@
 
 
 def ladder_kernel(parity, ids, virt_counts, pair_counts, eps, *refs):
-    pieces, (amp, eps_a, occ, send, energy, held, stage, sems) = refs[:-8], refs[-8:]
+    if parity == 0:
+        pieces, (amp, eps_a, occ, send, energy, held, stage, sems) = refs[:-8], refs[-8:]
+    else:
+        pieces, (amp, eps_a, occ, energy0, send, held, stage, sems, energy, extra) = refs[:-10], refs[-10:]
     me, virt = ids[0], ids[1]
     h = 2 * me + parity
     mask = jnp.where((iota((1, KQ), 1) & (BLK - 1)) < virt_counts[h], 1.0, 0.0).astype(jnp.bfloat16)
@@ -113,31 +117,49 @@
         copy = pltpu.make_async_copy(stage.at[block], send.at[:, pl.ds(block * RBLK, RBLK)], sems.at[block])
         copy.start()
         copies.append(copy)
+    if parity == 1:
+        value = jnp.concatenate([energy0[...], energy[...]], axis=0)
+        high = value.astype(jnp.bfloat16).astype(jnp.float32)
+        rest = value - high
+        middle = rest.astype(jnp.bfloat16).astype(jnp.float32)
+        low = rest - middle
+        terms = jnp.concatenate([high, middle, low, jnp.zeros((2, PCAP), jnp.float32)], axis=0)
+        spread = jnp.broadcast_to(terms[None], (VIRTS, OWN, PCAP)).reshape(NV, PCAP)
+        owner = (iota((NV, PCAP), 1) // MINE) == (iota((NV, PCAP), 0) // OWN)
+        spread = jnp.where(owner, spread, 0.0).astype(jnp.bfloat16)
+        lane = (iota((PCAP, EXTRA), 0) & (MINE - 1)) == iota((PCAP, EXTRA), 1)
+        select = jnp.where(lane, 1.0, 0.0).astype(jnp.bfloat16)
+        extra[...] = jnp.dot(spread, select, preferred_element_type=jnp.float32).astype(jnp.bfloat16)
+        copy = pltpu.make_async_copy(extra, send.at[:, pl.ds(PCAP, EXTRA)], sems.at[PCAP // RBLK])
+        copy.start()
+        copies.append(copy)
     for copy in copies:
         copy.wait()
 
 
-def ladder(parity, scalars, pieces, amp, eps_a, occ):
+def ladder(parity, scalars, pieces, amp, eps_a, occ, *energy0):
     vmem = pl.BlockSpec(memory_space=pltpu.VMEM)
+    columns = PCAP if parity == 0 else PCAP + EXTRA
+    row = jax.ShapeDtypeStruct((1, PCAP), jnp.float32)
+    scratch = [
+        pltpu.VMEM((NV, SLABS * KS), jnp.bfloat16),
+        pltpu.VMEM((PCAP // RBLK, NV, RBLK), jnp.bfloat16),
+        pltpu.SemaphoreType.DMA((PCAP // RBLK + 1,)),
+    ]
+    if parity == 1:
+        scratch += [pltpu.VMEM((1, PCAP), jnp.float32), pltpu.VMEM((NV, EXTRA), jnp.bfloat16)]
     return pl.pallas_call(
         lambda *refs: ladder_kernel(parity, *refs),
-        in_specs=[pl.BlockSpec(memory_space=pltpu.SMEM)] * 4 + [vmem] * (len(pieces) + 3),
-        out_specs=[pl.BlockSpec(memory_space=pl.ANY), vmem],
-        out_shape=[
-            jax.ShapeDtypeStruct((NV, PCAP), jnp.bfloat16),
-            jax.ShapeDtypeStruct((1, PCAP), jnp.float32),
-        ],
-        scratch_shapes=[
-            pltpu.VMEM((NV, SLABS * KS), jnp.bfloat16),
-            pltpu.VMEM((PCAP // RBLK, NV, RBLK), jnp.bfloat16),
-            pltpu.SemaphoreType.DMA((PCAP // RBLK,)),
-        ],
+        in_specs=[pl.BlockSpec(memory_space=pltpu.SMEM)] * 4 + [vmem] * (len(pieces) + 3 + len(energy0)),
+        out_specs=[pl.BlockSpec(memory_space=pl.ANY)] + [vmem] * (1 - parity),
+        out_shape=[jax.ShapeDtypeStruct((NV, columns), jnp.bfloat16)] + [row] * (1 - parity),
+        scratch_shapes=scratch,
         compiler_params=pltpu.CompilerParams(vmem_limit_bytes=VMEM),
         cost_estimate=pl.CostEstimate(
             flops=2 * NV * PCAP * SLABS * KS, bytes_accessed=7 << 20, transcendentals=0
         ),
         name="ladder",
-    )(*scalars, *pieces, amp, eps_a, occ)
+    )(*scalars, *pieces, amp, eps_a, occ, *energy0)
 
 
 def put(block, out, perm):
@@ -156,27 +178,44 @@
     put(block, out, perm)
 
 
-def place_odd_kernel(block, before, out, perm):
+def place_odd_kernel(block, extra, before, out, energy, perm):
     put(block, out, perm)
+
+    @pl.when(pl.program_id(0) == 0)
+    def _():
+        values = extra[...].astype(jnp.float32)
+        kind = iota((NV, EXTRA), 0) & (OWN - 1)
+        for parity in range(2):
+            mine = (kind < 6) & ((kind & 1) == parity)
+            summed = jnp.sum(jnp.where(mine, values, 0.0), axis=0, keepdims=True)
+            energy[parity : parity + 1, :] = summed[:, :MINE]
 
 
 def place(parity, block, before=None):
     in_specs = [pl.BlockSpec((NV, RBLK), lambda i: (0, i))]
+    out_spec = pl.BlockSpec((1, RBLK, NV), lambda i: (parity, i, 0))
+    out = jax.ShapeDtypeStruct((2, PCAP, NV), jnp.bfloat16)
     common = dict(
         grid=(PCAP // RBLK,),
-        out_specs=pl.BlockSpec((1, RBLK, NV), lambda i: (parity, i, 0)),
-        out_shape=jax.ShapeDtypeStruct((2, PCAP, NV), jnp.bfloat16),
         scratch_shapes=[pltpu.VMEM((NV, NV), jnp.bfloat16)],
         compiler_params=pltpu.CompilerParams(vmem_limit_bytes=VMEM),
         cost_estimate=pl.CostEstimate(flops=2 * NV * NV * PCAP, bytes_accessed=2 << 20, transcendentals=0),
         name="place",
     )
     if parity == 0:
-        return pl.pallas_call(place_even_kernel, in_specs=in_specs, **common)(block)
-    in_specs.append(pl.BlockSpec(memory_space=pl.ANY))
+        return pl.pallas_call(place_even_kernel, in_specs=in_specs, out_specs=out_spec, out_shape=out, **common)(block)
+    in_specs += [
+        pl.BlockSpec((NV, EXTRA), lambda i: (0, PCAP // EXTRA)),
+        pl.BlockSpec(memory_space=pl.ANY),
+    ]
     return pl.pallas_call(
-        place_odd_kernel, in_specs=in_specs, input_output_aliases={1: 0}, **common
-    )(block, before)
+        place_odd_kernel,
+        in_specs=in_specs,
+        out_specs=[out_spec, pl.BlockSpec((2, MINE), lambda i: (0, 0))],
+        out_shape=[out, jax.ShapeDtypeStruct((2, MINE), jnp.float32)],
+        input_output_aliases={2: 0},
+        **common,
+    )(block, block, before)
 
 
 def pick(ids, table):
@@ -208,15 +247,11 @@
     left, far, right = step(plus, 1), step(far, 2), step(minus, 3)
     send, energy0 = ladder(0, scalars, (even,), amp[0], eps_a, occ)
     first = across(send)
-    send, energy1 = ladder(1, scalars, (own, left, far, right), amp[1], eps_a, occ)
+    (send,) = ladder(1, scalars, (own, left, far, right), amp[1], eps_a, occ, energy0)
     first, send = lax.optimization_barrier((first, send))
     second = across(send)
-    energy = jnp.concatenate([energy0, energy1], axis=0)
-    for bit in range(6):
-        energy = energy + lax.ppermute(energy, "virt", [(i, i ^ (1 << bit)) for i in range(VIRTS)])
-    energy = lax.dynamic_slice_in_dim(energy, virt * MINE, MINE, axis=1)
     out = place(0, first)
-    return place(1, second, out), energy
+    return tuple(place(1, second, out))
 
 
 def solution(mesh):

time: 150 us -> 134 us (0.89)
  the two profiles are of different devices: /device:TPU:6 before, /device:TPU:1 now
where the time goes in v4:
time: 134 us; the launch traced here: 133 us
  waiting for transfers between devices  60.1 us (45%)
  starting transfers between devices  33.9 us (25%)
  Pallas kernels  20.2 us (15%)
  local copies, waits for them, and re-layouts  17.2 us (13%)
    all_to_all x2, waiting for transfers between devices, across(): return lax.all_to_all(value, 'virt', 0, 0, tiled=True)  28.7 us
    all_to_all x2, starting transfers between devices, across(): return lax.all_to_all(value, 'virt', 0, 0, tiled=True)  25.9 us
    ppermute x3, waiting for transfers between devices, step(): return lax.ppermute(value, 'pair', [(i, (i + by) % 4) for i in range(4)])  19.3 us
    all_to_all x1, waiting for transfers between devices, shards(): even = lax.all_to_all(even, 'pair', 0, 0, tiled=True)  12.1 us
    unnamed x20, local copies, waits for them, and re-layouts  9.08 us
    pallas_call x2, Pallas kernels, ladder(): pl.pallas_call(lambda *refs: ladder_kernel(parity, *refs), in_specs=[pl.B...  9 us
    slice x1, local copies, waits for them, and re-layouts, shards(): amp = [jnp.transpose(amplitudes[parity], (1, 0, 2)) for parity in range(2)]  7.93 us
    pallas_call x1, Pallas kernels, regroup(): pl.pallas_call(regroup_kernel, grid_spec=pltpu.PrefetchScalarGridSpec(num...  5.72 us
  transfers between devices with their start and end apart: 6, of which 5 were waited for; matrix products, arithmetic and copies ran while one was open for 12% of the time, Pallas kernels for 6%

profile of v4, /device:TPU:1, one launch (start us, length us, event | category | flops | bytes accessed | tf_op | source)
XLA Modules:
  0.0 133.2 jit_solution(5808407160129537309)
XLA Ops:
  0.6 5.7 %regroup.1 = (bf16[4,2,512,256]{3,2,1,0:T(8,128)(2,1)}, bf16[2,512,256]{2,1,0:T(8,128)(2,1)}, bf16[2,512,256]{2,1,0:T(8,128)(2,1)}, bf16[2,512,256]{2,1,0:T(8,128)(2,1)}, bf16[2,512,256]{2,1,0:T(8,128)(2,1)}) custom-call(s32[1]{0:T(128)} %bitcast.pair_ref, bf16[2,4096,256]{2,1,0:T(8,128)(2,1)} %bitcast.26), custom_call_target="tpu_custom_call" | custom-call | tf_op jit(solution)/shard_map/regroup/pallas_call | solution.py:55
  6.4 5.0 %all-to-all-start = ((bf16[4,2,512,256]{3,2,1,0:T(8,128)(2,1)}), bf16[4,2,512,256]{3,2,1,0:T(8,128)(2,1)S(1)}, u32[]{:S(2)}, u32[]{:S(2)}) async-start(bf16[4,2,512,256]{3,2,1,0:T(8,128)(2,1)} %get-tuple-element.15), calls=%async_computation | async-start | bytes 4194304 | tf_op jit(solution)/shard_map/all_to_all | solution.py:238
  11.4 7.9 %fusion.2 = (bf16[1,1024,2,1024]{3,2,1,0:T(2,128)(2,1)}, bf16[1,1024,2,1024]{3,2,1,0:T(2,128)(2,1)S(1)}) fusion(bf16[2,1024,2,1024]{3,2,1,0:T(2,128)(2,1)} %param.7), kind=kLoop, calls=%fused_computation.7 | loop fusion | bytes 16777216 | tf_op jit(solution)/shard_map/slice | solution.py:240
  19.3 0.0 copy-start.6
  19.3 0.0 copy-start.3
  19.3 0.0 copy-start.4
  19.3 3.3 %copy.35 = bf16[1,1024,2,1024]{3,1,2,0:T(8,128)(2,1)} copy(bf16[1,1024,2,1024]{3,2,1,0:T(2,128)(2,1)S(1)} %get-tuple-element.29) | data formatting | bytes 8388608
  22.6 0.0 copy-done.1
  22.6 0.1 copy.21.refs_6_.refs_9_
  22.8 0.1 pad_add_fusion.refs_0_
  22.9 0.0 copy-done.5
  22.9 0.0 copy-done.6
  22.9 0.9 fusion
  23.8 12.1 %all-to-all-done.refs_4_ = bf16[4,2,512,256]{3,2,1,0:T(8,128)(2,1)S(1)} async-done(((bf16[4,2,512,256]{3,2,1,0:T(8,128)(2,1)}), bf16[4,2,512,256]{3,2,1,0:T(8,128)(2,1)S(1)}, u32[]{:S(2)}, u32[]{:S(2)}) %all-to-all-start) | async-done | bytes 2097184 | tf_op jit(solution)/shard_map/all_to_all | solution.py:238
  35.9 0.0 copy-done.4
  35.9 2.2 %copy-done = bf16[1,1024,2,1024]{3,1,2,0:T(8,128)(2,1)S(1)} copy-done((bf16[1,1024,2,1024]{3,1,2,0:T(8,128)(2,1)S(1)}, bf16[1,1024,2,1024]{3,1,2,0:T(8,128)(2,1)}, u32[]{:S(2)}) %copy-start) | copy-done | bytes 4194328
  38.1 4.1 %ladder.2 = (bf16[512,1024]{1,0:T(8,128)(2,1)}, f32[1,1024]{1,0:T(1,128)S(1)}) custom-call(s32[2]{0:T(128)S(1)} %pad_add_fusion.refs_0_, s32[8]{0:T(128)S(1)} %copy-done.3, s32[8]{0:T(128)S(1)} %copy-done.4, f32[512]{0:T(512)S(1)} %copy-done.1, bf16[4,2,512,256]{3,2,1,0:T(8,128)(2,1)S(1)} %all-to-all-done.refs_4_, bf16[2,1024,1024]{2,1,0:T(8,128)(2,1)S(1)} %bitcast.24, ...), custom_call_target="tpu_custom_call" | custom-call | flops 2147483648 | bytes 7340032 | tf_op jit(solution)/shard_map/ladder/pallas_call | solution.py:151
  42.2 14.4 %all-to-all-start.1 = ((bf16[64,8,1024]{2,1,0:T(8,128)(2,1)}), bf16[64,8,1024]{2,1,0:T(8,128)(2,1)S(1)}, u32[]{:S(2)}, u32[]{:S(2)}) async-start(bf16[64,8,1024]{2,1,0:T(8,128)(2,1)} %bitcast.7), calls=%async_computation.1 | async-start | bytes 2097152 | tf_op jit(solution)/shard_map/all_to_all | solution.py:231
  56.6 0.4 collective-permute-start
  56.9 1.8 %collective-permute-start.1 = (bf16[2,512,256]{2,1,0:T(8,128)(2,1)S(1)}, bf16[2,512,256]{2,1,0:T(8,128)(2,1)S(1)}, u32[]{:S(2)}, u32[]{:S(2)}) collective-permute-start(bf16[2,512,256]{2,1,0:T(8,128)(2,1)S(1)} %copy-done.8), channel_id=1, source_target_pairs={{0,2},{1,3},{2,0},{3,1},{4,6},{5,7},{6,4},{7,5},{8,10},{9,11},{10,... | collective-permute-start | bytes 1572872 | tf_op jit(solution)/shard_map/ppermute | solution.py:227
  58.7 0.0 copy-done.7
  58.7 0.9 collective-permute-start.2
  59.6 3.6 %copy.34 = bf16[1,1024,2,1024]{3,1,2,0:T(8,128)(2,1)S(1)} copy(bf16[1,1024,2,1024]{3,2,1,0:T(2,128)(2,1)} %get-tuple-element.28) | data formatting | bytes 8388608
  63.1 8.5 %collective-permute-done.refs_5_ = bf16[2,512,256]{2,1,0:T(8,128)(2,1)S(1)} collective-permute-done((bf16[2,512,256]{2,1,0:T(8,128)(2,1)}, bf16[2,512,256]{2,1,0:T(8,128)(2,1)S(1)}, u32[]{:S(2)}, u32[]{:S(2)}) %collective-permute-start) | collective-permute-done | bytes 524320 | tf_op jit(solution)/shard_map/ppermute | solution.py:227
  71.7 10.1 %collective-permute-done.1.refs_6_ = bf16[2,512,256]{2,1,0:T(8,128)(2,1)S(1)} collective-permute-done((bf16[2,512,256]{2,1,0:T(8,128)(2,1)S(1)}, bf16[2,512,256]{2,1,0:T(8,128)(2,1)S(1)}, u32[]{:S(2)}, u32[]{:S(2)}) %collective-permute-start.1) | collective-permute-done | bytes 524320 | tf_op jit(solution)/shard_map/ppermute | solution.py:227
  81.8 0.7 collective-permute-done.2.refs_7_
  82.5 4.9 %ladder.3 = bf16[512,1152]{1,0:T(8,128)(2,1)} custom-call(s32[2]{0:T(128)S(1)} %pad_add_fusion.refs_0_, s32[8]{0:T(128)S(1)} %copy-done.3, s32[8]{0:T(128)S(1)} %copy-done.4, f32[512]{0:T(512)S(1)} %copy-done.1, bf16[2,512,256]{2,1,0:T(8,128)(2,1)S(1)} %copy-done.2, bf16[2,512,256]{2,1,0:T(8,128)(2,1)S(1)} %collective-permute-done.refs_5_, ...), custom_call_target="tpu_custom_call" | custom-call | flops 2147483648 | bytes 7340032 | tf_op jit(solution)/shard_map/ladder/pallas_call | solution.py:151
  87.4 0.0 all-to-all-done.1
  87.4 11.6 %all-to-all-start.2 = ((bf16[64,8,1152]{2,1,0:T(8,128)(2,1)}), bf16[64,8,1152]{2,1,0:T(8,128)(2,1)S(1)}, u32[]{:S(2)}, u32[]{:S(2)}) async-start(bf16[64,8,1152]{2,1,0:T(8,128)(2,1)} %bitcast.11), calls=%async_computation.2 | async-start | bytes 2359296 | tf_op jit(solution)/shard_map/all_to_all | solution.py:231
  99.0 2.7 %place.2.before = bf16[2,1024,512]{2,1,0:T(8,128)(2,1)} custom-call(bf16[512,1024]{1,0:T(8,128)(2,1)S(1)} %bitcast.22), custom_call_target="tpu_custom_call" | custom-call | flops 536870912 | bytes 2097152 | tf_op jit(solution)/shard_map/place/pallas_call | solution.py:206
  101.6 28.7 %all-to-all-done.2 = bf16[64,8,1152]{2,1,0:T(8,128)(2,1)S(1)} async-done(((bf16[64,8,1152]{2,1,0:T(8,128)(2,1)}), bf16[64,8,1152]{2,1,0:T(8,128)(2,1)S(1)}, u32[]{:S(2)}, u32[]{:S(2)}) %all-to-all-start.2) | async-done | bytes 1179680 | tf_op jit(solution)/shard_map/all_to_all | solution.py:231
  130.4 2.8 %place.3 = (bf16[2,1024,512]{2,1,0:T(8,128)(2,1)}, f32[2,16]{1,0:T(2,128)}) custom-call(bf16[512,1152]{1,0:T(8,128)(2,1)S(1)} %bitcast.20, bf16[512,1152]{1,0:T(8,128)(2,1)S(1)} %bitcast.21, bf16[2,1024,512]{2,1,0:T(8,128)(2,1)} %place.2.before), custom_call_target="tpu_custom_call", output_to_operand_aliasing={{0}: (2, {})} | custom-call | flops 536870912 | bytes 2097152 | tf_op jit(solution)/shard_map/place/pallas_call | solution.py:211
  (11 shorter events, 0.0 us)
Async XLA Ops:
  6.4 29.6 %all-to-all-start = ((bf16[4,2,512,256]{3,2,1,0:T(8,128)(2,1)}), bf16[4,2,512,256]{3,2,1,0:T(8,128)(2,1)S(1)}, u32[]{:S(2)}, u32[]{:S(2)}) async-start(bf16[4,2,512,256]{3,2,1,0:T(8,128)(2,1)} %get-tuple-element.15), calls=%async_computation | async-start | bytes 4194304 | tf_op jit(solution)/shard_map/all_to_all | solution.py:238
  19.3 3.3 %copy-start.1 = (f32[512]{0:T(512)S(1)}, f32[512]{0:T(512)}, u32[]{:S(2)}) copy-start(f32[512]{0:T(512)} %refs_3_.3) | copy-start | bytes 6148
  19.3 3.6 %copy-start.5 = (s32[2,1024,2]{1,2,0:T(2,128)S(1)}, s32[2,1024,2]{1,2,0:T(2,128)}, u32[]{:S(2)}) copy-start(s32[2,1024,2]{1,2,0:T(2,128)} %param.11) | copy-start | bytes 49156
  19.3 3.6 %copy-start.6 = (f32[100]{0:T(128)S(1)}, f32[100]{0:T(128)}, u32[]{:S(2)}) copy-start(f32[100]{0:T(128)} %param.12) | copy-start | bytes 1204
  19.3 16.6 %copy-start.3 = (s32[8]{0:T(128)S(1)}, s32[8]{0:T(128)}, u32[]{:S(2)}) copy-start(s32[8]{0:T(128)} %refs_1_.3) | copy-start | bytes 100
  19.3 16.6 %copy-start.4 = (s32[8]{0:T(128)S(1)}, s32[8]{0:T(128)}, u32[]{:S(2)}) copy-start(s32[8]{0:T(128)} %refs_2_.3) | copy-start | bytes 100
  35.9 2.2 %copy-start = (bf16[1,1024,2,1024]{3,1,2,0:T(8,128)(2,1)S(1)}, bf16[1,1024,2,1024]{3,1,2,0:T(8,128)(2,1)}, u32[]{:S(2)}) copy-start(bf16[1,1024,2,1024]{3,1,2,0:T(8,128)(2,1)} %copy.35) | copy-start | bytes 12582916
  42.2 14.8 %copy-start.8 = (bf16[2,512,256]{2,1,0:T(8,128)(2,1)S(1)}, bf16[2,512,256]{2,1,0:T(8,128)(2,1)}, u32[]{:S(2)}) copy-start(bf16[2,512,256]{2,1,0:T(8,128)(2,1)} %get-tuple-element.23) | copy-start | bytes 1572868
  42.2 16.5 %copy-start.7 = (bf16[2,512,256]{2,1,0:T(8,128)(2,1)S(1)}, bf16[2,512,256]{2,1,0:T(8,128)(2,1)}, u32[]{:S(2)}) copy-start(bf16[2,512,256]{2,1,0:T(8,128)(2,1)} %get-tuple-element.24) | copy-start | bytes 1572868
  42.2 45.2 %all-to-all-start.1 = ((bf16[64,8,1024]{2,1,0:T(8,128)(2,1)}), bf16[64,8,1024]{2,1,0:T(8,128)(2,1)S(1)}, u32[]{:S(2)}, u32[]{:S(2)}) async-start(bf16[64,8,1024]{2,1,0:T(8,128)(2,1)} %bitcast.7), calls=%async_computation.1 | async-start | bytes 2097152 | tf_op jit(solution)/shard_map/all_to_all | solution.py:231
  56.6 15.1 %collective-permute-start = (bf16[2,512,256]{2,1,0:T(8,128)(2,1)}, bf16[2,512,256]{2,1,0:T(8,128)(2,1)S(1)}, u32[]{:S(2)}, u32[]{:S(2)}) collective-permute-start(bf16[2,512,256]{2,1,0:T(8,128)(2,1)} %get-tuple-element.22), channel_id=1, source_target_pairs={{0,1},{1,2},{2,3},{3,0},{4,5},{5,6},{6,7},{7,4},{8,9},{9,10},{10,1... | collective-permute-start | bytes 1572872 | tf_op jit(solution)/shard_map/ppermute | solution.py:227
  56.9 24.8 %collective-permute-start.1 = (bf16[2,512,256]{2,1,0:T(8,128)(2,1)S(1)}, bf16[2,512,256]{2,1,0:T(8,128)(2,1)S(1)}, u32[]{:S(2)}, u32[]{:S(2)}) collective-permute-start(bf16[2,512,256]{2,1,0:T(8,128)(2,1)S(1)} %copy-done.8), channel_id=1, source_target_pairs={{0,2},{1,3},{2,0},{3,1},{4,6},{5,7},{6,4},{7,5},{8,10},{9,11},{10,... | collective-permute-start | bytes 1572872 | tf_op jit(solution)/shard_map/ppermute | solution.py:227
  58.7 23.7 %collective-permute-start.2 = (bf16[2,512,256]{2,1,0:T(8,128)(2,1)S(1)}, bf16[2,512,256]{2,1,0:T(8,128)(2,1)S(1)}, u32[]{:S(2)}, u32[]{:S(2)}) collective-permute-start(bf16[2,512,256]{2,1,0:T(8,128)(2,1)S(1)} %copy-done.7), channel_id=1, source_target_pairs={{0,3},{1,0},{2,1},{3,2},{4,7},{5,4},{6,5},{7,6},{8,11},{9,8},{10,9... | collective-permute-start | bytes 1572872 | tf_op jit(solution)/shard_map/ppermute | solution.py:227
  59.6 22.9 %copy-start.2 = (bf16[2,512,256]{2,1,0:T(8,128)(2,1)S(1)}, bf16[2,512,256]{2,1,0:T(8,128)(2,1)}, u32[]{:S(2)}) copy-start(bf16[2,512,256]{2,1,0:T(8,128)(2,1)} %get-tuple-element.21.refs_4_) | copy-start | bytes 1572868
  87.4 42.9 %all-to-all-start.2 = ((bf16[64,8,1152]{2,1,0:T(8,128)(2,1)}), bf16[64,8,1152]{2,1,0:T(8,128)(2,1)S(1)}, u32[]{:S(2)}, u32[]{:S(2)}) async-start(bf16[64,8,1152]{2,1,0:T(8,128)(2,1)} %bitcast.11), calls=%async_computation.2 | async-start | bytes 2359296 | tf_op jit(solution)/shard_map/all_to_all | solution.py:231

commit v5 on v4

--- a/solution.py
+++ b/solution.py
@@ -26,13 +26,14 @@
     return lax.broadcasted_iota(jnp.int32, shape, axis)
 
 
-def regroup_kernel(pair_ref, x_ref, even, own, plus, far, minus, perm, held):
+def regroup_kernel(parity, pair_ref, x_ref, *refs):
+    outs, (perm, held) = refs[:-2], refs[-2:]
     rows = SUB * IRREPS
 
     @pl.when((pl.program_id(0) == 0) & (pl.program_id(1) == 0))
     def _():
-        to, source = iota((rows, rows), 0), iota((rows, rows), 1)
-        at = (to & (SUB - 1)) * IRREPS + (to >> 5)
+        to, source = iota((rows // 2, rows), 0), iota((rows // 2, rows), 1)
+        at = (to & (SUB - 1)) * IRREPS + 2 * (to >> 5) + parity
         perm[...] = jnp.where(at == source, 1.0, 0.0).astype(jnp.bfloat16)
 
     for sub in range(ABLK // SUB):
@@ -40,41 +41,56 @@
         moved = jnp.dot(perm[...], block, preferred_element_type=jnp.float32).astype(jnp.bfloat16)
         at = slice(sub * SUB, (sub + 1) * SUB)
         for pair in range(4):
-            even[pair, 0, at, :] = moved[(2 * pair) * SUB : (2 * pair + 1) * SUB]
-            held[pair, at, :] = moved[(2 * pair + 1) * SUB : (2 * pair + 2) * SUB]
-    me = pair_ref[0]
-    own[0] = held[me]
-    plus[0] = held[(me + 1) % 4]
-    far[0] = held[(me + 2) % 4]
-    minus[0] = held[(me + 3) % 4]
-
-
-def regroup(pair_id, integrals):
-    each = pltpu.HBM((SLABS, NV, KQ), jnp.bfloat16)
-    spec = pl.BlockSpec((1, ABLK, KQ), lambda s, i, me: (s, i, 0))
+            piece = moved[pair * SUB : (pair + 1) * SUB]
+            if parity == 0:
+                outs[0][pair, 0, at, :] = piece
+            else:
+                held[pair, at, :] = piece
+    if parity == 1:
+        me = pair_ref[0]
+        for shift in range(4):
+            outs[shift][0] = held[(me + shift) % 4]
+
+
+def regroup(parity, pair_id, integrals):
+    if parity == 0:
+        specs = [pl.BlockSpec((4, 1, ABLK, KQ), lambda s, i, me: (0, s, i, 0))]
+        shapes = [pltpu.HBM((4, SLABS, NV, KQ), jnp.bfloat16)]
+    else:
+        specs = [pl.BlockSpec((1, ABLK, KQ), lambda s, i, me: (s, i, 0))] * 4
+        shapes = [pltpu.HBM((SLABS, NV, KQ), jnp.bfloat16)] * 4
     return pl.pallas_call(
-        regroup_kernel,
+        lambda *refs: regroup_kernel(parity, *refs),
         grid_spec=pltpu.PrefetchScalarGridSpec(
             num_scalar_prefetch=1,
             grid=(SLABS, NV // ABLK),
             in_specs=[pl.BlockSpec((1, ABLK * IRREPS, KQ), lambda s, i, me: (s, i, 0))],
-            out_specs=[pl.BlockSpec((4, 1, ABLK, KQ), lambda s, i, me: (0, s, i, 0))] + [spec] * 4,
+            out_specs=specs,
             scratch_shapes=[
-                pltpu.VMEM((SUB * IRREPS, SUB * IRREPS), jnp.bfloat16),
+                pltpu.VMEM((SUB * IRREPS // 2, SUB * IRREPS), jnp.bfloat16),
                 pltpu.VMEM((4, ABLK, KQ), jnp.bfloat16),
             ],
         ),
-        out_shape=[pltpu.HBM((4, SLABS, NV, KQ), jnp.bfloat16)] + [each] * 4,
+        out_shape=shapes,
         compiler_params=pltpu.CompilerParams(vmem_limit_bytes=3 * VMEM),
+        cost_estimate=pl.CostEstimate(flops=1 << 30, bytes_accessed=6 << 20, transcendentals=0),
         name="regroup",
     )(pair_id, integrals.reshape(SLABS, NV * IRREPS, KQ))
 
 
 def ladder_kernel(parity, ids, virt_counts, pair_counts, eps, *refs):
     if parity == 0:
-        pieces, (amp, eps_a, occ, send, energy, held, stage, sems) = refs[:-8], refs[-8:]
+        pieces, (amp_hbm, eps_a, occ, send, energy, held, stage, sems, amp, loads) = refs[:-10], refs[-10:]
     else:
-        pieces, (amp, eps_a, occ, energy0, send, held, stage, sems, energy, extra) = refs[:-10], refs[-10:]
+        pieces, (amp_hbm, eps_a, occ, energy0, send, held, stage, sems, amp, loads, energy, extra) = (
+            refs[:-12],
+            refs[-12:],
+        )
+    fetches = []
+    for block in range(PCAP // RBLK):
+        rows = pl.ds(block * RBLK, RBLK)
+        fetches.append(pltpu.make_async_copy(amp_hbm.at[:, rows, :], amp.at[:, rows, :], loads.at[block]))
+        fetches[-1].start()
     me, virt = ids[0], ids[1]
     h = 2 * me + parity
     mask = jnp.where((iota((1, KQ), 1) & (BLK - 1)) < virt_counts[h], 1.0, 0.0).astype(jnp.bfloat16)
@@ -92,6 +108,7 @@
     copies = []
     for block in range(PCAP // RBLK):
         at = slice(block * RBLK, (block + 1) * RBLK)
+        fetches[block].wait()
         total = None
         for slab in range(SLABS):
             term = lax.dot_general(
@@ -145,21 +162,26 @@
         pltpu.VMEM((NV, SLABS * KS), jnp.bfloat16),
         pltpu.VMEM((PCAP // RBLK, NV, RBLK), jnp.bfloat16),
         pltpu.SemaphoreType.DMA((PCAP // RBLK + 1,)),
+        pltpu.VMEM((SLABS, PCAP, KS), jnp.bfloat16),
+        pltpu.SemaphoreType.DMA((PCAP // RBLK,)),
     ]
     if parity == 1:
         scratch += [pltpu.VMEM((1, PCAP), jnp.float32), pltpu.VMEM((NV, EXTRA), jnp.bfloat16)]
     return pl.pallas_call(
         lambda *refs: ladder_kernel(parity, *refs),
-        in_specs=[pl.BlockSpec(memory_space=pltpu.SMEM)] * 4 + [vmem] * (len(pieces) + 3 + len(energy0)),
+        in_specs=[pl.BlockSpec(memory_space=pltpu.SMEM)] * 4
+        + [vmem] * len(pieces)
+        + [pl.BlockSpec(memory_space=pltpu.HBM)]
+        + [vmem] * (2 + len(energy0)),
         out_specs=[pl.BlockSpec(memory_space=pl.ANY)] + [vmem] * (1 - parity),
         out_shape=[jax.ShapeDtypeStruct((NV, columns), jnp.bfloat16)] + [row] * (1 - parity),
         scratch_shapes=scratch,
         compiler_params=pltpu.CompilerParams(vmem_limit_bytes=VMEM),
         cost_estimate=pl.CostEstimate(
-            flops=2 * NV * PCAP * SLABS * KS, bytes_accessed=7 << 20, transcendentals=0
+            flops=(1 + parity * 8) * 2 * NV * PCAP * SLABS * KS, bytes_accessed=7 << 20, transcendentals=0
         ),
         name="ladder",
-    )(*scalars, *pieces, amp, eps_a, occ, *energy0)
+    )(*scalars, *pieces, pltpu.with_memory_space_constraint(amp, pltpu.HBM), eps_a, occ, *energy0)
 
 
 def put(block, out, perm):
@@ -234,7 +256,8 @@
 def shards(amplitudes, integrals, virt_counts, pair_counts, pair_list, eps_occ, eps_virt):
     me = lax.axis_index("pair").astype(jnp.int32)
     virt = lax.axis_index("virt").astype(jnp.int32)
-    even, own, plus, far, minus = regroup(me[None], integrals)
+    (even,) = regroup(0, me[None], integrals)
+    own, plus, far, minus = regroup(1, me[None], integrals)
     even = lax.all_to_all(even, "pair", 0, 0, tiled=True)
 
     amp = [jnp.transpose(amplitudes[parity], (1, 0, 2)) for parity in range(2)]

time: 134 us -> 130 us (0.970)
  Pallas kernels: 20.2 us -> 31.5 us
  waiting for transfers between devices: 60.1 us -> 50.3 us
  starting transfers between devices: 33.9 us -> 28.7 us
    ppermute x3, waiting for transfers between devices: 19.3 us -> 0.01 us  [step(): return lax.ppermute(value, 'pair', [(i, (i + by) % 4) for i in range(4)])]
    all_to_all x2, waiting for transfers between devices: 28.7 us -> 42.9 us  [across(): return lax.all_to_all(value, 'virt', 0, 0, tiled=True)]
    pallas_call x2, Pallas kernels: 9 us -> 16.4 us  [ladder(): pl.pallas_call(lambda *refs: ladder_kernel(parity, *refs), in_specs=[pl.B...]
    all_to_all x2, starting transfers between devices: 25.9 us -> 21 us  [across(): return lax.all_to_all(value, 'virt', 0, 0, tiled=True)]
    all_to_all x1, waiting for transfers between devices: 12.1 us -> 7.33 us  [shards(): even = lax.all_to_all(even, 'pair', 0, 0, tiled=True)]
    pallas_call x1 -> x2, Pallas kernels: 5.72 us -> 9.61 us  [regroup(): pl.pallas_call(lambda *refs: regroup_kernel(parity, *refs), grid_spec=plt...]
    unnamed x20 -> x24, local copies, waits for them, and re-layouts: 9.08 us -> 9.48 us
  transfers between devices with their start and end apart: 6 -> 6, of which waited for: 5 -> 3; matrix products, arithmetic and copies ran while one was open for 12% -> 14% of each run, Pallas kernels for 6% -> 18%
where the time goes in v5:
time: 130 us
  waiting for transfers between devices  50.3 us (39%)
  Pallas kernels  31.5 us (24%)
  starting transfers between devices  28.7 us (22%)
  local copies, waits for them, and re-layouts  17.6 us (14%)
    all_to_all x2, waiting for transfers between devices, across(): return lax.all_to_all(value, 'virt', 0, 0, tiled=True)  42.9 us
    all_to_all x2, starting transfers between devices, across(): return lax.all_to_all(value, 'virt', 0, 0, tiled=True)  21 us
    pallas_call x2, Pallas kernels, ladder(): pl.pallas_call(lambda *refs: ladder_kernel(parity, *refs), in_specs=[pl.B...  16.4 us
    pallas_call x2, Pallas kernels, regroup(): pl.pallas_call(lambda *refs: regroup_kernel(parity, *refs), grid_spec=plt...  9.61 us
    unnamed x24, local copies, waits for them, and re-layouts  9.48 us
    slice x1, local copies, waits for them, and re-layouts, shards(): amp = [jnp.transpose(amplitudes[parity], (1, 0, 2)) for parity in range(2)]  7.92 us
    all_to_all x1, waiting for transfers between devices, shards(): even = lax.all_to_all(even, 'pair', 0, 0, tiled=True)  7.33 us
    all_to_all x1, starting transfers between devices, shards(): even = lax.all_to_all(even, 'pair', 0, 0, tiled=True)  5.01 us
  transfers between devices with their start and end apart: 6, of which 3 were waited for; matrix products, arithmetic and copies ran while one was open for 14% of the time, Pallas kernels for 18%

profile of v5, /device:TPU:1, one launch (start us, length us, event | category | flops | bytes accessed | tf_op | source)
XLA Modules:
  0.0 129.8 jit_solution(2862654664410480405)
XLA Ops:
  0.6 4.8 %regroup.2 = bf16[4,2,512,256]{3,2,1,0:T(8,128)(2,1)} custom-call(s32[1]{0:T(128)} %bitcast.refs_0_, bf16[2,4096,256]{2,1,0:T(8,128)(2,1)} %bitcast.24), custom_call_target="tpu_custom_call" | custom-call | flops 1073741824 | bytes 6291456 | tf_op jit(solution)/shard_map/regroup/pallas_call | solution.py:62
  5.4 5.0 %all-to-all-start = ((bf16[4,2,512,256]{3,2,1,0:T(8,128)(2,1)}), bf16[4,2,512,256]{3,2,1,0:T(8,128)(2,1)S(1)}, u32[]{:S(2)}, u32[]{:S(2)}) async-start(bf16[4,2,512,256]{3,2,1,0:T(8,128)(2,1)} %regroup.2), calls=%async_computation | async-start | bytes 4194304 | tf_op jit(solution)/shard_map/all_to_all | solution.py:261
  10.4 7.9 %fusion.2 = (bf16[1,1024,2,1024]{3,2,1,0:T(2,128)(2,1)}, bf16[1,1024,2,1024]{3,2,1,0:T(2,128)(2,1)S(1)}) fusion(bf16[2,1024,2,1024]{3,2,1,0:T(2,128)(2,1)} %param.7), kind=kLoop, calls=%fused_computation.7 | loop fusion | bytes 16777216 | tf_op jit(solution)/shard_map/slice | solution.py:263
  18.3 3.3 %copy.35 = bf16[1,1024,2,1024]{3,1,2,0:T(8,128)(2,1)} copy(bf16[1,1024,2,1024]{3,2,1,0:T(2,128)(2,1)S(1)} %get-tuple-element.27) | data formatting | bytes 8388608
  21.7 0.1 copy.21.refs_6_.refs_9_
  21.8 0.0 copy-start.9
  21.8 0.0 copy-start.10
  21.8 0.0 copy-start.2
  21.8 0.0 copy-start.3
  21.9 4.8 %regroup.3 = (bf16[2,512,256]{2,1,0:T(8,128)(2,1)}, bf16[2,512,256]{2,1,0:T(8,128)(2,1)}, bf16[2,512,256]{2,1,0:T(8,128)(2,1)}, bf16[2,512,256]{2,1,0:T(8,128)(2,1)}) custom-call(s32[1]{0:T(128)} %bitcast.refs_0_, bf16[2,4096,256]{2,1,0:T(8,128)(2,1)} %bitcast.25), custom_call_target="tpu_custom_call" | custom-call | flops 1073741824 | bytes 6291456 | tf_op jit(solution)/shard_map/regroup/pallas_call | solution.py:62
  26.7 0.9 fusion
  27.6 7.3 %all-to-all-done.refs_4_ = bf16[4,2,512,256]{3,2,1,0:T(8,128)(2,1)S(1)} async-done(((bf16[4,2,512,256]{3,2,1,0:T(8,128)(2,1)}), bf16[4,2,512,256]{3,2,1,0:T(8,128)(2,1)S(1)}, u32[]{:S(2)}, u32[]{:S(2)}) %all-to-all-start) | async-done | bytes 2097184 | tf_op jit(solution)/shard_map/all_to_all | solution.py:261
  35.0 0.3 collective-permute-start
  35.3 1.8 %collective-permute-start.1 = (bf16[2,512,256]{2,1,0:T(8,128)(2,1)}, bf16[2,512,256]{2,1,0:T(8,128)(2,1)S(1)}, u32[]{:S(2)}, u32[]{:S(2)}) collective-permute-start(bf16[2,512,256]{2,1,0:T(8,128)(2,1)} %get-tuple-element.21), channel_id=1, source_target_pairs={{0,2},{1,3},{2,0},{3,1},{4,6},{5,7},{6,4},{7,5},{8,10},{9,11},{10,... | collective-permute-start | bytes 1572872 | tf_op jit(solution)/shard_map/ppermute | solution.py:249
  37.0 0.6 collective-permute-start.2
  37.7 0.1 pad_add_fusion.refs_0_
  37.7 7.7 %ladder.2 = (bf16[512,1024]{1,0:T(8,128)(2,1)}, f32[1,1024]{1,0:T(1,128)S(1)}) custom-call(s32[2]{0:T(128)S(1)} %pad_add_fusion.refs_0_, s32[8]{0:T(128)S(1)} %copy-done.2, s32[8]{0:T(128)S(1)} %copy-done.3, f32[512]{0:T(512)S(1)} %copy-done, bf16[4,2,512,256]{3,2,1,0:T(8,128)(2,1)S(1)} %all-to-all-done.refs_4_, bf16[2,1024,1024]{2,1,0:T(8,128)(2,1)} %bitcast.26, ...), custom_call_target="tpu_custom_call" | custom-call | flops 2147483648 | bytes 7340032 | tf_op jit(solution)/shard_map/ladder/pallas_call | solution.py:170
  45.5 0.6 copy-done.7
  46.1 14.8 %all-to-all-start.1 = ((bf16[64,8,1024]{2,1,0:T(8,128)(2,1)}), bf16[64,8,1024]{2,1,0:T(8,128)(2,1)S(1)}, u32[]{:S(2)}, u32[]{:S(2)}) async-start(bf16[64,8,1024]{2,1,0:T(8,128)(2,1)} %bitcast.7), calls=%async_computation.1 | async-start | bytes 2097152 | tf_op jit(solution)/shard_map/all_to_all | solution.py:253
  60.9 0.0 copy-start.1
  60.9 0.0 copy-start.4
  60.9 0.0 copy-start.6
  60.9 5.5 %copy.34 = bf16[1,1024,2,1024]{3,1,2,0:T(8,128)(2,1)} copy(bf16[1,1024,2,1024]{3,2,1,0:T(2,128)(2,1)} %get-tuple-element.26) | data formatting | bytes 8388608
  66.5 0.0 collective-permute-done.refs_5_
  66.5 0.0 collective-permute-done.1.refs_6_
  66.5 0.0 collective-permute-done.2.refs_7_
  66.5 8.7 %ladder.3 = bf16[512,1152]{1,0:T(8,128)(2,1)} custom-call(s32[2]{0:T(128)S(1)} %copy-done.6, s32[8]{0:T(128)S(1)} %copy-done.2, s32[8]{0:T(128)S(1)} %copy-done.4, f32[512]{0:T(512)S(1)} %copy-done, bf16[2,512,256]{2,1,0:T(8,128)(2,1)S(1)} %copy-done.1, bf16[2,512,256]{2,1,0:T(8,128)(2,1)S(1)} %collective-permute-done.refs_5_, ...), custom_call_target="tpu_custom_call" | custom-call | flops 19327352832 | bytes 7340032 | tf_op jit(solution)/shard_map/ladder/pallas_call | solution.py:170
  75.2 14.2 %all-to-all-done.1 = bf16[64,8,1024]{2,1,0:T(8,128)(2,1)S(1)} async-done(((bf16[64,8,1024]{2,1,0:T(8,128)(2,1)}), bf16[64,8,1024]{2,1,0:T(8,128)(2,1)S(1)}, u32[]{:S(2)}, u32[]{:S(2)}) %all-to-all-start.1) | async-done | bytes 1048608 | tf_op jit(solution)/shard_map/all_to_all | solution.py:253
  89.4 6.2 %all-to-all-start.2 = ((bf16[64,8,1152]{2,1,0:T(8,128)(2,1)}), bf16[64,8,1152]{2,1,0:T(8,128)(2,1)S(1)}, u32[]{:S(2)}, u32[]{:S(2)}) async-start(bf16[64,8,1152]{2,1,0:T(8,128)(2,1)} %bitcast.11), calls=%async_computation.2 | async-start | bytes 2359296 | tf_op jit(solution)/shard_map/all_to_all | solution.py:253
  95.6 2.7 %place.2.before = bf16[2,1024,512]{2,1,0:T(8,128)(2,1)} custom-call(bf16[512,1024]{1,0:T(8,128)(2,1)S(1)} %bitcast.22), custom_call_target="tpu_custom_call" | custom-call | flops 536870912 | bytes 2097152 | tf_op jit(solution)/shard_map/place/pallas_call | solution.py:228
  98.3 28.7 %all-to-all-done.2 = bf16[64,8,1152]{2,1,0:T(8,128)(2,1)S(1)} async-done(((bf16[64,8,1152]{2,1,0:T(8,128)(2,1)}), bf16[64,8,1152]{2,1,0:T(8,128)(2,1)S(1)}, u32[]{:S(2)}, u32[]{:S(2)}) %all-to-all-start.2) | async-done | bytes 1179680 | tf_op jit(solution)/shard_map/all_to_all | solution.py:253
  127.0 2.8 %place.3 = (bf16[2,1024,512]{2,1,0:T(8,128)(2,1)}, f32[2,16]{1,0:T(2,128)}) custom-call(bf16[512,1152]{1,0:T(8,128)(2,1)S(1)} %bitcast.20, bf16[512,1152]{1,0:T(8,128)(2,1)S(1)} %bitcast.21, bf16[2,1024,512]{2,1,0:T(8,128)(2,1)} %place.2.before), custom_call_target="tpu_custom_call", output_to_operand_aliasing={{0}: (2, {})} | custom-call | flops 536870912 | bytes 2097152 | tf_op jit(solution)/shard_map/place/pallas_call | solution.py:233
  (16 shorter events, 0.1 us)
Async XLA Ops:
  5.4 29.6 %all-to-all-start = ((bf16[4,2,512,256]{3,2,1,0:T(8,128)(2,1)}), bf16[4,2,512,256]{3,2,1,0:T(8,128)(2,1)S(1)}, u32[]{:S(2)}, u32[]{:S(2)}) async-start(bf16[4,2,512,256]{3,2,1,0:T(8,128)(2,1)} %regroup.2), calls=%async_computation | async-start | bytes 4194304 | tf_op jit(solution)/shard_map/all_to_all | solution.py:261
  18.3 3.3 %copy-start = (f32[512]{0:T(512)S(1)}, f32[512]{0:T(512)}, u32[]{:S(2)}) copy-start(f32[512]{0:T(512)} %refs_3_.3) | copy-start | bytes 6148
  21.8 4.9 %copy-start.9 = (s32[2,1024,2]{1,2,0:T(2,128)S(1)}, s32[2,1024,2]{1,2,0:T(2,128)}, u32[]{:S(2)}) copy-start(s32[2,1024,2]{1,2,0:T(2,128)} %param.11) | copy-start | bytes 49156
  21.8 4.9 %copy-start.10 = (f32[100]{0:T(128)S(1)}, f32[100]{0:T(128)}, u32[]{:S(2)}) copy-start(f32[100]{0:T(128)} %param.12) | copy-start | bytes 1204
  21.8 15.9 %copy-start.2 = (s32[8]{0:T(128)S(1)}, s32[8]{0:T(128)}, u32[]{:S(2)}) copy-start(s32[8]{0:T(128)} %refs_1_.3) | copy-start | bytes 100
  21.8 15.9 %copy-start.3 = (s32[8]{0:T(128)S(1)}, s32[8]{0:T(128)}, u32[]{:S(2)}) copy-start(s32[8]{0:T(128)} %refs_2_.3) | copy-start | bytes 100
  35.0 31.5 %collective-permute-start = (bf16[2,512,256]{2,1,0:T(8,128)(2,1)}, bf16[2,512,256]{2,1,0:T(8,128)(2,1)S(1)}, u32[]{:S(2)}, u32[]{:S(2)}) collective-permute-start(bf16[2,512,256]{2,1,0:T(8,128)(2,1)} %get-tuple-element.20), channel_id=1, source_target_pairs={{0,1},{1,2},{2,3},{3,0},{4,5},{5,6},{6,7},{7,4},{8,9},{9,10},{10,1... | collective-permute-start | bytes 1572872 | tf_op jit(solution)/shard_map/ppermute | solution.py:249
  35.3 31.2 %collective-permute-start.1 = (bf16[2,512,256]{2,1,0:T(8,128)(2,1)}, bf16[2,512,256]{2,1,0:T(8,128)(2,1)S(1)}, u32[]{:S(2)}, u32[]{:S(2)}) collective-permute-start(bf16[2,512,256]{2,1,0:T(8,128)(2,1)} %get-tuple-element.21), channel_id=1, source_target_pairs={{0,2},{1,3},{2,0},{3,1},{4,6},{5,7},{6,4},{7,5},{8,10},{9,11},{10,... | collective-permute-start | bytes 1572872 | tf_op jit(solution)/shard_map/ppermute | solution.py:249
  37.0 29.4 %collective-permute-start.2 = (bf16[2,512,256]{2,1,0:T(8,128)(2,1)}, bf16[2,512,256]{2,1,0:T(8,128)(2,1)}, u32[]{:S(2)}, u32[]{:S(2)}) collective-permute-start(bf16[2,512,256]{2,1,0:T(8,128)(2,1)} %get-tuple-element.22), channel_id=1, source_target_pairs={{0,3},{1,0},{2,1},{3,2},{4,7},{5,4},{6,5},{7,6},{8,11},{9,8},{10,9... | collective-permute-start | bytes 1572872 | tf_op jit(solution)/shard_map/ppermute | solution.py:249
  37.7 7.7 %copy-start.5 = (s32[2]{0:T(128)}, s32[2]{0:T(128)S(1)}, u32[]{:S(2)}) copy-start(s32[2]{0:T(128)S(1)} %pad_add_fusion.refs_0_) | copy-start | bytes 28
  45.5 0.6 copy-start.7
  46.1 43.3 %all-to-all-start.1 = ((bf16[64,8,1024]{2,1,0:T(8,128)(2,1)}), bf16[64,8,1024]{2,1,0:T(8,128)(2,1)S(1)}, u32[]{:S(2)}, u32[]{:S(2)}) async-start(bf16[64,8,1024]{2,1,0:T(8,128)(2,1)} %bitcast.7), calls=%async_computation.1 | async-start | bytes 2097152 | tf_op jit(solution)/shard_map/all_to_all | solution.py:253
  60.9 5.6 %copy-start.1 = (bf16[2,512,256]{2,1,0:T(8,128)(2,1)S(1)}, bf16[2,512,256]{2,1,0:T(8,128)(2,1)}, u32[]{:S(2)}) copy-start(bf16[2,512,256]{2,1,0:T(8,128)(2,1)} %get-tuple-element.19.refs_4_) | copy-start | bytes 1572868
  60.9 5.6 %copy-start.4 = (s32[8]{0:T(128)S(1)}, s32[8]{0:T(128)}, u32[]{:S(2)}) copy-start(s32[8]{0:T(128)} %refs_2_.3) | copy-start | bytes 100
  60.9 5.6 %copy-start.6 = (s32[2]{0:T(128)S(1)}, s32[2]{0:T(128)}, u32[]{:S(2)}) copy-start(s32[2]{0:T(128)} %copy-done.5) | copy-start | bytes 28
  60.9 5.6 %copy-start.8 = (f32[1,1024]{1,0:T(1,128)S(1)}, f32[1,1024]{1,0:T(1,128)}, u32[]{:S(2)}) copy-start(f32[1,1024]{1,0:T(1,128)} %copy-done.7) | copy-start | bytes 12292
  89.4 37.6 %all-to-all-start.2 = ((bf16[64,8,1152]{2,1,0:T(8,128)(2,1)}), bf16[64,8,1152]{2,1,0:T(8,128)(2,1)S(1)}, u32[]{:S(2)}, u32[]{:S(2)}) async-start(bf16[64,8,1152]{2,1,0:T(8,128)(2,1)} %bitcast.11), calls=%async_computation.2 | async-start | bytes 2359296 | tf_op jit(solution)/shard_map/all_to_all | solution.py:253

commit v6 on v5

v6 whole, which is shorter than its diff:
```python
import jax
import jax.numpy as jnp
from jax import lax
from jax.experimental import pallas as pl
from jax.experimental.pallas import tpu as pltpu
from jax.sharding import PartitionSpec as P

IRREPS = 8
NV = 512
BLK = 64
SLABS = 2
PCAP = 1024
KQ = 256
KS = 1024
VIRTS = 64
OWN = NV // VIRTS
MINE = PCAP // VIRTS
VMEM = 20 * 1024 * 1024
ABLK = 256
SUB = 32
RBLK = 512
EXTRA = 128


def iota(shape, axis):
    return lax.broadcasted_iota(jnp.int32, shape, axis)


def regroup_kernel(parity, pair_ref, x_hbm, *refs):
    outs, (x, held, loads, stores) = refs[:-4], refs[-4:]
    parts = [(slab, block) for slab in range(SLABS) for block in range(NV // ABLK)]
    fetches = []
    for slab, block in parts:
        at = pl.ds(block * ABLK * IRREPS, ABLK * IRREPS)
        fetch = pltpu.make_async_copy(x_hbm.at[slab, at, :], x.at[slab, at, :], loads.at[slab, block])
        fetch.start()
        fetches.append(fetch)
    rows = SUB * IRREPS
    to, source = iota((rows // 2, rows), 0), iota((rows // 2, rows), 1)
    perm = jnp.where((to & (SUB - 1)) * IRREPS + 2 * (to >> 5) + parity == source, 1.0, 0.0).astype(jnp.bfloat16)
    copies = []
    for fetch, (slab, block) in zip(fetches, parts):
        fetch.wait()
        for sub in range(ABLK // SUB):
            first = block * ABLK + sub * SUB
            moved = jnp.dot(
                perm,
                x[slab, first * IRREPS : first * IRREPS + rows, :],
                preferred_element_type=jnp.float32,
            ).astype(jnp.bfloat16)
            for pair in range(4):
                held[pair, slab, first : first + SUB, :] = moved[pair * SUB : (pair + 1) * SUB]
        if parity == 0:
            at = pl.ds(block * ABLK, ABLK)
            copy = pltpu.make_async_copy(
                held.at[:, slab, at, :], outs[0].at[:, slab, at, :], stores.at[slab * (NV // ABLK) + block]
            )
            copy.start()
            copies.append(copy)
    if parity == 1:
        me = pair_ref[0]
        for shift in range(4):
            copy = pltpu.make_async_copy(held.at[(me + shift) % 4], outs[shift], stores.at[shift])
            copy.start()
            copies.append(copy)
    for copy in copies:
        copy.wait()


def regroup(parity, pair_id, integrals):
    if parity == 0:
        shapes = [pltpu.HBM((4, SLABS, NV, KQ), jnp.bfloat16)]
    else:
        shapes = [pltpu.HBM((SLABS, NV, KQ), jnp.bfloat16)] * 4
    flat = pltpu.with_memory_space_constraint(integrals.reshape(SLABS, NV * IRREPS, KQ), pltpu.HBM)
    return pl.pallas_call(
        lambda *refs: regroup_kernel(parity, *refs),
        in_specs=[pl.BlockSpec(memory_space=pltpu.SMEM), pl.BlockSpec(memory_space=pltpu.HBM)],
        out_specs=[pl.BlockSpec(memory_space=pltpu.HBM)] * len(shapes),
        out_shape=shapes,
        scratch_shapes=[
            pltpu.VMEM((SLABS, NV * IRREPS, KQ), jnp.bfloat16),
            pltpu.VMEM((4, SLABS, NV, KQ), jnp.bfloat16),
            pltpu.SemaphoreType.DMA((SLABS, NV // ABLK)),
            pltpu.SemaphoreType.DMA((SLABS * (NV // ABLK),)),
        ],
        compiler_params=pltpu.CompilerParams(vmem_limit_bytes=VMEM),
        cost_estimate=pl.CostEstimate(flops=1 << 30, bytes_accessed=6 << 20, transcendentals=0),
        name="regroup",
    )(pair_id, flat)


def ladder_kernel(parity, ids, virt_counts, pair_counts, eps, *refs):
    if parity == 0:
        pieces, (amp, eps_a, occ, send, energy_out, held, stage, sems, energy) = refs[:-9], refs[-9:]
    else:
        pieces, (amp, eps_a, occ, energy0, send, held, stage, sems, energy, extra) = refs[:-10], refs[-10:]
    me, virt = ids[0], ids[1]
    h = 2 * me + parity
    mask = jnp.where((iota((1, KQ), 1) & (BLK - 1)) < virt_counts[h], 1.0, 0.0).astype(jnp.bfloat16)
    for slab in range(SLABS):
        if parity == 0:
            for source in range(4):
                to = slab * KS + source * KQ
                held[:, to : to + KQ] = pieces[0][source, slab] * mask
        else:
            for shift, piece in zip((0, 3, 2, 1), pieces):
                to = pl.multiple_of(slab * KS + ((me + shift) % 4) * KQ, KQ)
                held[:, pl.ds(to, KQ)] = piece[slab] * mask
    slot = iota((BLK, RBLK), 0)
    column = iota((BLK, RBLK), 1)
    copies = []
    for block in range(PCAP // RBLK):
        at = slice(block * RBLK, (block + 1) * RBLK)
        total = None
        for slab in range(SLABS):
            term = lax.dot_general(
                held[:, slab * KS : (slab + 1) * KS],
                amp[slab, at, :],
                (((1,), (1,)), ((), ())),
                preferred_element_type=jnp.float32,
            )
            total = term if total is None else total + term
        occ_row = occ[parity : parity + 1, at]
        live_row = block * RBLK + column < pair_counts[h]
        summed = jnp.zeros((1, RBLK), jnp.float32)
        for ha in range(IRREPS):
            rows = slice(ha * BLK, (ha + 1) * BLK)
            hb = jnp.bitwise_xor(h, ha)
            part = total[rows]
            denom = (eps_a[rows, :] + eps[hb * BLK + virt]) - occ_row
            live_a = jnp.where(virt < virt_counts[hb], virt_counts[ha], 0)
            ratio = jnp.where((slot < live_a) & live_row, part / denom, 0.0)
            summed = summed + jnp.sum(ratio * part, axis=0, keepdims=True)
            stage[block, rows, :] = ratio.astype(jnp.bfloat16)
        energy[:, at] = summed / (NV * BLK)
        copy = pltpu.make_async_copy(stage.at[block], send.at[:, pl.ds(block * RBLK, RBLK)], sems.at[block])
        copy.start()
        copies.append(copy)
    if parity == 0:
        copy = pltpu.make_async_copy(energy, energy_out, sems.at[PCAP // RBLK])
        copy.start()
        copies.append(copy)
    else:
        value = jnp.concatenate([energy0[...], energy[...]], axis=0)
        high = value.astype(jnp.bfloat16).astype(jnp.float32)
        rest = value - high
        middle = rest.astype(jnp.bfloat16).astype(jnp.float32)
        low = rest - middle
        terms = jnp.concatenate([high, middle, low, jnp.zeros((2, PCAP), jnp.float32)], axis=0)
        spread = jnp.broadcast_to(terms[None], (VIRTS, OWN, PCAP)).reshape(NV, PCAP)
        owner = (iota((NV, PCAP), 1) // MINE) == (iota((NV, PCAP), 0) // OWN)
        spread = jnp.where(owner, spread, 0.0).astype(jnp.bfloat16)
        lane = (iota((PCAP, EXTRA), 0) & (MINE - 1)) == iota((PCAP, EXTRA), 1)
        select = jnp.where(lane, 1.0, 0.0).astype(jnp.bfloat16)
        extra[...] = jnp.dot(spread, select, preferred_element_type=jnp.float32).astype(jnp.bfloat16)
        copy = pltpu.make_async_copy(extra, send.at[:, pl.ds(PCAP, EXTRA)], sems.at[PCAP // RBLK])
        copy.start()
        copies.append(copy)
    for copy in copies:
        copy.wait()


def ladder(parity, scalars, pieces, amp, eps_a, occ, *energy0):
    vmem = pl.BlockSpec(memory_space=pltpu.VMEM)
    columns = PCAP if parity == 0 else PCAP + EXTRA
    row = pltpu.HBM((1, PCAP), jnp.float32)
    scratch = [
        pltpu.VMEM((NV, SLABS * KS), jnp.bfloat16),
        pltpu.VMEM((PCAP // RBLK, NV, RBLK), jnp.bfloat16),
        pltpu.SemaphoreType.DMA((PCAP // RBLK + 1,)),
        pltpu.VMEM((1, PCAP), jnp.float32),
    ]
    if parity == 1:
        scratch.append(pltpu.VMEM((NV, EXTRA), jnp.bfloat16))
    return pl.pallas_call(
        lambda *refs: ladder_kernel(parity, *refs),
        in_specs=[pl.BlockSpec(memory_space=pltpu.SMEM)] * 4
        + [vmem] * (len(pieces) + 3 + len(energy0)),
        out_specs=[pl.BlockSpec(memory_space=pltpu.HBM)] * (2 - parity),
        out_shape=[pltpu.HBM((NV, columns), jnp.bfloat16)] + [row] * (1 - parity),
        scratch_shapes=scratch,
        compiler_params=pltpu.CompilerParams(vmem_limit_bytes=VMEM),
        cost_estimate=pl.CostEstimate(
            flops=(1 + parity * 8) * 2 * NV * PCAP * SLABS * KS, bytes_accessed=7 << 20, transcendentals=0
        ),
        name="ladder",
    )(*scalars, *pieces, amp, eps_a, occ, *energy0)


def place_kernel(parity, block, *refs):
    if parity == 0:
        out, stage, sems = refs
    else:
        _, out, energy, stage, sems = refs
    source, to = iota((NV, NV), 0), iota((NV, NV), 1)
    perm = jnp.where((source & (OWN - 1)) * BLK + (source >> 3) == to, 1.0, 0.0).astype(jnp.bfloat16)
    copies = []
    for part in range(PCAP // RBLK):
        stage[part] = lax.dot_general(
            block[:, part * RBLK : (part + 1) * RBLK],
            perm,
            (((0,), (0,)), ((), ())),
            preferred_element_type=jnp.float32,
        ).astype(jnp.bfloat16)
        copy = pltpu.make_async_copy(stage.at[part], out.at[parity, pl.ds(part * RBLK, RBLK), :], sems.at[part])
        copy.start()
        copies.append(copy)
    if parity == 1:
        values = block[:, PCAP : PCAP + EXTRA].astype(jnp.float32)
        kind = iota((NV, EXTRA), 0) & (OWN - 1)
        for which in range(2):
            mine = (kind < 6) & ((kind & 1) == which)
            summed = jnp.sum(jnp.where(mine, values, 0.0), axis=0, keepdims=True)
            energy[which : which + 1, :] = summed[:, :MINE]
    for copy in copies:
        copy.wait()


def place(parity, block, *before):
    vmem = pl.BlockSpec(memory_space=pltpu.VMEM)
    hbm = pl.BlockSpec(memory_space=pl.ANY)
    out = jax.ShapeDtypeStruct((2, PCAP, NV), jnp.bfloat16)
    return pl.pallas_call(
        lambda *refs: place_kernel(parity, *refs),
        in_specs=[vmem] + [hbm] * parity,
        out_specs=[hbm] + [vmem] * parity,
        out_shape=[out] + [jax.ShapeDtypeStruct((2, MINE), jnp.float32)] * parity,
        input_output_aliases={1: 0} if parity else {},
        scratch_shapes=[
            pltpu.VMEM((PCAP // RBLK, RBLK, NV), jnp.bfloat16),
            pltpu.SemaphoreType.DMA((PCAP // RBLK,)),
        ],
        compiler_params=pltpu.CompilerParams(vmem_limit_bytes=VMEM),
        cost_estimate=pl.CostEstimate(flops=2 * NV * NV * PCAP, bytes_accessed=2 << 20, transcendentals=0),
        name="place",
    )(block, *before)


def pick(ids, table):
    onehot = ids[..., None] == jnp.arange(table.shape[0], dtype=jnp.int32)
    return jnp.sum(jnp.where(onehot, table, 0), axis=-1)


def step(value, by):
    return lax.ppermute(value, "pair", [(i, (i + by) % 4) for i in range(4)])


def across(value):
    return lax.all_to_all(value, "virt", 0, 0, tiled=True)


def shards(amplitudes, integrals, virt_counts, pair_counts, pair_list, eps_occ, eps_virt):
    me = lax.axis_index("pair").astype(jnp.int32)
    virt = lax.axis_index("virt").astype(jnp.int32)
    (even,) = regroup(0, me[None], integrals)
    own, plus, far, minus = regroup(1, me[None], integrals)
    even = lax.all_to_all(even, "pair", 0, 0, tiled=True)

    amp = [jnp.transpose(amplitudes[parity], (1, 0, 2)) for parity in range(2)]
    occ_terms = pick(pair_list, eps_occ)
    occ = occ_terms[:, :, 0] + occ_terms[:, :, 1]
    eps_a = eps_virt[:, None]
    scalars = (jnp.stack([me, virt]), virt_counts, pair_counts, eps_virt)

    even, plus, far, minus = lax.optimization_barrier((even, plus, far, minus))
    left, far, right = step(plus, 1), step(far, 2), step(minus, 3)
    send, energy0 = ladder(0, scalars, (even,), amp[0], eps_a, occ)
    first = across(send)
    (send,) = ladder(1, scalars, (own, left, far, right), amp[1], eps_a, occ, energy0)
    first, send = lax.optimization_barrier((first, send))
    second = across(send)
    (out,) = place(0, first)
    return tuple(place(1, second, out))


def solution(mesh):
    placed = (
        P("pair", None, None, None),
        P(None, None, None, ("virt", "pair")),
        P(),
        P(),
        P("pair", None, None),
        P(),
        P(),
    )
    return jax.shard_map(
        shards,
        mesh=mesh,
        in_specs=placed,
        out_specs=(P("pair", None, "virt"), P("pair", "virt")),
        check_vma=False,
    )
```

time: 130 us -> 126 us (0.969)
  Pallas kernels: 31.5 us -> 20.5 us
  waiting for transfers between devices: 50.3 us -> 57.5 us
    pallas_call x2, Pallas kernels: 16.4 us -> 9.44 us  [ladder(): pl.pallas_call(lambda *refs: ladder_kernel(parity, *refs), in_specs=[pl.B...]
    all_to_all x2, waiting for transfers between devices: 42.9 us -> 49.2 us  [across(): return lax.all_to_all(value, 'virt', 0, 0, tiled=True)]
    pallas_call x4, Pallas kernels: 15.1 us -> 11.1 us  [the longest x2 7.24 us: regroup(): pl.pallas_call(lambda *refs: regroup_kernel(parity, *refs), in_specs=[pl....]
  transfers between devices with their start and end apart: 6 -> 6, of which waited for: 3 -> 3; matrix products, arithmetic and copies ran while one was open for 14% -> 13% of each run, Pallas kernels for 18% -> 12%
where the time goes in v6:
time: 126 us
  waiting for transfers between devices  57.5 us (46%)
  starting transfers between devices  28.7 us (23%)
  Pallas kernels  20.5 us (16%)
  local copies, waits for them, and re-layouts  17.2 us (14%)
    all_to_all x2, waiting for transfers between devices, across(): return lax.all_to_all(value, 'virt', 0, 0, tiled=True)  49.2 us
    all_to_all x2, starting transfers between devices, across(): return lax.all_to_all(value, 'virt', 0, 0, tiled=True)  21 us
    pallas_call x2, Pallas kernels, ladder(): pl.pallas_call(lambda *refs: ladder_kernel(parity, *refs), in_specs=[pl.B...  9.44 us
    unnamed x24, local copies, waits for them, and re-layouts  9.08 us
    all_to_all x1, waiting for transfers between devices, shards(): even = lax.all_to_all(even, 'pair', 0, 0, tiled=True)  8.24 us
    slice x1, local copies, waits for them, and re-layouts, shards(): amp = [jnp.transpose(amplitudes[parity], (1, 0, 2)) for parity in range(2)]  7.92 us
    pallas_call x2, Pallas kernels, regroup(): pl.pallas_call(lambda *refs: regroup_kernel(parity, *refs), in_specs=[pl....  7.24 us
    all_to_all x1, starting transfers between devices, shards(): even = lax.all_to_all(even, 'pair', 0, 0, tiled=True)  5.03 us
  transfers between devices with their start and end apart: 6, of which 3 were waited for; matrix products, arithmetic and copies ran while one was open for 13% of the time, Pallas kernels for 12%

profile of v6, /device:TPU:1, one launch (start us, length us, event | category | flops | bytes accessed | tf_op | source)
XLA Modules:
  0.0 125.9 jit_solution(2613070477406765632)
XLA Ops:
  0.6 3.3 %regroup.2 = bf16[4,2,512,256]{3,2,1,0:T(8,128)(2,1)} custom-call(s32[1]{0:T(128)} %bitcast.refs_0_, bf16[2,4096,256]{2,1,0:T(8,128)(2,1)} %bitcast.25), custom_call_target="tpu_custom_call" | custom-call | flops 1073741824 | bytes 6291456 | tf_op jit(solution)/shard_map/regroup/pallas_call | solution.py:76
  4.0 5.0 %all-to-all-start = ((bf16[4,2,512,256]{3,2,1,0:T(8,128)(2,1)}), bf16[4,2,512,256]{3,2,1,0:T(8,128)(2,1)S(1)}, u32[]{:S(2)}, u32[]{:S(2)}) async-start(bf16[4,2,512,256]{3,2,1,0:T(8,128)(2,1)} %regroup.2), calls=%async_computation | async-start | bytes 4194304 | tf_op jit(solution)/shard_map/all_to_all | solution.py:258
  9.0 7.9 %fusion.2 = (bf16[1,1024,2,1024]{3,2,1,0:T(2,128)(2,1)}, bf16[1,1024,2,1024]{3,2,1,0:T(2,128)(2,1)S(1)}) fusion(bf16[2,1024,2,1024]{3,2,1,0:T(2,128)(2,1)} %param.7), kind=kLoop, calls=%fused_computation.7 | loop fusion | bytes 16777216 | tf_op jit(solution)/shard_map/slice | solution.py:260
  16.9 3.3 %copy.35 = bf16[1,1024,2,1024]{3,1,2,0:T(8,128)(2,1)} copy(bf16[1,1024,2,1024]{3,2,1,0:T(2,128)(2,1)S(1)} %get-tuple-element.27) | data formatting | bytes 8388608
  20.2 0.1 copy.21.refs_6_.refs_9_
  20.4 0.0 copy-start.9
  20.4 0.0 copy-start.10
  20.4 0.0 copy-start.3
  20.4 0.0 copy-start.4
  20.4 3.9 %regroup.3 = (bf16[2,512,256]{2,1,0:T(8,128)(2,1)}, bf16[2,512,256]{2,1,0:T(8,128)(2,1)}, bf16[2,512,256]{2,1,0:T(8,128)(2,1)}, bf16[2,512,256]{2,1,0:T(8,128)(2,1)}) custom-call(s32[1]{0:T(128)} %bitcast.refs_0_, bf16[2,4096,256]{2,1,0:T(8,128)(2,1)} %bitcast.26), custom_call_target="tpu_custom_call" | custom-call | flops 1073741824 | bytes 6291456 | tf_op jit(solution)/shard_map/regroup/pallas_call | solution.py:76
  24.4 0.9 fusion
  25.3 8.2 %all-to-all-done.refs_4_ = bf16[4,2,512,256]{3,2,1,0:T(8,128)(2,1)S(1)} async-done(((bf16[4,2,512,256]{3,2,1,0:T(8,128)(2,1)}), bf16[4,2,512,256]{3,2,1,0:T(8,128)(2,1)S(1)}, u32[]{:S(2)}, u32[]{:S(2)}) %all-to-all-start) | async-done | bytes 2097184 | tf_op jit(solution)/shard_map/all_to_all | solution.py:258
  33.6 0.3 collective-permute-start
  33.9 1.8 %collective-permute-start.1 = (bf16[2,512,256]{2,1,0:T(8,128)(2,1)}, bf16[2,512,256]{2,1,0:T(8,128)(2,1)S(1)}, u32[]{:S(2)}, u32[]{:S(2)}) collective-permute-start(bf16[2,512,256]{2,1,0:T(8,128)(2,1)} %get-tuple-element.21), channel_id=1, source_target_pairs={{0,2},{1,3},{2,0},{3,1},{4,6},{5,7},{6,4},{7,5},{8,10},{9,11},{10,... | collective-permute-start | bytes 1572872 | tf_op jit(solution)/shard_map/ppermute | solution.py:246
  35.6 0.6 collective-permute-start.2
  36.3 0.1 pad_add_fusion.refs_0_
  36.3 2.2 %copy-done = bf16[1,1024,2,1024]{3,1,2,0:T(8,128)(2,1)S(1)} copy-done((bf16[1,1024,2,1024]{3,1,2,0:T(8,128)(2,1)S(1)}, bf16[1,1024,2,1024]{3,1,2,0:T(8,128)(2,1)}, u32[]{:S(2)}) %copy-start) | copy-done | bytes 4194328
  38.5 4.0 %ladder.2 = (bf16[512,1024]{1,0:T(8,128)(2,1)}, f32[1,1024]{1,0:T(1,128)}) custom-call(s32[2]{0:T(128)S(1)} %pad_add_fusion.refs_0_, s32[8]{0:T(128)S(1)} %copy-done.3, s32[8]{0:T(128)S(1)} %copy-done.4, f32[512]{0:T(512)S(1)} %copy-done.1, bf16[4,2,512,256]{3,2,1,0:T(8,128)(2,1)S(1)} %all-to-all-done.refs_4_, bf16[2,1024,1024]{2,1,0:T(8,128)(2,1)S(1)} %bitcast.22, ...), custom_call_target="tpu_custom_call" | custom-call | flops 2147483648 | bytes 7340032 | tf_op jit(solution)/shard_map/ladder/pallas_call | solution.py:176
  42.6 14.8 %all-to-all-start.1 = ((bf16[64,8,1024]{2,1,0:T(8,128)(2,1)}), bf16[64,8,1024]{2,1,0:T(8,128)(2,1)S(1)}, u32[]{:S(2)}, u32[]{:S(2)}) async-start(bf16[64,8,1024]{2,1,0:T(8,128)(2,1)} %bitcast.28), calls=%async_computation.1 | async-start | bytes 2097152 | tf_op jit(solution)/shard_map/all_to_all | solution.py:250
  57.4 0.0 copy-start.2
  57.4 0.0 copy-start.5
  57.4 0.0 copy-start.7
  57.4 3.5 %copy.34 = bf16[1,1024,2,1024]{3,1,2,0:T(8,128)(2,1)S(1)} copy(bf16[1,1024,2,1024]{3,2,1,0:T(2,128)(2,1)} %get-tuple-element.26) | data formatting | bytes 8388608
  61.0 0.0 collective-permute-done.refs_5_
  61.0 0.0 collective-permute-done.1.refs_6_
  61.0 0.0 collective-permute-done.2.refs_7_
  61.0 5.4 %ladder.3 = bf16[512,1152]{1,0:T(8,128)(2,1)} custom-call(s32[2]{0:T(128)S(1)} %copy-done.7, s32[8]{0:T(128)S(1)} %copy-done.3, s32[8]{0:T(128)S(1)} %copy-done.5, f32[512]{0:T(512)S(1)} %copy-done.1, bf16[2,512,256]{2,1,0:T(8,128)(2,1)S(1)} %copy-done.2, bf16[2,512,256]{2,1,0:T(8,128)(2,1)S(1)} %collective-permute-done.refs_5_, ...), custom_call_target="tpu_custom_call" | custom-call | flops 19327352832 | bytes 7340032 | tf_op jit(solution)/shard_map/ladder/pallas_call | solution.py:176
  66.4 19.5 %all-to-all-done.1 = bf16[64,8,1024]{2,1,0:T(8,128)(2,1)S(1)} async-done(((bf16[64,8,1024]{2,1,0:T(8,128)(2,1)}), bf16[64,8,1024]{2,1,0:T(8,128)(2,1)S(1)}, u32[]{:S(2)}, u32[]{:S(2)}) %all-to-all-start.1) | async-done | bytes 1048608 | tf_op jit(solution)/shard_map/all_to_all | solution.py:250
  85.9 6.2 %all-to-all-start.2 = ((bf16[64,8,1152]{2,1,0:T(8,128)(2,1)}), bf16[64,8,1152]{2,1,0:T(8,128)(2,1)S(1)}, u32[]{:S(2)}, u32[]{:S(2)}) async-start(bf16[64,8,1152]{2,1,0:T(8,128)(2,1)} %bitcast.27), calls=%async_computation.2 | async-start | bytes 2359296 | tf_op jit(solution)/shard_map/all_to_all | solution.py:250
  92.1 1.6 %place.2.refs_1_ = bf16[2,1024,512]{2,1,0:T(8,128)(2,1)} custom-call(bf16[512,1024]{1,0:T(8,128)(2,1)S(1)} %bitcast.21), custom_call_target="tpu_custom_call" | custom-call | flops 536870912 | bytes 2097152 | tf_op jit(solution)/shard_map/place/pallas_call | solution.py:224
  93.8 29.7 %all-to-all-done.2 = bf16[64,8,1152]{2,1,0:T(8,128)(2,1)S(1)} async-done(((bf16[64,8,1152]{2,1,0:T(8,128)(2,1)}), bf16[64,8,1152]{2,1,0:T(8,128)(2,1)S(1)}, u32[]{:S(2)}, u32[]{:S(2)}) %all-to-all-start.2) | async-done | bytes 1179680 | tf_op jit(solution)/shard_map/all_to_all | solution.py:250
  123.5 2.2 %place.3 = (bf16[2,1024,512]{2,1,0:T(8,128)(2,1)}, f32[2,16]{1,0:T(2,128)}) custom-call(bf16[512,1152]{1,0:T(8,128)(2,1)S(1)} %bitcast.20, bf16[2,1024,512]{2,1,0:T(8,128)(2,1)} %place.2.refs_1_), custom_call_target="tpu_custom_call", output_to_operand_aliasing={{0}: (1, {})} | custom-call | flops 536870912 | bytes 2097152 | tf_op jit(solution)/shard_map/place/pallas_call | solution.py:224
  (16 shorter events, 0.1 us)
Async XLA Ops:
  4.0 29.6 %all-to-all-start = ((bf16[4,2,512,256]{3,2,1,0:T(8,128)(2,1)}), bf16[4,2,512,256]{3,2,1,0:T(8,128)(2,1)S(1)}, u32[]{:S(2)}, u32[]{:S(2)}) async-start(bf16[4,2,512,256]{3,2,1,0:T(8,128)(2,1)} %regroup.2), calls=%async_computation | async-start | bytes 4194304 | tf_op jit(solution)/shard_map/all_to_all | solution.py:258
  16.9 3.3 %copy-start.1 = (f32[512]{0:T(512)S(1)}, f32[512]{0:T(512)}, u32[]{:S(2)}) copy-start(f32[512]{0:T(512)} %refs_3_.3) | copy-start | bytes 6148
  20.4 4.0 %copy-start.9 = (s32[2,1024,2]{1,2,0:T(2,128)S(1)}, s32[2,1024,2]{1,2,0:T(2,128)}, u32[]{:S(2)}) copy-start(s32[2,1024,2]{1,2,0:T(2,128)} %param.11) | copy-start | bytes 49156
  20.4 3.9 %copy-start.10 = (f32[100]{0:T(128)S(1)}, f32[100]{0:T(128)}, u32[]{:S(2)}) copy-start(f32[100]{0:T(128)} %param.12) | copy-start | bytes 1204
  20.4 15.9 %copy-start.3 = (s32[8]{0:T(128)S(1)}, s32[8]{0:T(128)}, u32[]{:S(2)}) copy-start(s32[8]{0:T(128)} %refs_1_.3) | copy-start | bytes 100
  20.4 15.9 %copy-start.4 = (s32[8]{0:T(128)S(1)}, s32[8]{0:T(128)}, u32[]{:S(2)}) copy-start(s32[8]{0:T(128)} %refs_2_.3) | copy-start | bytes 100
  33.6 27.4 %collective-permute-start = (bf16[2,512,256]{2,1,0:T(8,128)(2,1)}, bf16[2,512,256]{2,1,0:T(8,128)(2,1)S(1)}, u32[]{:S(2)}, u32[]{:S(2)}) collective-permute-start(bf16[2,512,256]{2,1,0:T(8,128)(2,1)} %get-tuple-element.20), channel_id=1, source_target_pairs={{0,1},{1,2},{2,3},{3,0},{4,5},{5,6},{6,7},{7,4},{8,9},{9,10},{10,1... | collective-permute-start | bytes 1572872 | tf_op jit(solution)/shard_map/ppermute | solution.py:246
  33.9 27.1 %collective-permute-start.1 = (bf16[2,512,256]{2,1,0:T(8,128)(2,1)}, bf16[2,512,256]{2,1,0:T(8,128)(2,1)S(1)}, u32[]{:S(2)}, u32[]{:S(2)}) collective-permute-start(bf16[2,512,256]{2,1,0:T(8,128)(2,1)} %get-tuple-element.21), channel_id=1, source_target_pairs={{0,2},{1,3},{2,0},{3,1},{4,6},{5,7},{6,4},{7,5},{8,10},{9,11},{10,... | collective-permute-start | bytes 1572872 | tf_op jit(solution)/shard_map/ppermute | solution.py:246
  35.6 25.3 %collective-permute-start.2 = (bf16[2,512,256]{2,1,0:T(8,128)(2,1)}, bf16[2,512,256]{2,1,0:T(8,128)(2,1)}, u32[]{:S(2)}, u32[]{:S(2)}) collective-permute-start(bf16[2,512,256]{2,1,0:T(8,128)(2,1)} %get-tuple-element.22), channel_id=1, source_target_pairs={{0,3},{1,0},{2,1},{3,2},{4,7},{5,4},{6,5},{7,6},{8,11},{9,8},{10,9... | collective-permute-start | bytes 1572872 | tf_op jit(solution)/shard_map/ppermute | solution.py:246
  36.3 6.3 %copy-start.6 = (s32[2]{0:T(128)}, s32[2]{0:T(128)S(1)}, u32[]{:S(2)}) copy-start(s32[2]{0:T(128)S(1)} %pad_add_fusion.refs_0_) | copy-start | bytes 28
  36.3 2.2 %copy-start = (bf16[1,1024,2,1024]{3,1,2,0:T(8,128)(2,1)S(1)}, bf16[1,1024,2,1024]{3,1,2,0:T(8,128)(2,1)}, u32[]{:S(2)}) copy-start(bf16[1,1024,2,1024]{3,1,2,0:T(8,128)(2,1)} %copy.35) | copy-start | bytes 12582916
  42.6 43.3 %all-to-all-start.1 = ((bf16[64,8,1024]{2,1,0:T(8,128)(2,1)}), bf16[64,8,1024]{2,1,0:T(8,128)(2,1)S(1)}, u32[]{:S(2)}, u32[]{:S(2)}) async-start(bf16[64,8,1024]{2,1,0:T(8,128)(2,1)} %bitcast.28), calls=%async_computation.1 | async-start | bytes 2097152 | tf_op jit(solution)/shard_map/all_to_all | solution.py:250
  57.4 3.6 %copy-start.2 = (bf16[2,512,256]{2,1,0:T(8,128)(2,1)S(1)}, bf16[2,512,256]{2,1,0:T(8,128)(2,1)}, u32[]{:S(2)}) copy-start(bf16[2,512,256]{2,1,0:T(8,128)(2,1)} %get-tuple-element.19.refs_4_) | copy-start | bytes 1572868
  57.4 3.6 %copy-start.5 = (s32[8]{0:T(128)S(1)}, s32[8]{0:T(128)}, u32[]{:S(2)}) copy-start(s32[8]{0:T(128)} %refs_2_.3) | copy-start | bytes 100
  57.4 3.6 %copy-start.7 = (s32[2]{0:T(128)S(1)}, s32[2]{0:T(128)}, u32[]{:S(2)}) copy-start(s32[2]{0:T(128)} %copy-done.6) | copy-start | bytes 28
  57.4 3.6 %copy-start.8 = (f32[1,1024]{1,0:T(1,128)S(1)}, f32[1,1024]{1,0:T(1,128)}, u32[]{:S(2)}) copy-start(f32[1,1024]{1,0:T(1,128)} %get-tuple-element.23.refs_11_) | copy-start | bytes 12292
  85.9 37.6 %all-to-all-start.2 = ((bf16[64,8,1152]{2,1,0:T(8,128)(2,1)}), bf16[64,8,1152]{2,1,0:T(8,128)(2,1)S(1)}, u32[]{:S(2)}, u32[]{:S(2)}) async-start(bf16[64,8,1152]{2,1,0:T(8,128)(2,1)} %bitcast.27), calls=%async_computation.2 | async-start | bytes 2359296 | tf_op jit(solution)/shard_map/all_to_all | solution.py:250

commit v7 on v6

--- a/solution.py
+++ b/solution.py
@@ -192,10 +192,20 @@
     if parity == 0:
         out, stage, sems = refs
     else:
-        _, out, energy, stage, sems = refs
+        _, out, energy_out, stage, sems, energy = refs
     source, to = iota((NV, NV), 0), iota((NV, NV), 1)
     perm = jnp.where((source & (OWN - 1)) * BLK + (source >> 3) == to, 1.0, 0.0).astype(jnp.bfloat16)
     copies = []
+    if parity == 1:
+        values = block[:, PCAP : PCAP + EXTRA].astype(jnp.float32)
+        kind = iota((NV, EXTRA), 0) & (OWN - 1)
+        for which in range(2):
+            mine = (kind < 6) & ((kind & 1) == which)
+            summed = jnp.sum(jnp.where(mine, values, 0.0), axis=0, keepdims=True)
+            energy[which : which + 1, :] = summed[:, :MINE]
+        copy = pltpu.make_async_copy(energy, energy_out, sems.at[PCAP // RBLK])
+        copy.start()
+        copies.append(copy)
     for part in range(PCAP // RBLK):
         stage[part] = lax.dot_general(
             block[:, part * RBLK : (part + 1) * RBLK],
@@ -206,13 +216,6 @@
         copy = pltpu.make_async_copy(stage.at[part], out.at[parity, pl.ds(part * RBLK, RBLK), :], sems.at[part])
         copy.start()
         copies.append(copy)
-    if parity == 1:
-        values = block[:, PCAP : PCAP + EXTRA].astype(jnp.float32)
-        kind = iota((NV, EXTRA), 0) & (OWN - 1)
-        for which in range(2):
-            mine = (kind < 6) & ((kind & 1) == which)
-            summed = jnp.sum(jnp.where(mine, values, 0.0), axis=0, keepdims=True)
-            energy[which : which + 1, :] = summed[:, :MINE]
     for copy in copies:
         copy.wait()
 
@@ -224,13 +227,14 @@
     return pl.pallas_call(
         lambda *refs: place_kernel(parity, *refs),
         in_specs=[vmem] + [hbm] * parity,
-        out_specs=[hbm] + [vmem] * parity,
+        out_specs=[hbm] * (1 + parity),
         out_shape=[out] + [jax.ShapeDtypeStruct((2, MINE), jnp.float32)] * parity,
         input_output_aliases={1: 0} if parity else {},
         scratch_shapes=[
             pltpu.VMEM((PCAP // RBLK, RBLK, NV), jnp.bfloat16),
-            pltpu.SemaphoreType.DMA((PCAP // RBLK,)),
-        ],
+            pltpu.SemaphoreType.DMA((PCAP // RBLK + 1,)),
+        ]
+        + [pltpu.VMEM((2, MINE), jnp.float32)] * parity,
         compiler_params=pltpu.CompilerParams(vmem_limit_bytes=VMEM),
         cost_estimate=pl.CostEstimate(flops=2 * NV * NV * PCAP, bytes_accessed=2 << 20, transcendentals=0),
         name="place",
@@ -263,7 +267,7 @@
     eps_a = eps_virt[:, None]
     scalars = (jnp.stack([me, virt]), virt_counts, pair_counts, eps_virt)
 
-    even, plus, far, minus = lax.optimization_barrier((even, plus, far, minus))
+    amp[0], plus, far, minus = lax.optimization_barrier((amp[0], plus, far, minus))
     left, far, right = step(plus, 1), step(far, 2), step(minus, 3)
     send, energy0 = ladder(0, scalars, (even,), amp[0], eps_a, occ)
     first = across(send)

time: 126 us -> 124 us (0.984)
  waiting for transfers between devices: 57.5 us -> 52.3 us
  starting transfers between devices: 28.7 us -> 32 us
    all_to_all x1, waiting for transfers between devices: 8.24 us -> 3.08 us  [shards(): even = lax.all_to_all(even, 'pair', 0, 0, tiled=True)]
    ppermute x3, starting transfers between devices: 2.68 us -> 5.12 us  [step(): return lax.ppermute(value, 'pair', [(i, (i + by) % 4) for i in range(4)])]
where the time goes in v7:
time: 124 us; the launch traced here: 123 us
  waiting for transfers between devices  52.3 us (42%)
  starting transfers between devices  32 us (26%)
  Pallas kernels  20 us (16%)
  local copies, waits for them, and re-layouts  17.2 us (14%)
    all_to_all x2, waiting for transfers between devices, across(): return lax.all_to_all(value, 'virt', 0, 0, tiled=True)  49.2 us
    all_to_all x2, starting transfers between devices, across(): return lax.all_to_all(value, 'virt', 0, 0, tiled=True)  21.9 us
    pallas_call x2, Pallas kernels, ladder(): pl.pallas_call(lambda *refs: ladder_kernel(parity, *refs), in_specs=[pl.B...  9.38 us
    unnamed x24, local copies, waits for them, and re-layouts  9.07 us
    slice x1, local copies, waits for them, and re-layouts, shards(): amp = [jnp.transpose(amplitudes[parity], (1, 0, 2)) for parity in range(2)]  7.92 us
    pallas_call x2, Pallas kernels, regroup(): pl.pallas_call(lambda *refs: regroup_kernel(parity, *refs), in_specs=[pl....  7.27 us
    ppermute x3, starting transfers between devices, step(): return lax.ppermute(value, 'pair', [(i, (i + by) % 4) for i in range(4)])  5.12 us
    all_to_all x1, starting transfers between devices, shards(): even = lax.all_to_all(even, 'pair', 0, 0, tiled=True)  5.03 us
  transfers between devices with their start and end apart: 6, of which 3 were waited for; matrix products, arithmetic and copies ran while one was open for 13% of the time, Pallas kernels for 12%

profile of v7, /device:TPU:1, one launch (start us, length us, event | category | flops | bytes accessed | tf_op | source)
XLA Modules:
  0.0 123.5 jit_solution(10612416737532421200)
XLA Ops:
  0.6 3.3 %regroup.2 = bf16[4,2,512,256]{3,2,1,0:T(8,128)(2,1)} custom-call(s32[1]{0:T(128)} %bitcast.refs_0_, bf16[2,4096,256]{2,1,0:T(8,128)(2,1)} %bitcast.25), custom_call_target="tpu_custom_call" | custom-call | flops 1073741824 | bytes 6291456 | tf_op jit(solution)/shard_map/regroup/pallas_call | solution.py:76
  4.0 5.0 %all-to-all-start = ((bf16[4,2,512,256]{3,2,1,0:T(8,128)(2,1)}), bf16[4,2,512,256]{3,2,1,0:T(8,128)(2,1)S(1)}, u32[]{:S(2)}, u32[]{:S(2)}) async-start(bf16[4,2,512,256]{3,2,1,0:T(8,128)(2,1)} %regroup.2), calls=%async_computation | async-start | bytes 4194304 | tf_op jit(solution)/shard_map/all_to_all | solution.py:262
  9.0 7.9 %fusion.2 = (bf16[1,1024,2,1024]{3,2,1,0:T(2,128)(2,1)}, bf16[1,1024,2,1024]{3,2,1,0:T(2,128)(2,1)S(1)}) fusion(bf16[2,1024,2,1024]{3,2,1,0:T(2,128)(2,1)} %param.7), kind=kLoop, calls=%fused_computation.7 | loop fusion | bytes 16777216 | tf_op jit(solution)/shard_map/slice | solution.py:264
  16.9 3.3 %copy.35 = bf16[1,1024,2,1024]{3,1,2,0:T(8,128)(2,1)} copy(bf16[1,1024,2,1024]{3,2,1,0:T(2,128)(2,1)S(1)} %get-tuple-element.27) | data formatting | bytes 8388608
  20.3 0.0 copy-start.4
  20.3 3.9 %regroup.3 = (bf16[2,512,256]{2,1,0:T(8,128)(2,1)}, bf16[2,512,256]{2,1,0:T(8,128)(2,1)}, bf16[2,512,256]{2,1,0:T(8,128)(2,1)}, bf16[2,512,256]{2,1,0:T(8,128)(2,1)}) custom-call(s32[1]{0:T(128)} %bitcast.refs_0_, bf16[2,4096,256]{2,1,0:T(8,128)(2,1)} %bitcast.26), custom_call_target="tpu_custom_call" | custom-call | flops 1073741824 | bytes 6291456 | tf_op jit(solution)/shard_map/regroup/pallas_call | solution.py:76
  24.2 1.5 %collective-permute-start = (bf16[2,512,256]{2,1,0:T(8,128)(2,1)}, bf16[2,512,256]{2,1,0:T(8,128)(2,1)S(1)}, u32[]{:S(2)}, u32[]{:S(2)}) collective-permute-start(bf16[2,512,256]{2,1,0:T(8,128)(2,1)} %get-tuple-element.20), channel_id=1, source_target_pairs={{0,1},{1,2},{2,3},{3,0},{4,5},{5,6},{6,7},{7,4},{8,9},{9,10},{10,1... | collective-permute-start | bytes 1572872 | tf_op jit(solution)/shard_map/ppermute | solution.py:250
  25.7 2.4 %collective-permute-start.1 = (bf16[2,512,256]{2,1,0:T(8,128)(2,1)}, bf16[2,512,256]{2,1,0:T(8,128)(2,1)S(1)}, u32[]{:S(2)}, u32[]{:S(2)}) collective-permute-start(bf16[2,512,256]{2,1,0:T(8,128)(2,1)} %get-tuple-element.21), channel_id=1, source_target_pairs={{0,2},{1,3},{2,0},{3,1},{4,6},{5,7},{6,4},{7,5},{8,10},{9,11},{10,... | collective-permute-start | bytes 1572872 | tf_op jit(solution)/shard_map/ppermute | solution.py:250
  28.1 1.2 collective-permute-start.2
  29.3 0.1 copy.21.refs_6_.refs_9_
  29.5 0.0 copy-done.9
  29.5 0.0 copy-done.10
  29.5 0.9 fusion
  30.4 0.1 pad_add_fusion.refs_0_
  30.5 3.1 %all-to-all-done.refs_4_ = bf16[4,2,512,256]{3,2,1,0:T(8,128)(2,1)S(1)} async-done(((bf16[4,2,512,256]{3,2,1,0:T(8,128)(2,1)}), bf16[4,2,512,256]{3,2,1,0:T(8,128)(2,1)S(1)}, u32[]{:S(2)}, u32[]{:S(2)}) %all-to-all-start) | async-done | bytes 2097184 | tf_op jit(solution)/shard_map/all_to_all | solution.py:262
  33.6 0.0 copy-done.3
  33.6 2.2 %copy-done = bf16[1,1024,2,1024]{3,1,2,0:T(8,128)(2,1)S(1)} copy-done((bf16[1,1024,2,1024]{3,1,2,0:T(8,128)(2,1)S(1)}, bf16[1,1024,2,1024]{3,1,2,0:T(8,128)(2,1)}, u32[]{:S(2)}) %copy-start) | copy-done | bytes 4194328
  35.8 4.0 %ladder.2 = (bf16[512,1024]{1,0:T(8,128)(2,1)}, f32[1,1024]{1,0:T(1,128)}) custom-call(s32[2]{0:T(128)S(1)} %pad_add_fusion.refs_0_, s32[8]{0:T(128)S(1)} %copy-done.3, s32[8]{0:T(128)S(1)} %copy-done.4, f32[512]{0:T(512)S(1)} %copy-done.1, bf16[4,2,512,256]{3,2,1,0:T(8,128)(2,1)S(1)} %all-to-all-done.refs_4_, bf16[2,1024,1024]{2,1,0:T(8,128)(2,1)S(1)} %bitcast.22, ...), custom_call_target="tpu_custom_call" | custom-call | flops 2147483648 | bytes 7340032 | tf_op jit(solution)/shard_map/ladder/pallas_call | solution.py:176
  39.8 15.7 %all-to-all-start.1 = ((bf16[64,8,1024]{2,1,0:T(8,128)(2,1)}), bf16[64,8,1024]{2,1,0:T(8,128)(2,1)S(1)}, u32[]{:S(2)}, u32[]{:S(2)}) async-start(bf16[64,8,1024]{2,1,0:T(8,128)(2,1)} %bitcast.28), calls=%async_computation.1 | async-start | bytes 2097152 | tf_op jit(solution)/shard_map/all_to_all | solution.py:254
  55.5 0.0 copy-start.2
  55.6 0.0 copy-start.5
  55.6 0.0 copy-start.7
  55.6 3.5 %copy.34 = bf16[1,1024,2,1024]{3,1,2,0:T(8,128)(2,1)S(1)} copy(bf16[1,1024,2,1024]{3,2,1,0:T(2,128)(2,1)} %get-tuple-element.26) | data formatting | bytes 8388608
  59.1 0.0 collective-permute-done.refs_5_
  59.1 0.0 collective-permute-done.1.refs_6_
  59.2 0.0 collective-permute-done.2.refs_7_
  59.2 5.4 %ladder.3 = bf16[512,1152]{1,0:T(8,128)(2,1)} custom-call(s32[2]{0:T(128)S(1)} %copy-done.7, s32[8]{0:T(128)S(1)} %copy-done.3, s32[8]{0:T(128)S(1)} %copy-done.5, f32[512]{0:T(512)S(1)} %copy-done.1, bf16[2,512,256]{2,1,0:T(8,128)(2,1)S(1)} %copy-done.2, bf16[2,512,256]{2,1,0:T(8,128)(2,1)S(1)} %collective-permute-done.refs_5_, ...), custom_call_target="tpu_custom_call" | custom-call | flops 19327352832 | bytes 7340032 | tf_op jit(solution)/shard_map/ladder/pallas_call | solution.py:176
  64.6 19.5 %all-to-all-done.1 = bf16[64,8,1024]{2,1,0:T(8,128)(2,1)S(1)} async-done(((bf16[64,8,1024]{2,1,0:T(8,128)(2,1)}), bf16[64,8,1024]{2,1,0:T(8,128)(2,1)S(1)}, u32[]{:S(2)}, u32[]{:S(2)}) %all-to-all-start.1) | async-done | bytes 1048608 | tf_op jit(solution)/shard_map/all_to_all | solution.py:254
  84.1 6.2 %all-to-all-start.2 = ((bf16[64,8,1152]{2,1,0:T(8,128)(2,1)}), bf16[64,8,1152]{2,1,0:T(8,128)(2,1)S(1)}, u32[]{:S(2)}, u32[]{:S(2)}) async-start(bf16[64,8,1152]{2,1,0:T(8,128)(2,1)} %bitcast.27), calls=%async_computation.2 | async-start | bytes 2359296 | tf_op jit(solution)/shard_map/all_to_all | solution.py:254
  90.3 1.6 %place.2.refs_1_ = bf16[2,1024,512]{2,1,0:T(8,128)(2,1)} custom-call(bf16[512,1024]{1,0:T(8,128)(2,1)S(1)} %bitcast.21), custom_call_target="tpu_custom_call" | custom-call | flops 536870912 | bytes 2097152 | tf_op jit(solution)/shard_map/place/pallas_call | solution.py:227
  91.9 29.7 %all-to-all-done.2 = bf16[64,8,1152]{2,1,0:T(8,128)(2,1)S(1)} async-done(((bf16[64,8,1152]{2,1,0:T(8,128)(2,1)}), bf16[64,8,1152]{2,1,0:T(8,128)(2,1)S(1)}, u32[]{:S(2)}, u32[]{:S(2)}) %all-to-all-start.2) | async-done | bytes 1179680 | tf_op jit(solution)/shard_map/all_to_all | solution.py:254
  121.7 1.7 %place.3 = (bf16[2,1024,512]{2,1,0:T(8,128)(2,1)}, f32[2,16]{1,0:T(2,128)}) custom-call(bf16[512,1152]{1,0:T(8,128)(2,1)S(1)} %bitcast.20, bf16[2,1024,512]{2,1,0:T(8,128)(2,1)} %place.2.refs_1_), custom_call_target="tpu_custom_call", output_to_operand_aliasing={{0}: (1, {})} | custom-call | flops 536870912 | bytes 2097152 | tf_op jit(solution)/shard_map/place/pallas_call | solution.py:227
  (16 shorter events, 0.1 us)
Async XLA Ops:
  4.0 29.6 %all-to-all-start = ((bf16[4,2,512,256]{3,2,1,0:T(8,128)(2,1)}), bf16[4,2,512,256]{3,2,1,0:T(8,128)(2,1)S(1)}, u32[]{:S(2)}, u32[]{:S(2)}) async-start(bf16[4,2,512,256]{3,2,1,0:T(8,128)(2,1)} %regroup.2), calls=%async_computation | async-start | bytes 4194304 | tf_op jit(solution)/shard_map/all_to_all | solution.py:262
  20.2 9.1 %copy-start.1 = (f32[512]{0:T(512)S(1)}, f32[512]{0:T(512)}, u32[]{:S(2)}) copy-start(f32[512]{0:T(512)} %refs_3_.3) | copy-start | bytes 6148
  20.2 9.2 %copy-start.9 = (s32[2,1024,2]{1,2,0:T(2,128)S(1)}, s32[2,1024,2]{1,2,0:T(2,128)}, u32[]{:S(2)}) copy-start(s32[2,1024,2]{1,2,0:T(2,128)} %param.11) | copy-start | bytes 49156
  20.2 9.2 %copy-start.10 = (f32[100]{0:T(128)S(1)}, f32[100]{0:T(128)}, u32[]{:S(2)}) copy-start(f32[100]{0:T(128)} %param.12) | copy-start | bytes 1204
  20.2 13.4 %copy-start.3 = (s32[8]{0:T(128)S(1)}, s32[8]{0:T(128)}, u32[]{:S(2)}) copy-start(s32[8]{0:T(128)} %refs_1_.3) | copy-start | bytes 100
  20.3 13.4 %copy-start.4 = (s32[8]{0:T(128)S(1)}, s32[8]{0:T(128)}, u32[]{:S(2)}) copy-start(s32[8]{0:T(128)} %refs_2_.3) | copy-start | bytes 100
  24.2 34.9 %collective-permute-start = (bf16[2,512,256]{2,1,0:T(8,128)(2,1)}, bf16[2,512,256]{2,1,0:T(8,128)(2,1)S(1)}, u32[]{:S(2)}, u32[]{:S(2)}) collective-permute-start(bf16[2,512,256]{2,1,0:T(8,128)(2,1)} %get-tuple-element.20), channel_id=1, source_target_pairs={{0,1},{1,2},{2,3},{3,0},{4,5},{5,6},{6,7},{7,4},{8,9},{9,10},{10,1... | collective-permute-start | bytes 1572872 | tf_op jit(solution)/shard_map/ppermute | solution.py:250
  25.7 33.4 %collective-permute-start.1 = (bf16[2,512,256]{2,1,0:T(8,128)(2,1)}, bf16[2,512,256]{2,1,0:T(8,128)(2,1)S(1)}, u32[]{:S(2)}, u32[]{:S(2)}) collective-permute-start(bf16[2,512,256]{2,1,0:T(8,128)(2,1)} %get-tuple-element.21), channel_id=1, source_target_pairs={{0,2},{1,3},{2,0},{3,1},{4,6},{5,7},{6,4},{7,5},{8,10},{9,11},{10,... | collective-permute-start | bytes 1572872 | tf_op jit(solution)/shard_map/ppermute | solution.py:250
  28.1 31.0 %collective-permute-start.2 = (bf16[2,512,256]{2,1,0:T(8,128)(2,1)}, bf16[2,512,256]{2,1,0:T(8,128)(2,1)}, u32[]{:S(2)}, u32[]{:S(2)}) collective-permute-start(bf16[2,512,256]{2,1,0:T(8,128)(2,1)} %get-tuple-element.22), channel_id=1, source_target_pairs={{0,3},{1,0},{2,1},{3,2},{4,7},{5,4},{6,5},{7,6},{8,11},{9,8},{10,9... | collective-permute-start | bytes 1572872 | tf_op jit(solution)/shard_map/ppermute | solution.py:250
  30.5 9.3 %copy-start.6 = (s32[2]{0:T(128)}, s32[2]{0:T(128)S(1)}, u32[]{:S(2)}) copy-start(s32[2]{0:T(128)S(1)} %pad_add_fusion.refs_0_) | copy-start | bytes 28
  33.6 2.2 %copy-start = (bf16[1,1024,2,1024]{3,1,2,0:T(8,128)(2,1)S(1)}, bf16[1,1024,2,1024]{3,1,2,0:T(8,128)(2,1)}, u32[]{:S(2)}) copy-start(bf16[1,1024,2,1024]{3,1,2,0:T(8,128)(2,1)} %copy.35) | copy-start | bytes 12582916
  39.8 44.3 %all-to-all-start.1 = ((bf16[64,8,1024]{2,1,0:T(8,128)(2,1)}), bf16[64,8,1024]{2,1,0:T(8,128)(2,1)S(1)}, u32[]{:S(2)}, u32[]{:S(2)}) async-start(bf16[64,8,1024]{2,1,0:T(8,128)(2,1)} %bitcast.28), calls=%async_computation.1 | async-start | bytes 2097152 | tf_op jit(solution)/shard_map/all_to_all | solution.py:254
  55.5 3.6 %copy-start.2 = (bf16[2,512,256]{2,1,0:T(8,128)(2,1)S(1)}, bf16[2,512,256]{2,1,0:T(8,128)(2,1)}, u32[]{:S(2)}) copy-start(bf16[2,512,256]{2,1,0:T(8,128)(2,1)} %get-tuple-element.19.refs_4_) | copy-start | bytes 1572868
  55.6 3.6 %copy-start.5 = (s32[8]{0:T(128)S(1)}, s32[8]{0:T(128)}, u32[]{:S(2)}) copy-start(s32[8]{0:T(128)} %refs_2_.3) | copy-start | bytes 100
  55.6 3.6 %copy-start.7 = (s32[2]{0:T(128)S(1)}, s32[2]{0:T(128)}, u32[]{:S(2)}) copy-start(s32[2]{0:T(128)} %copy-done.6) | copy-start | bytes 28
  55.6 3.6 %copy-start.8 = (f32[1,1024]{1,0:T(1,128)S(1)}, f32[1,1024]{1,0:T(1,128)}, u32[]{:S(2)}) copy-start(f32[1,1024]{1,0:T(1,128)} %get-tuple-element.23.refs_11_) | copy-start | bytes 12292
  84.1 37.6 %all-to-all-start.2 = ((bf16[64,8,1152]{2,1,0:T(8,128)(2,1)}), bf16[64,8,1152]{2,1,0:T(8,128)(2,1)S(1)}, u32[]{:S(2)}, u32[]{:S(2)}) async-start(bf16[64,8,1152]{2,1,0:T(8,128)(2,1)} %bitcast.27), calls=%async_computation.2 | async-start | bytes 2359296 | tf_op jit(solution)/shard_map/all_to_all | solution.py:254

commit v8 on v7

--- a/solution.py
+++ b/solution.py
@@ -267,7 +267,8 @@
     eps_a = eps_virt[:, None]
     scalars = (jnp.stack([me, virt]), virt_counts, pair_counts, eps_virt)
 
-    amp[0], plus, far, minus = lax.optimization_barrier((amp[0], plus, far, minus))
+    amp[0], far = lax.optimization_barrier((amp[0], far))
+    occ, plus, minus = lax.optimization_barrier((occ, plus, minus))
     left, far, right = step(plus, 1), step(far, 2), step(minus, 3)
     send, energy0 = ladder(0, scalars, (even,), amp[0], eps_a, occ)
     first = across(send)

time: 124 us -> 124 us (level)
  no operation moved by 1% of the time
where the time goes in v8:
time: 124 us
  waiting for transfers between devices  52.3 us (42%)
  starting transfers between devices  32 us (26%)
  Pallas kernels  20 us (16%)
  local copies, waits for them, and re-layouts  17.2 us (14%)
    all_to_all x2, waiting for transfers between devices, across(): return lax.all_to_all(value, 'virt', 0, 0, tiled=True)  49.2 us
    all_to_all x2, starting transfers between devices, across(): return lax.all_to_all(value, 'virt', 0, 0, tiled=True)  21.9 us
    pallas_call x2, Pallas kernels, ladder(): pl.pallas_call(lambda *refs: ladder_kernel(parity, *refs), in_specs=[pl.B...  9.4 us
    unnamed x24, local copies, waits for them, and re-layouts  9.08 us
    slice x1, local copies, waits for them, and re-layouts, shards(): amp = [jnp.transpose(amplitudes[parity], (1, 0, 2)) for parity in range(2)]  7.92 us
    pallas_call x2, Pallas kernels, regroup(): pl.pallas_call(lambda *refs: regroup_kernel(parity, *refs), in_specs=[pl....  7.29 us
    ppermute x3, starting transfers between devices, step(): return lax.ppermute(value, 'pair', [(i, (i + by) % 4) for i in range(4)])  5.12 us
    all_to_all x1, starting transfers between devices, shards(): even = lax.all_to_all(even, 'pair', 0, 0, tiled=True)  5.03 us
  transfers between devices with their start and end apart: 6, of which 3 were waited for; matrix products, arithmetic and copies ran while one was open for 13% of the time, Pallas kernels for 12%

profile of v8, /device:TPU:1, one launch (start us, length us, event | category | flops | bytes accessed | tf_op | source)
XLA Modules:
  0.0 123.5 jit_solution(8645992635837627317)
XLA Ops:
  0.6 3.3 %regroup.2 = bf16[4,2,512,256]{3,2,1,0:T(8,128)(2,1)} custom-call(s32[1]{0:T(128)} %bitcast.refs_0_, bf16[2,4096,256]{2,1,0:T(8,128)(2,1)} %bitcast.25), custom_call_target="tpu_custom_call" | custom-call | flops 1073741824 | bytes 6291456 | tf_op jit(solution)/shard_map/regroup/pallas_call | solution.py:76
  4.0 0.0 copy-start.9
  4.0 0.0 copy-start.10
  4.0 5.0 %all-to-all-start = ((bf16[4,2,512,256]{3,2,1,0:T(8,128)(2,1)}), bf16[4,2,512,256]{3,2,1,0:T(8,128)(2,1)S(1)}, u32[]{:S(2)}, u32[]{:S(2)}) async-start(bf16[4,2,512,256]{3,2,1,0:T(8,128)(2,1)} %regroup.2), calls=%async_computation | async-start | bytes 4194304 | tf_op jit(solution)/shard_map/all_to_all | solution.py:262
  9.0 0.0 copy-done.9
  9.0 0.0 copy-done.10
  9.0 0.9 fusion
  10.0 3.9 %regroup.3 = (bf16[2,512,256]{2,1,0:T(8,128)(2,1)}, bf16[2,512,256]{2,1,0:T(8,128)(2,1)}, bf16[2,512,256]{2,1,0:T(8,128)(2,1)}, bf16[2,512,256]{2,1,0:T(8,128)(2,1)}) custom-call(s32[1]{0:T(128)} %bitcast.refs_0_, bf16[2,4096,256]{2,1,0:T(8,128)(2,1)} %bitcast.26), custom_call_target="tpu_custom_call" | custom-call | flops 1073741824 | bytes 6291456 | tf_op jit(solution)/shard_map/regroup/pallas_call | solution.py:76
  14.0 1.5 %collective-permute-start = (bf16[2,512,256]{2,1,0:T(8,128)(2,1)}, bf16[2,512,256]{2,1,0:T(8,128)(2,1)S(1)}, u32[]{:S(2)}, u32[]{:S(2)}) collective-permute-start(bf16[2,512,256]{2,1,0:T(8,128)(2,1)} %get-tuple-element.22), channel_id=1, source_target_pairs={{0,1},{1,2},{2,3},{3,0},{4,5},{5,6},{6,7},{7,4},{8,9},{9,10},{10,1... | collective-permute-start | bytes 1572872 | tf_op jit(solution)/shard_map/ppermute | solution.py:250
  15.5 7.9 %fusion.2 = (bf16[1,1024,2,1024]{3,2,1,0:T(2,128)(2,1)}, bf16[1,1024,2,1024]{3,2,1,0:T(2,128)(2,1)S(1)}) fusion(bf16[2,1024,2,1024]{3,2,1,0:T(2,128)(2,1)} %param.7), kind=kLoop, calls=%fused_computation.7 | loop fusion | bytes 16777216 | tf_op jit(solution)/shard_map/slice | solution.py:264
  23.4 0.0 copy-start.4
  23.4 3.3 %copy.35 = bf16[1,1024,2,1024]{3,1,2,0:T(8,128)(2,1)} copy(bf16[1,1024,2,1024]{3,2,1,0:T(2,128)(2,1)S(1)} %get-tuple-element.29) | data formatting | bytes 8388608
  26.7 2.4 %collective-permute-start.1 = (bf16[2,512,256]{2,1,0:T(8,128)(2,1)}, bf16[2,512,256]{2,1,0:T(8,128)(2,1)S(1)}, u32[]{:S(2)}, u32[]{:S(2)}) collective-permute-start(bf16[2,512,256]{2,1,0:T(8,128)(2,1)} %get-tuple-element.23), channel_id=1, source_target_pairs={{0,2},{1,3},{2,0},{3,1},{4,6},{5,7},{6,4},{7,5},{8,10},{9,11},{10,... | collective-permute-start | bytes 1572872 | tf_op jit(solution)/shard_map/ppermute | solution.py:250
  29.1 1.2 collective-permute-start.2
  30.3 0.1 copy.21.refs_6_.refs_9_
  30.5 0.1 pad_add_fusion.refs_0_
  30.6 3.1 %all-to-all-done.refs_4_ = bf16[4,2,512,256]{3,2,1,0:T(8,128)(2,1)S(1)} async-done(((bf16[4,2,512,256]{3,2,1,0:T(8,128)(2,1)}), bf16[4,2,512,256]{3,2,1,0:T(8,128)(2,1)S(1)}, u32[]{:S(2)}, u32[]{:S(2)}) %all-to-all-start) | async-done | bytes 2097184 | tf_op jit(solution)/shard_map/all_to_all | solution.py:262
  33.6 2.2 %copy-done = bf16[1,1024,2,1024]{3,1,2,0:T(8,128)(2,1)S(1)} copy-done((bf16[1,1024,2,1024]{3,1,2,0:T(8,128)(2,1)S(1)}, bf16[1,1024,2,1024]{3,1,2,0:T(8,128)(2,1)}, u32[]{:S(2)}) %copy-start) | copy-done | bytes 4194328
  35.8 4.0 %ladder.2 = (bf16[512,1024]{1,0:T(8,128)(2,1)}, f32[1,1024]{1,0:T(1,128)}) custom-call(s32[2]{0:T(128)S(1)} %pad_add_fusion.refs_0_, s32[8]{0:T(128)S(1)} %copy-done.3, s32[8]{0:T(128)S(1)} %copy-done.4, f32[512]{0:T(512)S(1)} %copy-done.1, bf16[4,2,512,256]{3,2,1,0:T(8,128)(2,1)S(1)} %all-to-all-done.refs_4_, bf16[2,1024,1024]{2,1,0:T(8,128)(2,1)S(1)} %bitcast.22, ...), custom_call_target="tpu_custom_call" | custom-call | flops 2147483648 | bytes 7340032 | tf_op jit(solution)/shard_map/ladder/pallas_call | solution.py:176
  39.9 15.7 %all-to-all-start.1 = ((bf16[64,8,1024]{2,1,0:T(8,128)(2,1)}), bf16[64,8,1024]{2,1,0:T(8,128)(2,1)S(1)}, u32[]{:S(2)}, u32[]{:S(2)}) async-start(bf16[64,8,1024]{2,1,0:T(8,128)(2,1)} %bitcast.28), calls=%async_computation.1 | async-start | bytes 2097152 | tf_op jit(solution)/shard_map/all_to_all | solution.py:254
  55.6 0.0 copy-start.5
  55.6 0.0 copy-start.7
  55.6 3.5 %copy.34 = bf16[1,1024,2,1024]{3,1,2,0:T(8,128)(2,1)S(1)} copy(bf16[1,1024,2,1024]{3,2,1,0:T(2,128)(2,1)} %get-tuple-element.28) | data formatting | bytes 8388608
  59.2 0.0 collective-permute-done.refs_5_
  59.2 0.0 collective-permute-done.1.refs_6_
  59.2 0.0 collective-permute-done.2.refs_7_
  59.2 5.4 %ladder.3 = bf16[512,1152]{1,0:T(8,128)(2,1)} custom-call(s32[2]{0:T(128)S(1)} %copy-done.7, s32[8]{0:T(128)S(1)} %copy-done.3, s32[8]{0:T(128)S(1)} %copy-done.5, f32[512]{0:T(512)S(1)} %copy-done.1, bf16[2,512,256]{2,1,0:T(8,128)(2,1)S(1)} %copy-done.2, bf16[2,512,256]{2,1,0:T(8,128)(2,1)S(1)} %collective-permute-done.refs_5_, ...), custom_call_target="tpu_custom_call" | custom-call | flops 19327352832 | bytes 7340032 | tf_op jit(solution)/shard_map/ladder/pallas_call | solution.py:176
  64.6 19.5 %all-to-all-done.1 = bf16[64,8,1024]{2,1,0:T(8,128)(2,1)S(1)} async-done(((bf16[64,8,1024]{2,1,0:T(8,128)(2,1)}), bf16[64,8,1024]{2,1,0:T(8,128)(2,1)S(1)}, u32[]{:S(2)}, u32[]{:S(2)}) %all-to-all-start.1) | async-done | bytes 1048608 | tf_op jit(solution)/shard_map/all_to_all | solution.py:254
  84.1 6.2 %all-to-all-start.2 = ((bf16[64,8,1152]{2,1,0:T(8,128)(2,1)}), bf16[64,8,1152]{2,1,0:T(8,128)(2,1)S(1)}, u32[]{:S(2)}, u32[]{:S(2)}) async-start(bf16[64,8,1152]{2,1,0:T(8,128)(2,1)} %bitcast.27), calls=%async_computation.2 | async-start | bytes 2359296 | tf_op jit(solution)/shard_map/all_to_all | solution.py:254
  90.3 1.6 %place.2.refs_1_ = bf16[2,1024,512]{2,1,0:T(8,128)(2,1)} custom-call(bf16[512,1024]{1,0:T(8,128)(2,1)S(1)} %bitcast.21), custom_call_target="tpu_custom_call" | custom-call | flops 536870912 | bytes 2097152 | tf_op jit(solution)/shard_map/place/pallas_call | solution.py:227
  91.9 29.7 %all-to-all-done.2 = bf16[64,8,1152]{2,1,0:T(8,128)(2,1)S(1)} async-done(((bf16[64,8,1152]{2,1,0:T(8,128)(2,1)}), bf16[64,8,1152]{2,1,0:T(8,128)(2,1)S(1)}, u32[]{:S(2)}, u32[]{:S(2)}) %all-to-all-start.2) | async-done | bytes 1179680 | tf_op jit(solution)/shard_map/all_to_all | solution.py:254
  121.7 1.7 %place.3 = (bf16[2,1024,512]{2,1,0:T(8,128)(2,1)}, f32[2,16]{1,0:T(2,128)}) custom-call(bf16[512,1152]{1,0:T(8,128)(2,1)S(1)} %bitcast.20, bf16[2,1024,512]{2,1,0:T(8,128)(2,1)} %place.2.refs_1_), custom_call_target="tpu_custom_call", output_to_operand_aliasing={{0}: (1, {})} | custom-call | flops 536870912 | bytes 2097152 | tf_op jit(solution)/shard_map/place/pallas_call | solution.py:227
  (16 shorter events, 0.1 us)
Async XLA Ops:
  4.0 5.1 %copy-start.9 = (s32[2,1024,2]{1,2,0:T(2,128)S(1)}, s32[2,1024,2]{1,2,0:T(2,128)}, u32[]{:S(2)}) copy-start(s32[2,1024,2]{1,2,0:T(2,128)} %param.11) | copy-start | bytes 49156
  4.0 5.0 %copy-start.10 = (f32[100]{0:T(128)S(1)}, f32[100]{0:T(128)}, u32[]{:S(2)}) copy-start(f32[100]{0:T(128)} %param.12) | copy-start | bytes 1204
  4.0 29.6 %all-to-all-start = ((bf16[4,2,512,256]{3,2,1,0:T(8,128)(2,1)}), bf16[4,2,512,256]{3,2,1,0:T(8,128)(2,1)S(1)}, u32[]{:S(2)}, u32[]{:S(2)}) async-start(bf16[4,2,512,256]{3,2,1,0:T(8,128)(2,1)} %regroup.2), calls=%async_computation | async-start | bytes 4194304 | tf_op jit(solution)/shard_map/all_to_all | solution.py:262
  14.0 45.2 %collective-permute-start = (bf16[2,512,256]{2,1,0:T(8,128)(2,1)}, bf16[2,512,256]{2,1,0:T(8,128)(2,1)S(1)}, u32[]{:S(2)}, u32[]{:S(2)}) collective-permute-start(bf16[2,512,256]{2,1,0:T(8,128)(2,1)} %get-tuple-element.22), channel_id=1, source_target_pairs={{0,1},{1,2},{2,3},{3,0},{4,5},{5,6},{6,7},{7,4},{8,9},{9,10},{10,1... | collective-permute-start | bytes 1572872 | tf_op jit(solution)/shard_map/ppermute | solution.py:250
  23.4 6.9 %copy-start.1 = (f32[512]{0:T(512)S(1)}, f32[512]{0:T(512)}, u32[]{:S(2)}) copy-start(f32[512]{0:T(512)} %refs_3_.3) | copy-start | bytes 6148
  23.4 10.2 %copy-start.3 = (s32[8]{0:T(128)S(1)}, s32[8]{0:T(128)}, u32[]{:S(2)}) copy-start(s32[8]{0:T(128)} %refs_1_.3) | copy-start | bytes 100
  23.4 10.2 %copy-start.4 = (s32[8]{0:T(128)S(1)}, s32[8]{0:T(128)}, u32[]{:S(2)}) copy-start(s32[8]{0:T(128)} %refs_2_.3) | copy-start | bytes 100
  26.7 32.4 %collective-permute-start.1 = (bf16[2,512,256]{2,1,0:T(8,128)(2,1)}, bf16[2,512,256]{2,1,0:T(8,128)(2,1)S(1)}, u32[]{:S(2)}, u32[]{:S(2)}) collective-permute-start(bf16[2,512,256]{2,1,0:T(8,128)(2,1)} %get-tuple-element.23), channel_id=1, source_target_pairs={{0,2},{1,3},{2,0},{3,1},{4,6},{5,7},{6,4},{7,5},{8,10},{9,11},{10,... | collective-permute-start | bytes 1572872 | tf_op jit(solution)/shard_map/ppermute | solution.py:250
  29.1 30.0 %collective-permute-start.2 = (bf16[2,512,256]{2,1,0:T(8,128)(2,1)}, bf16[2,512,256]{2,1,0:T(8,128)(2,1)}, u32[]{:S(2)}, u32[]{:S(2)}) collective-permute-start(bf16[2,512,256]{2,1,0:T(8,128)(2,1)} %get-tuple-element.24), channel_id=1, source_target_pairs={{0,3},{1,0},{2,1},{3,2},{4,7},{5,4},{6,5},{7,6},{8,11},{9,8},{10,9... | collective-permute-start | bytes 1572872 | tf_op jit(solution)/shard_map/ppermute | solution.py:250
  30.6 9.3 %copy-start.6 = (s32[2]{0:T(128)}, s32[2]{0:T(128)S(1)}, u32[]{:S(2)}) copy-start(s32[2]{0:T(128)S(1)} %pad_add_fusion.refs_0_) | copy-start | bytes 28
  33.6 2.2 %copy-start = (bf16[1,1024,2,1024]{3,1,2,0:T(8,128)(2,1)S(1)}, bf16[1,1024,2,1024]{3,1,2,0:T(8,128)(2,1)}, u32[]{:S(2)}) copy-start(bf16[1,1024,2,1024]{3,1,2,0:T(8,128)(2,1)} %copy.35) | copy-start | bytes 12582916
  39.9 44.3 %all-to-all-start.1 = ((bf16[64,8,1024]{2,1,0:T(8,128)(2,1)}), bf16[64,8,1024]{2,1,0:T(8,128)(2,1)S(1)}, u32[]{:S(2)}, u32[]{:S(2)}) async-start(bf16[64,8,1024]{2,1,0:T(8,128)(2,1)} %bitcast.28), calls=%async_computation.1 | async-start | bytes 2097152 | tf_op jit(solution)/shard_map/all_to_all | solution.py:254
  55.6 3.6 %copy-start.2 = (bf16[2,512,256]{2,1,0:T(8,128)(2,1)S(1)}, bf16[2,512,256]{2,1,0:T(8,128)(2,1)}, u32[]{:S(2)}) copy-start(bf16[2,512,256]{2,1,0:T(8,128)(2,1)} %get-tuple-element.21.refs_4_) | copy-start | bytes 1572868
  55.6 3.6 %copy-start.5 = (s32[8]{0:T(128)S(1)}, s32[8]{0:T(128)}, u32[]{:S(2)}) copy-start(s32[8]{0:T(128)} %refs_2_.3) | copy-start | bytes 100
  55.6 3.6 %copy-start.7 = (s32[2]{0:T(128)S(1)}, s32[2]{0:T(128)}, u32[]{:S(2)}) copy-start(s32[2]{0:T(128)} %copy-done.6) | copy-start | bytes 28
  55.6 3.6 %copy-start.8 = (f32[1,1024]{1,0:T(1,128)S(1)}, f32[1,1024]{1,0:T(1,128)}, u32[]{:S(2)}) copy-start(f32[1,1024]{1,0:T(1,128)} %get-tuple-element.25.refs_11_) | copy-start | bytes 12292
  84.1 37.6 %all-to-all-start.2 = ((bf16[64,8,1152]{2,1,0:T(8,128)(2,1)}), bf16[64,8,1152]{2,1,0:T(8,128)(2,1)S(1)}, u32[]{:S(2)}, u32[]{:S(2)}) async-start(bf16[64,8,1152]{2,1,0:T(8,128)(2,1)} %bitcast.27), calls=%async_computation.2 | async-start | bytes 2359296 | tf_op jit(solution)/shard_map/all_to_all | solution.py:254
